TPU v7x, 32 devices: a whole 2x2x4 slice. The times are simulated.
32 devices in a mesh: fsdp: 32 (over z, y, x, core).
Axes of the slice: x: 2, y: 2, z: 4, core: 2. Of those that a mesh axis runs over, the one named last changes fastest.
Arguments:
- tokens: bfloat16 [6144, 2048], P('fsdp'), may hold values from -6 to 6
- segments: int32 [96, 64], P('fsdp'), may hold values from 0 to 2, never falling along the last dimension, each value on 1 to 48 neighbouring positions
- micro_live: int32 [32], P('fsdp'), may hold values from 2 to 3, as said below
- cotangent: bfloat16 [6144, 2048], P('fsdp'), may hold values from -6 to 6
- w_query: bfloat16 [2048, 2048], P('fsdp'), may hold values from -0.125 to 0.125
- key_weight: bfloat16 [2048, 1024], P('fsdp'), may hold values from -0.125 to 0.125
- value_weight: bfloat16 [2048, 1024], P('fsdp'), may hold values from -0.125 to 0.125
- w_output: bfloat16 [2048, 2048], P('fsdp'), may hold values from -0.5 to 0.5
- attn_gain: bfloat16 [2048], P('fsdp'), may hold values from 0.5 to 1.5
- query_norm_gain: bfloat16 [128], P('fsdp'), may hold values from 1.09375 to 1.6953125
- key_gain: bfloat16 [128], P('fsdp'), may hold values from 1.09375 to 1.6953125
- w_gate: bfloat16 [2048, 6144], P('fsdp'), may hold values from -0.125 to 0.125
- w_up: bfloat16 [2048, 6144], P('fsdp'), may hold values from -0.125 to 0.125
- w_down: bfloat16 [6144, 2048], P('fsdp'), may hold values from -0.109375 to 0.109375
- mlp_gain: bfloat16 [2048], P('fsdp'), may hold values from 0.5 to 1.5
Outputs:
- layer_out: bfloat16 [6144, 2048], P('fsdp')
- grad_tokens: bfloat16 [6144, 2048], P('fsdp')
- grad_query: float32 [2048, 2048], P('fsdp')
- grad_key: float32 [2048, 1024], P('fsdp')
- value_weight_gradient: float32 [2048, 1024], P('fsdp')
- grad_output: float32 [2048, 2048], P('fsdp')
- grad_attn_gain: float32 [2048], P('fsdp')
- grad_query_gain: float32 [128], P('fsdp')
- grad_key_gain: float32 [128], P('fsdp')
- grad_gate: float32 [2048, 6144], P('fsdp')
- grad_up: float32 [2048, 6144], P('fsdp')
- grad_down: float32 [6144, 2048], P('fsdp')
- grad_mlp_gain: float32 [2048], P('fsdp')
Inputs may be any that keep to these rules, and one draw needn't show every extreme that they name: `segments`: within each micro-batch the ids start at 0 and never fall; a document has 1 to 48 rows. `micro_live`: exactly half of the devices have 3 live micro-batches, the others 2.
All inputs are finite; a program needn't handle non-finite values.
Results may differ from a plain program's by a relative error of at most 0.015.
Values may be sent and summed in bfloat16 or wider, within the bound.
A program may use at most 384 MiB of HBM per device.

v0:
```python
import jax
import jax.numpy as jnp
from jax import lax
from jax.sharding import PartitionSpec as P

QUERY_HEADS = 16
KEY_VALUE_HEADS = 8
HEAD_SIZE = 128


epsilon = 1e-06
base_theta = 1000000.0


def root_mean_square_norm(values, gain):
    return values * lax.rsqrt(jnp.mean(values * values, axis=-1, keepdims=True) + epsilon) * gain


def doc_positions(segments):
    earlier = (segments[:, None, :] < segments[:, :, None]).astype(jnp.int32)
    starts = jnp.sum(earlier, axis=2)
    token_positions = lax.broadcasted_iota(jnp.int32, segments.shape, 1)
    return (token_positions - starts).astype(jnp.float32)


def apply_rotation(values, token_positions):
    half = values.shape[-1] // 2
    freqs = base_theta ** (-jnp.arange(half, dtype=jnp.float32) * 2.0 / values.shape[-1])
    angles = token_positions[:, :, None, None] * freqs
    cosine = jnp.cos(angles)
    sine = jnp.sin(angles)
    first = values[..., :half]
    second = values[..., half:]
    return jnp.concatenate(
        [first * cosine - second * sine, second * cosine + first * sine], axis=-1
    )


def allowed(segments):
    sequence_length = segments.shape[1]
    query_at = lax.broadcasted_iota(jnp.int32, (sequence_length, sequence_length), 0)
    key_at = lax.broadcasted_iota(jnp.int32, (sequence_length, sequence_length), 1)
    return (segments[:, :, None] == segments[:, None, :]) & (key_at <= query_at)[None]


def dot_last(left, right):
    return lax.dot_general(
        left, right, (((1,), (1,)), ((), ())), preferred_element_type=jnp.float32
    )


def dot_first(left, right):
    return lax.dot_general(
        left, right, (((0,), (0,)), ((), ())), preferred_element_type=jnp.float32
    )


def simple_product(left, right):
    return jnp.dot(left, right, preferred_element_type=jnp.float32)


def attn_scores(query_block_rows, key_b, visible):
    scores = jnp.einsum(
        "bikgd,bjkd->bkgij", query_block_rows, key_b, preferred_element_type=jnp.float32
    ) * HEAD_SIZE ** (-0.5)
    return jnp.where(visible[:, None, None], scores, -1e30)


def local(
    tokens,
    segments,
    micro_live,
    cotangent,
    w_query,
    key_weight,
    value_weight,
    w_output,
    attn_gain,
    query_norm_gain,
    key_gain,
    w_gate,
    w_up,
    w_down,
    mlp_gain,
):
    micro_batch_index, sequence_length = segments.shape
    query_group_count = QUERY_HEADS // KEY_VALUE_HEADS
    token_total_count = tokens.shape[0]
    token_positions = doc_positions(segments)
    visible = allowed(segments)
    slot_live = (lax.broadcasted_iota(jnp.int32, (micro_batch_index, 1), 0) < micro_live[0]).astype(
        jnp.float32
    )
    row_live = jnp.broadcast_to(slot_live, (micro_batch_index, sequence_length)).reshape(
        token_total_count, 1
    )

    def head_prep(query_projected, key_projected, gain_query, gain_key):
        query_heads = query_projected.reshape(
            micro_batch_index, sequence_length, QUERY_HEADS, HEAD_SIZE
        )
        key_head_rows = key_projected.reshape(
            micro_batch_index, sequence_length, KEY_VALUE_HEADS, HEAD_SIZE
        )
        return (
            apply_rotation(root_mean_square_norm(query_heads, gain_query), token_positions),
            apply_rotation(root_mean_square_norm(key_head_rows, gain_key), token_positions),
        )

    attn_set = (
        lax.all_gather(w_query, "fsdp", axis=0, tiled=True),
        lax.all_gather(key_weight, "fsdp", axis=0, tiled=True),
        lax.all_gather(value_weight, "fsdp", axis=0, tiled=True),
        lax.all_gather(w_output, "fsdp", axis=0, tiled=True),
        lax.all_gather(attn_gain, "fsdp", axis=0, tiled=True),
        lax.all_gather(query_norm_gain, "fsdp", axis=0, tiled=True),
        lax.all_gather(key_gain, "fsdp", axis=0, tiled=True),
    )
    full_query, full_key, gathered_value_weight, full_output, full_again, full_qgain, full_kgain = (
        attn_set
    )
    norm_gain = full_again.astype(jnp.float32)
    qgain_f = full_qgain.astype(jnp.float32)
    kgain_f = full_kgain.astype(jnp.float32)
    inputs = tokens.astype(jnp.float32)
    normalized_input_rows = root_mean_square_norm(inputs, norm_gain).astype(jnp.bfloat16)
    query_projected = simple_product(normalized_input_rows, full_query)
    key_projected = simple_product(normalized_input_rows, full_key)
    value_block_rows = (
        simple_product(normalized_input_rows, gathered_value_weight)
        .astype(jnp.bfloat16)
        .reshape(micro_batch_index, sequence_length, KEY_VALUE_HEADS, HEAD_SIZE)
    )
    query_rotated, key_rot = head_prep(query_projected, key_projected, qgain_f, kgain_f)
    query_block_rows = query_rotated.astype(jnp.bfloat16).reshape(
        micro_batch_index, sequence_length, KEY_VALUE_HEADS, query_group_count, HEAD_SIZE
    )
    key_b = key_rot.astype(jnp.bfloat16)
    scores = attn_scores(query_block_rows, key_b, visible)
    top = jnp.max(scores, axis=-1, keepdims=True)
    log_total = top + jnp.log(jnp.sum(jnp.exp(scores - top), axis=-1, keepdims=True))
    probs_b = jnp.exp(scores - log_total).astype(jnp.bfloat16)
    context_b = jnp.einsum(
        "bkgij,bjkd->bikgd", probs_b, value_block_rows, preferred_element_type=jnp.float32
    )
    context_b = context_b.astype(jnp.bfloat16).reshape(token_total_count, QUERY_HEADS * HEAD_SIZE)
    middle = inputs + simple_product(context_b, full_output)
    mlp_set = (
        lax.all_gather(w_gate, "fsdp", axis=0, tiled=True),
        lax.all_gather(w_up, "fsdp", axis=0, tiled=True),
        lax.all_gather(w_down, "fsdp", axis=0, tiled=True),
        lax.all_gather(mlp_gain, "fsdp", axis=0, tiled=True),
    )
    full_gate, full_up, full_down, full_mgain = mlp_set
    mlp_norm_gain = full_mgain.astype(jnp.float32)
    normed_two_b = root_mean_square_norm(middle, mlp_norm_gain).astype(jnp.bfloat16)
    gate = simple_product(normed_two_b, full_gate)
    up_part = simple_product(normed_two_b, full_up)
    sigma = jax.nn.sigmoid(gate)
    silu_gate = gate * sigma
    act_b = (silu_gate * up_part).astype(jnp.bfloat16)
    layer_out = (row_live * (middle + simple_product(act_b, full_down))).astype(jnp.bfloat16)
    cot_b = cotangent * row_live.astype(jnp.bfloat16)
    grad_act = dot_last(cot_b, full_down)
    grad_gate_b = (grad_act * up_part * (sigma * (1.0 + gate * (1.0 - sigma)))).astype(jnp.bfloat16)
    grad_up_b = (grad_act * silu_gate).astype(jnp.bfloat16)
    grad_normed_two = dot_last(grad_gate_b, full_gate) + dot_last(grad_up_b, full_up)
    grad_down_w = dot_first(act_b, cot_b)
    grad_gate_w = dot_first(normed_two_b, grad_gate_b)
    grad_up_w = dot_first(normed_two_b, grad_up_b)
    _, pull_two = jax.vjp(root_mean_square_norm, middle, mlp_norm_gain)
    middle_part, grad_mgain = pull_two(grad_normed_two)
    grad_middle = cot_b.astype(jnp.float32) + middle_part
    full_query, full_key, gathered_value_weight, full_output, full_again, full_qgain, full_kgain = (
        lax.all_gather(w_query, "fsdp", axis=0, tiled=True),
        lax.all_gather(key_weight, "fsdp", axis=0, tiled=True),
        lax.all_gather(value_weight, "fsdp", axis=0, tiled=True),
        lax.all_gather(w_output, "fsdp", axis=0, tiled=True),
        lax.all_gather(attn_gain, "fsdp", axis=0, tiled=True),
        lax.all_gather(query_norm_gain, "fsdp", axis=0, tiled=True),
        lax.all_gather(key_gain, "fsdp", axis=0, tiled=True),
    )
    norm_gain = full_again.astype(jnp.float32)
    qgain_f = full_qgain.astype(jnp.float32)
    kgain_f = full_kgain.astype(jnp.float32)
    grad_attn_b = grad_middle.astype(jnp.bfloat16)
    grad_output_w = dot_first(context_b, grad_attn_b)
    grad_context_b = (
        dot_last(grad_attn_b, full_output)
        .astype(jnp.bfloat16)
        .reshape(micro_batch_index, sequence_length, KEY_VALUE_HEADS, query_group_count, HEAD_SIZE)
    )
    scores = attn_scores(query_block_rows, key_b, visible)
    probs = jnp.exp(scores - log_total)
    probs_b = probs.astype(jnp.bfloat16)
    value_weight_gradient = jnp.einsum(
        "bkgij,bikgd->bjkd", probs_b, grad_context_b, preferred_element_type=jnp.float32
    )
    grad_probs = jnp.einsum(
        "bikgd,bjkd->bkgij", grad_context_b, value_block_rows, preferred_element_type=jnp.float32
    )
    inner = jnp.sum(probs * grad_probs, axis=-1, keepdims=True)
    grad_scores_b = (probs * (grad_probs - inner)).astype(jnp.bfloat16)
    grad_query_rot = jnp.einsum(
        "bkgij,bjkd->bikgd", grad_scores_b, key_b, preferred_element_type=jnp.float32
    ) * HEAD_SIZE ** (-0.5)
    grad_key_rot = jnp.einsum(
        "bkgij,bikgd->bjkd", grad_scores_b, query_block_rows, preferred_element_type=jnp.float32
    ) * HEAD_SIZE ** (-0.5)
    _, pull_heads = jax.vjp(head_prep, query_projected, key_projected, qgain_f, kgain_f)
    grad_query_raw, grad_key_raw, grad_qgain, grad_kgain = pull_heads(
        (
            grad_query_rot.reshape(micro_batch_index, sequence_length, QUERY_HEADS, HEAD_SIZE),
            grad_key_rot,
        )
    )
    grad_query_b = grad_query_raw.astype(jnp.bfloat16)
    grad_key_b = grad_key_raw.astype(jnp.bfloat16)
    value_rows_gradient = value_weight_gradient.reshape(
        token_total_count, KEY_VALUE_HEADS * HEAD_SIZE
    ).astype(jnp.bfloat16)
    grad_normed = (
        dot_last(grad_query_b, full_query)
        + dot_last(grad_key_b, full_key)
        + dot_last(value_rows_gradient, gathered_value_weight)
    )
    grad_query_w = dot_first(normalized_input_rows, grad_query_b)
    grad_key_w = dot_first(normalized_input_rows, grad_key_b)
    grad_value_w = dot_first(normalized_input_rows, value_rows_gradient)
    _, pull_one = jax.vjp(root_mean_square_norm, inputs, norm_gain)
    input_part, grad_again = pull_one(grad_normed)
    grad_tokens = (grad_middle + input_part).astype(jnp.bfloat16)
    summed = tuple(
        (
            lax.psum_scatter(grad_query_w, "fsdp", scatter_dimension=0, tiled=True),
            lax.psum_scatter(grad_key_w, "fsdp", scatter_dimension=0, tiled=True),
            lax.psum_scatter(grad_value_w, "fsdp", scatter_dimension=0, tiled=True),
            lax.psum_scatter(grad_output_w, "fsdp", scatter_dimension=0, tiled=True),
            lax.psum_scatter(grad_again, "fsdp", scatter_dimension=0, tiled=True),
            lax.psum_scatter(grad_qgain, "fsdp", scatter_dimension=0, tiled=True),
            lax.psum_scatter(grad_kgain, "fsdp", scatter_dimension=0, tiled=True),
            lax.psum_scatter(grad_gate_w, "fsdp", scatter_dimension=0, tiled=True),
            lax.psum_scatter(grad_up_w, "fsdp", scatter_dimension=0, tiled=True),
            lax.psum_scatter(grad_down_w, "fsdp", scatter_dimension=0, tiled=True),
            lax.psum_scatter(grad_mgain, "fsdp", scatter_dimension=0, tiled=True),
        )
    )
    return (
        layer_out,
        grad_tokens,
        summed[0],
        summed[1],
        summed[2],
        summed[3],
        summed[4],
        summed[5],
        summed[6],
        summed[7],
        summed[8],
        summed[9],
        summed[10],
    )


def solution(mesh):
    return jax.shard_map(
        local,
        mesh=mesh,
        in_specs=(
            P("fsdp", None),
            P("fsdp", None),
            P("fsdp"),
            P("fsdp", None),
            P("fsdp", None),
            P("fsdp", None),
            P("fsdp", None),
            P("fsdp", None),
            P("fsdp"),
            P("fsdp"),
            P("fsdp"),
            P("fsdp", None),
            P("fsdp", None),
            P("fsdp", None),
            P("fsdp"),
        ),
        out_specs=(
            P("fsdp", None),
            P("fsdp", None),
            P("fsdp", None),
            P("fsdp", None),
            P("fsdp", None),
            P("fsdp", None),
            P("fsdp"),
            P("fsdp"),
            P("fsdp"),
            P("fsdp", None),
            P("fsdp", None),
            P("fsdp", None),
            P("fsdp"),
        ),
        check_vma=False,
    )
```

profile of v0, /device:TPU:0, one launch (start us, length us, event | category | flops | bytes accessed | tf_op | source)
XLA Modules:
  0.0 2821.7 jit_solution(6354077315156028194)
XLA Ops:
  13.0 42.1 %all-reduce.13 = (bf16[2048]{0:T(1024)(128)(2,1)S(1)}, bf16[128]{0:T(256)(128)(2,1)S(1)}, bf16[128]{0:T(256)(128)(2,1)S(1)}, bf16[2048]{0:T(1024)(128)(2,1)S(1)}) all-reduce(bf16[2048]{0:T(1024)(128)(2,1)S(1)} %dynamic-update-slice, bf16[128]{0:T(256)(128)(2,1)S(1)} %dynamic-update-slice.2, ...), channel_id=1, replica_groups=mesh['fsdp'=32] {'fsdp'}, use_global_device_ids=true, to_apply=%add.4 | all-reduce | flops 4352 | bytes 17408
  59.2 16.4 all-gather.10.cloned.1.call-done
  79.3 59.9 %all-gather.8.cloned.1.call-done = bf16[2048,1024]{1,0:T(8,128)(2,1)} async-done(((bf16[64,1024]{1,0:T(8,128)(2,1)}), bf16[2048,1024]{1,0:T(8,128)(2,1)}) %all-gather.8.cloned.1.call-update) | async-done | bytes 4194320 | tf_op jit(solution)/shard_map/all_gather | solution.py:113
  144.1 74.0 %all-gather.12.cloned.1.call-done = bf16[2048,2048]{1,0:T(8,128)(2,1)} async-done(((bf16[64,2048]{1,0:T(8,128)(2,1)}), bf16[2048,2048]{1,0:T(8,128)(2,1)}) %all-gather.12.cloned.1.call-update) | async-done | bytes 8388624 | tf_op jit(solution)/shard_map/all_gather | solution.py:111
  235.3 61.6 %all-gather.14.cloned.1.call-done = bf16[2048,2048]{1,0:T(8,128)(2,1)} async-done(((bf16[64,2048]{1,0:T(8,128)(2,1)}), bf16[2048,2048]{1,0:T(8,128)(2,1)}) %all-gather.14.cloned.1.call-update) | async-done | bytes 8388624 | tf_op jit(solution)/shard_map/all_gather | solution.py:114
  304.8 148.0 %all-gather.16.cloned.1.call-done = bf16[2048,6144]{1,0:T(8,128)(2,1)} async-done(((bf16[64,6144]{1,0:T(8,128)(2,1)}), bf16[2048,6144]{1,0:T(8,128)(2,1)}) %all-gather.16.cloned.1.call-update) | async-done | bytes 25165840 | tf_op jit(solution)/shard_map/all_gather | solution.py:149
  452.9 12.4 fusion.74
  465.3 143.1 %all-gather.18.cloned.1.call-done = bf16[2048,6144]{1,0:T(8,128)(2,1)} async-done(((bf16[64,6144]{1,0:T(8,128)(2,1)}), bf16[2048,6144]{1,0:T(8,128)(2,1)}) %all-gather.18.cloned.1.call-update) | async-done | bytes 25165840 | tf_op jit(solution)/shard_map/all_gather | solution.py:150
  608.4 12.6 fusion.75
  621.0 143.1 %all-gather.20.cloned.1.call-done = bf16[6144,2048]{1,0:T(8,128)(2,1)} async-done(((bf16[192,2048]{1,0:T(8,128)(2,1)}), bf16[6144,2048]{1,0:T(8,128)(2,1)}) %all-gather.20.cloned.1.call-update) | async-done | bytes 25165840 | tf_op jit(solution)/shard_map/all_gather | solution.py:151
  764.1 18.9 multiply_convert_fusion
  783.1 15.1 fusion.76
  798.2 16.4 multiply_reduce_fusion
  880.1 21.3 fusion.77
  901.8 21.5 fusion.78
  924.4 21.4 fusion.36
  958.7 40.2 %all-reduce.12 = (f32[2048]{0:T(1024)S(1)}, f32[128]{0:T(128)S(1)}, f32[128]{0:T(128)S(1)}, f32[2048]{0:T(1024)S(1)}) all-reduce(f32[2048]{0:T(1024)S(1)} %get-tuple-element.19, f32[128]{0:T(128)S(1)} %copy-done.58, f32[128]{0:T(128)S(1)} %copy-done.57, f32[2048]{0:T(1024)S(1)} %copy-done.54), channel_id=6, replica_groups=mesh['fsdp'=32] {'fsdp'}, use_global_device_ids=true, to_apply=%region_17.18.clone | all-reduce | flops 4352 | bytes 34816
  1004.3 12.0 fusion.2
  1016.3 114.3 %reduce-scatter.10.cloned.1.call-done = f32[64,1024]{1,0:T(8,128)} async-done(((f32[2048,1024]{1,0:T(8,128)}), f32[64,1024]{1,0:T(8,128)}) %reduce-scatter.10.cloned.1.call-update) | async-done | bytes 262160 | tf_op jit(solution)/shard_map/reduce_scatter | solution.py:236
  1130.6 181.6 %reduce-scatter.14.cloned.1.call-done = f32[64,2048]{1,0:T(8,128)} async-done(((f32[2048,2048]{1,0:T(8,128)}), f32[64,2048]{1,0:T(8,128)}) %reduce-scatter.14.cloned.1.call-update) | async-done | bytes 524304 | tf_op jit(solution)/shard_map/reduce_scatter | solution.py:238
  1312.2 187.3 %reduce-scatter.8.cloned.1.call-done = f32[64,2048]{1,0:T(8,128)} async-done(((f32[2048,2048]{1,0:T(8,128)}), f32[64,2048]{1,0:T(8,128)}) %reduce-scatter.8.cloned.1.call-update) | async-done | bytes 524304 | tf_op jit(solution)/shard_map/reduce_scatter | solution.py:235
  1499.5 440.1 %reduce-scatter.16.cloned.1.call-done = f32[64,6144]{1,0:T(8,128)} async-done(((f32[2048,6144]{1,0:T(8,128)}), f32[64,6144]{1,0:T(8,128)}) %reduce-scatter.16.cloned.1.call-update) | async-done | bytes 1572880 | tf_op jit(solution)/shard_map/reduce_scatter | solution.py:242
  1939.6 437.6 %reduce-scatter.18.cloned.1.call-done = f32[64,6144]{1,0:T(8,128)} async-done(((f32[2048,6144]{1,0:T(8,128)}), f32[64,6144]{1,0:T(8,128)}) %reduce-scatter.18.cloned.1.call-update) | async-done | bytes 1572880 | tf_op jit(solution)/shard_map/reduce_scatter | solution.py:243
  2377.2 437.5 %reduce-scatter.20.cloned.1.call-done = f32[192,2048]{1,0:T(8,128)} async-done(((f32[6144,2048]{1,0:T(8,128)}), f32[192,2048]{1,0:T(8,128)}) %reduce-scatter.20.cloned.1.call-update) | async-done | bytes 1572880 | tf_op jit(solution)/shard_map/reduce_scatter | solution.py:244
  (251 shorter events, 127.3 us)
Async XLA Ops:
  7.2 68.4 %all-gather.10.cloned.1.call-start = ((), (), s32[]{:S(2)}) async-start(), calls=%async_computation.8 | async-start | bytes 4325376 | tf_op jit(solution)/shard_map/all_gather | solution.py:112
  8.0 49.7 %copy-start.51 = (s32[3,64]{1,0:T(4,128)S(1)}, s32[3,64]{1,0:T(4,128)}, u32[]{:S(2)}) copy-start(s32[3,64]{1,0:T(4,128)} %param.16) | copy-start | bytes 2308
  8.0 49.8 %copy-start = (bf16[192,2048]{1,0:T(8,128)(2,1)S(1)}, bf16[192,2048]{1,0:T(8,128)(2,1)}, u32[]{:S(2)}) copy-start(bf16[192,2048]{1,0:T(8,128)(2,1)} %param.15) | copy-start | bytes 2359300
  8.0 131.2 %all-gather.8.cloned.1.call-start = ((), (), s32[]{:S(2)}) async-start(), calls=%async_computation.7 | async-start | bytes 4325376 | tf_op jit(solution)/shard_map/all_gather | solution.py:113
  8.7 209.4 %all-gather.12.cloned.1.call-start = ((), (), s32[]{:S(2)}) async-start(), calls=%async_computation.9 | async-start | bytes 8650752 | tf_op jit(solution)/shard_map/all_gather | solution.py:111
  9.5 287.4 %all-gather.14.cloned.1.call-start = ((), (), s32[]{:S(2)}) async-start(), calls=%async_computation.10 | async-start | bytes 8650752 | tf_op jit(solution)/shard_map/all_gather | solution.py:114
  10.0 442.8 %all-gather.16.cloned.1.call-start = ((), (), s32[]{:S(2)}) async-start(), calls=%async_computation.11 | async-start | bytes 25952256 | tf_op jit(solution)/shard_map/all_gather | solution.py:149
  10.6 597.8 %all-gather.18.cloned.1.call-start = ((), (), s32[]{:S(2)}) async-start(), calls=%async_computation.12 | async-start | bytes 25952256 | tf_op jit(solution)/shard_map/all_gather | solution.py:150
  11.2 752.9 %all-gather.20.cloned.1.call-start = ((), (), s32[]{:S(2)}) async-start(), calls=%async_computation.13 | async-start | bytes 25952256 | tf_op jit(solution)/shard_map/all_gather | solution.py:151
  11.9 1004.4 %reduce-scatter.12.cloned.1.call-start = ((), (), s32[]{:S(2)}) async-start(), calls=%async_computation.16 | async-start | bytes 8650752 | tf_op jit(solution)/shard_map/reduce_scatter | solution.py:237
  59.2 83.6 %copy-start.30 = (f32[3,64,64]{2,1,0:T(8,128)}, f32[3,64,64]{2,1,0:T(8,128)S(1)}, u32[]{:S(2)}) copy-start(f32[3,64,64]{2,1,0:T(8,128)S(1)} %get-tuple-element.42) | copy-start | bytes 147460
  59.2 83.6 %copy-start.34 = (f32[3,64,64]{2,1,0:T(8,128)}, f32[3,64,64]{2,1,0:T(8,128)S(1)}, u32[]{:S(2)}) copy-start(f32[3,64,64]{2,1,0:T(8,128)S(1)} %get-tuple-element.43) | copy-start | bytes 147460
  79.0 63.6 %copy-start.3 = (f32[24,8,8,128]{3,2,1,0:T(8,128)}, f32[24,8,8,128]{3,2,1,0:T(8,128)S(1)}, u32[]{:S(2)}) copy-start(f32[24,8,8,128]{3,2,1,0:T(8,128)S(1)} %copy.148) | copy-start | bytes 2359300
  79.3 63.2 %copy-start.47 = (f32[3,64,8]{1,2,0:T(8,128)}, f32[3,64,8]{1,2,0:T(8,128)S(1)}, u32[]{:S(2)}) copy-start(f32[3,64,8]{1,2,0:T(8,128)S(1)} %copy.113) | copy-start | bytes 18436
  142.5 86.7 %copy-start.23 = (bf16[3,64,8,128,1]{3,2,1,0,4:T(8,128)(2,1)}, bf16[3,64,8,128,1]{3,2,1,0,4:T(8,128)(2,1)S(1)}, u32[]{:S(2)}) copy-start(bf16[3,64,8,128,1]{3,2,1,0,4:T(8,128)(2,1)S(1)} %bitcast_bitcast_fusion) | copy-start | bytes 1179652
  235.3 68.4 %copy-start.50 = (f32[2048]{0:T(1024)S(1)}, f32[2048]{0:T(1024)}, u32[]{:S(2)}) copy-start(f32[2048]{0:T(1024)} %convert_element_type.126) | copy-start | bytes 24580
  465.3 298.8 %copy-start.59 = (bf16[192]{0:T(256)(128)(2,1)S(1)}, bf16[192]{0:T(256)(128)(2,1)}, u32[]{:S(2)}) copy-start(bf16[192]{0:T(256)(128)(2,1)} %convert_element_type.130) | copy-start | bytes 1156
  835.6 295.0 %reduce-scatter.10.cloned.1.call-start = ((), (), s32[]{:S(2)}) async-start(), calls=%async_computation.15 | async-start | bytes 8650752 | tf_op jit(solution)/shard_map/reduce_scatter | solution.py:236
  848.4 463.8 %reduce-scatter.14.cloned.1.call-start = ((), (), s32[]{:S(2)}) async-start(), calls=%async_computation.17 | async-start | bytes 17301504 | tf_op jit(solution)/shard_map/reduce_scatter | solution.py:238
  859.2 640.4 %reduce-scatter.8.cloned.1.call-start = ((), (), s32[]{:S(2)}) async-start(), calls=%async_computation.14 | async-start | bytes 17301504 | tf_op jit(solution)/shard_map/reduce_scatter | solution.py:235
  879.0 1060.6 %reduce-scatter.16.cloned.1.call-start = ((), (), s32[]{:S(2)}) async-start(), calls=%async_computation.18 | async-start | bytes 51904512 | tf_op jit(solution)/shard_map/reduce_scatter | solution.py:242
  901.5 1475.7 %reduce-scatter.18.cloned.1.call-start = ((), (), s32[]{:S(2)}) async-start(), calls=%async_computation.19 | async-start | bytes 51904512 | tf_op jit(solution)/shard_map/reduce_scatter | solution.py:243
  923.3 1891.4 %reduce-scatter.20.cloned.1.call-start = ((), (), s32[]{:S(2)}) async-start(), calls=%async_computation.20 | async-start | bytes 51904512 | tf_op jit(solution)/shard_map/reduce_scatter | solution.py:244
  955.8 45.5 %copy-start.6 = (f32[192,2048]{1,0:T(8,128)S(1)}, f32[192,2048]{1,0:T(8,128)}, u32[]{:S(2)}) copy-start(f32[192,2048]{1,0:T(8,128)} %copy-done.5) | copy-start | bytes 4718596
  (57 other events, 184.1 us)
Sparse Core Ops, SparseCore 0:
  10.9 64.6 all-gather.9
  78.4 60.6 all-gather.7
  142.0 75.9 all-gather.11
  220.8 76.0 all-gather.13
  299.6 153.2 all-gather.15
  455.6 152.7 all-gather.17
  611.3 152.7 all-gather.19
  835.7 147.2 reduce-scatter.11
  985.9 144.7 reduce-scatter.9
  1133.4 178.8 reduce-scatter.13
  1315.1 184.3 reduce-scatter.7
  1506.4 433.1 reduce-scatter.15
  1946.6 430.5 reduce-scatter.17
  2384.0 430.6 reduce-scatter.19
where the time goes:
time: 2830 us; the launch traced here: 2820 us
  waiting for transfers between devices  2450 us (87%)
  matrix products  222 us (8%)
  blocking collectives  82.4 us (3%)
  local copies, waits for them, and re-layouts  28.3 us (1%)
    reduce_scatter x1, waiting for transfers between devices, local(): lax.psum_scatter(grad_gate_w, 'fsdp', scatter_dimension=0, tiled=True)  440 us
    reduce_scatter x1, waiting for transfers between devices, local(): lax.psum_scatter(grad_up_w, 'fsdp', scatter_dimension=0, tiled=True)  438 us
    reduce_scatter x1, waiting for transfers between devices, local(): lax.psum_scatter(grad_down_w, 'fsdp', scatter_dimension=0, tiled=True)  438 us
    reduce_scatter x1, waiting for transfers between devices, local(): lax.psum_scatter(grad_query_w, 'fsdp', scatter_dimension=0, tiled=True)  187 us
    reduce_scatter x1, waiting for transfers between devices, local(): lax.psum_scatter(grad_output_w, 'fsdp', scatter_dimension=0, tiled=True)  182 us
    all_gather x1, waiting for transfers between devices, local(): lax.all_gather(w_gate, 'fsdp', axis=0, tiled=True)  148 us
    all_gather x1, waiting for transfers between devices, local(): lax.all_gather(w_up, 'fsdp', axis=0, tiled=True)  143 us
    all_gather x1, waiting for transfers between devices, local(): lax.all_gather(w_down, 'fsdp', axis=0, tiled=True)  143 us
  transfers between devices with their start and end apart: 14, of which 13 were waited for; matrix products, arithmetic and copies ran while one was open for 7% of the time, Pallas kernels for 0%

commit v1 on v0

v1 whole, which is shorter than its diff:
```python
import functools

import jax
import jax.numpy as jnp
from jax import lax
from jax.experimental import pallas as pl
from jax.experimental.pallas import tpu as pltpu
from jax.sharding import PartitionSpec as P

QUERY_HEADS = 16
KEY_VALUE_HEADS = 8
HEAD_SIZE = 128
TEAM = 8
CHUNKS = 2

epsilon = 1e-06
base_theta = 1000000.0
MESH = pl.DeviceIdType.MESH
f32 = jnp.float32
bf16 = jnp.bfloat16


def root_mean_square_norm(values, gain):
    return values * lax.rsqrt(jnp.mean(values * values, axis=-1, keepdims=True) + epsilon) * gain


def doc_positions(segments):
    earlier = (segments[:, None, :] < segments[:, :, None]).astype(jnp.int32)
    starts = jnp.sum(earlier, axis=2)
    token_positions = lax.broadcasted_iota(jnp.int32, segments.shape, 1)
    return (token_positions - starts).astype(jnp.float32)


def rotation_tables(token_positions):
    half = HEAD_SIZE // 2
    freqs = base_theta ** (-jnp.arange(half, dtype=jnp.float32) * 2.0 / HEAD_SIZE)
    angles = token_positions[:, :, None, None] * freqs
    return jnp.cos(angles), jnp.sin(angles)


def apply_rotation(values, tables):
    cosine, sine = tables
    half = values.shape[-1] // 2
    first = values[..., :half]
    second = values[..., half:]
    return jnp.concatenate(
        [first * cosine - second * sine, second * cosine + first * sine], axis=-1
    )


def allowed(segments):
    sequence_length = segments.shape[1]
    query_at = lax.broadcasted_iota(jnp.int32, (sequence_length, sequence_length), 0)
    key_at = lax.broadcasted_iota(jnp.int32, (sequence_length, sequence_length), 1)
    return (segments[:, :, None] == segments[:, None, :]) & (key_at <= query_at)[None]


def dot_last(left, right):
    return lax.dot_general(
        left, right, (((1,), (1,)), ((), ())), preferred_element_type=jnp.float32
    )


def dot_first(left, right):
    return lax.dot_general(
        left, right, (((0,), (0,)), ((), ())), preferred_element_type=jnp.float32
    )


def simple_product(left, right):
    return jnp.dot(left, right, preferred_element_type=jnp.float32)


def flipped(index, mask):
    for bit in (1, 2, 4):
        if mask & bit:
            index = index + bit * (1 - 2 * lax.rem(lax.div(index, bit), 2))
    return index


def greet(me, masks, others=()):
    barrier = pltpu.get_barrier_semaphore()
    for mask in masks:
        pl.semaphore_signal(
            barrier, inc=1, device_id=(flipped(me, mask),), device_id_type=MESH
        )
    for other in others:
        pl.semaphore_signal(barrier, inc=1, device_id=(other,), device_id_type=MESH)
    pl.semaphore_wait(barrier, len(masks) + len(others))


def remote(source, target, send, receive, device):
    return pltpu.make_async_remote_copy(
        src_ref=source,
        dst_ref=target,
        send_sem=send,
        recv_sem=receive,
        device_id=(device,),
        device_id_type=MESH,
    )


def params(collective, limit=None):
    if limit is None:
        return pltpu.CompilerParams(collective_id=collective, has_side_effects=True)
    return pltpu.CompilerParams(
        collective_id=collective, has_side_effects=True, vmem_limit_bytes=limit
    )


def swap_kernel(x_ref, o_ref, send, receive, own):
    me = lax.axis_index("fsdp")
    place = lax.rem(me, TEAM)
    keep = pltpu.make_async_copy(x_ref.at[place], o_ref.at[place], own)
    keep.start()
    greet(me, range(1, TEAM))
    copies = []
    for mask in (6, 7, 2, 3, 4, 5, 1):
        copy = remote(
            x_ref.at[flipped(place, mask)],
            o_ref.at[place],
            send.at[mask - 1],
            receive.at[mask - 1],
            flipped(me, mask),
        )
        copy.start()
        copies.append(copy)
    for copy in copies:
        copy.wait()
    keep.wait()


def swap(x, collective):
    return pl.pallas_call(
        swap_kernel,
        out_shape=jax.ShapeDtypeStruct(x.shape, x.dtype),
        in_specs=[pl.BlockSpec(memory_space=pl.ANY)],
        out_specs=pl.BlockSpec(memory_space=pl.ANY),
        scratch_shapes=[
            pltpu.SemaphoreType.DMA((TEAM - 1,)),
            pltpu.SemaphoreType.DMA((TEAM - 1,)),
            pltpu.SemaphoreType.DMA,
        ],
        compiler_params=params(collective),
    )(x)


def gather_kernel(x_ref, o_ref, send, receive, own):
    me = lax.axis_index("fsdp")
    place = lax.rem(me, TEAM)
    rows = x_ref.shape[0]
    half = rows // 2
    keep = pltpu.make_async_copy(x_ref, o_ref.at[place], own)
    keep.start()
    greet(me, (1, 2, 4))

    def part(ref, which):
        return ref.at[pl.ds(which * half, half)]

    def begin(source, slot, which, mask, k):
        copy = remote(
            source, part(o_ref.at[slot], which), send.at[k], receive.at[k], flipped(me, mask)
        )
        copy.start()
        return copy

    def relay(slot, which, mask, k):
        return begin(part(o_ref.at[slot], which), slot, which, mask, k)

    by_x, by_y, by_both = flipped(place, 2), flipped(place, 4), flipped(place, 6)
    x0 = begin(part(x_ref, 0), place, 0, 2, 0)
    y1 = begin(part(x_ref, 1), place, 1, 4, 1)
    x1 = begin(part(x_ref, 1), place, 1, 2, 2)
    y0 = begin(part(x_ref, 0), place, 0, 4, 3)
    late = [begin(part(x_ref, 0), place, 0, 1, 6), begin(part(x_ref, 1), place, 1, 1, 7)]
    x0.wait_recv()
    d0 = relay(by_x, 0, 4, 4)
    y1.wait_recv()
    d1 = relay(by_y, 1, 2, 5)
    late.append(relay(by_x, 0, 1, 8))
    late.append(relay(by_y, 1, 1, 9))
    x1.wait_recv()
    late.append(relay(by_x, 1, 1, 10))
    y0.wait_recv()
    late.append(relay(by_y, 0, 1, 11))
    d0.wait_recv()
    late.append(relay(by_both, 0, 1, 12))
    d1.wait_recv()
    late.append(relay(by_both, 1, 1, 13))
    for copy in late:
        copy.wait_recv()
    for copy in (x0, y1, x1, y0, d0, d1, *late):
        copy.wait_send()
    keep.wait()


def gather(x, collective):
    rows, width = x.shape
    whole = pl.pallas_call(
        gather_kernel,
        out_shape=jax.ShapeDtypeStruct((TEAM, rows, width), x.dtype),
        in_specs=[pl.BlockSpec(memory_space=pl.ANY)],
        out_specs=pl.BlockSpec(memory_space=pl.ANY),
        scratch_shapes=[
            pltpu.SemaphoreType.DMA((14,)),
            pltpu.SemaphoreType.DMA((14,)),
            pltpu.SemaphoreType.DMA,
        ],
        compiler_params=params(collective),
    )(x)
    return whole.reshape(TEAM * rows, width)


def reduce_kernel(part, out, mix, from_core, from_x, from_y, send, receive):
    me = lax.axis_index("fsdp")
    place = lax.rem(me, TEAM)
    rows = out.shape[0]
    half = rows // 2
    step = 16
    targets = [flipped(place, mask) for mask in (6, 2, 4, 0)]
    greet(me, (1, 2, 4))

    across = []
    for j, target in enumerate(targets):
        copy = remote(
            part.at[flipped(target, 1)], from_core.at[j], send.at[j], receive.at[j], flipped(me, 1)
        )
        copy.start()
        across.append(copy)

    def combine(j):
        across[j].wait_recv()

        @pl.loop(0, rows // step)
        def _(i):
            at = pl.ds(i * step, step)
            mix[j, at, :] = (
                part[targets[j], at, :].astype(f32) + from_core[j, at, :].astype(f32)
            ).astype(bf16)

    def begin(j, which, ref, slot, mask, k):
        copy = remote(
            mix.at[j, pl.ds(which * half, half)],
            ref.at[slot],
            send.at[k],
            receive.at[k],
            flipped(me, mask),
        )
        copy.start()
        return copy

    def add_relayed(j, which, ref):
        @pl.loop(0, half // step)
        def _(i):
            at = pl.ds(which * half + i * step, step)
            mix[j, at, :] = (
                mix[j, at, :].astype(f32) + ref[0, pl.ds(i * step, step), :].astype(f32)
            ).astype(bf16)

    combine(0)
    d_x = begin(0, 0, from_x, 0, 2, 4)
    d_y = begin(0, 1, from_y, 0, 4, 5)
    combine(1)
    x_0 = begin(1, 0, from_x, 1, 2, 6)
    combine(2)
    y_1 = begin(2, 1, from_y, 1, 4, 7)
    d_x.wait_recv()
    add_relayed(2, 0, from_x)
    y_0 = begin(2, 0, from_y, 2, 4, 8)
    d_y.wait_recv()
    add_relayed(1, 1, from_y)
    x_1 = begin(1, 1, from_x, 2, 2, 9)
    across[3].wait_recv()

    @pl.loop(0, rows // step)
    def _(i):
        at = pl.ds(i * step, step)
        out[at, :] = part[place, at, :].astype(f32) + from_core[3, at, :].astype(f32)

    def finish(which, slot_x, slot_y):
        @pl.loop(0, half // step)
        def _(i):
            at = pl.ds(which * half + i * step, step)
            here = pl.ds(i * step, step)
            out[at, :] = out[at, :] + (
                from_x[slot_x, here, :].astype(f32) + from_y[slot_y, here, :].astype(f32)
            )

    x_0.wait_recv()
    y_0.wait_recv()
    finish(0, 1, 2)
    y_1.wait_recv()
    x_1.wait_recv()
    finish(1, 2, 1)
    for copy in (*across, d_x, d_y, x_0, x_1, y_0, y_1):
        copy.wait_send()


def reduce(part, collective):
    rows, width = part.shape[0] // TEAM, part.shape[1]
    vmem = pl.BlockSpec(memory_space=pltpu.VMEM)
    return pl.pallas_call(
        reduce_kernel,
        out_shape=jax.ShapeDtypeStruct((rows, width), f32),
        in_specs=[vmem],
        out_specs=vmem,
        scratch_shapes=[
            pltpu.VMEM((4, rows, width), bf16),
            pltpu.VMEM((4, rows, width), bf16),
            pltpu.VMEM((3, rows // 2, width), bf16),
            pltpu.VMEM((3, rows // 2, width), bf16),
            pltpu.SemaphoreType.DMA((10,)),
            pltpu.SemaphoreType.DMA((10,)),
        ],
        compiler_params=params(collective, 40 * 2**20),
    )(part.reshape(TEAM, rows, width))


def spread_kernel(planes, back, x_ref, o_ref, send, receive, own):
    me = lax.axis_index("fsdp")
    place = lax.rem(me, TEAM)
    team = me - place
    greet(me, range(1, TEAM))

    def route(k, at_heads):
        if at_heads:
            block = planes * place + k
            return lax.rem(block, TEAM), lax.div(block, TEAM)
        block = TEAM * k + place
        return lax.div(block, planes), lax.rem(block, planes)

    def copies(k):
        partner, there = route(k, back)
        over = remote(x_ref.at[k], o_ref.at[there], send.at[k], receive.at[there], team + partner)
        here = pltpu.make_async_copy(x_ref.at[k], o_ref.at[there], own.at[k])
        return partner, over, here

    def incoming(k):
        partner, _ = route(k, not back)
        return partner, remote(x_ref.at[k], o_ref.at[k], send.at[k], receive.at[k], team + partner)

    for k in range(planes):
        partner, over, here = copies(k)
        pl.when(partner != place)(over.start)
        pl.when(partner == place)(here.start)
    for k in range(planes):
        partner, over, here = copies(k)
        pl.when(partner != place)(over.wait_send)
        pl.when(partner == place)(here.wait)
        partner, arriving = incoming(k)
        pl.when(partner != place)(arriving.wait_recv)


def spread(x, planes, back, collective):
    rows = x.shape[0] // planes
    moved = pl.pallas_call(
        functools.partial(spread_kernel, planes, back),
        out_shape=jax.ShapeDtypeStruct((planes, rows, x.shape[1]), x.dtype),
        in_specs=[pl.BlockSpec(memory_space=pl.ANY)],
        out_specs=pl.BlockSpec(memory_space=pl.ANY),
        scratch_shapes=[
            pltpu.SemaphoreType.DMA((planes,)),
            pltpu.SemaphoreType.DMA((planes,)),
            pltpu.SemaphoreType.DMA((planes,)),
        ],
        compiler_params=params(collective),
    )(x.reshape(planes, rows, x.shape[1]))
    return moved.reshape(x.shape)


def open_kernel(
    planes,
    qkv_in,
    gate_up_in,
    output_in,
    tokens_in,
    small_in,
    qkv,
    gate_up,
    output_raw,
    output,
    tokens,
    small,
    send,
    receive,
    own,
):
    me = lax.axis_index("fsdp")
    place = lax.rem(me, TEAM)
    plane = lax.div(me, TEAM)
    team = me - place
    total_devices = planes * TEAM
    others = [lax.rem(me + TEAM * k, total_devices) for k in range(1, planes)]
    rows = tokens_in.shape[0]
    half = rows // 2
    counter = iter(range(10**6))
    chunks = gate_up_in.shape[0]

    keeps = []
    locals_ = iter(range(10**6))

    def keep(source, target):
        copy = pltpu.make_async_copy(source, target, own.at[next(locals_)])
        copy.start()
        return copy

    keep_qkv = keep(qkv_in.at[place], qkv.at[plane, place])
    keep_output = keep(output_in, output_raw.at[plane])
    keep_small = keep(small_in, small.at[me])
    keeps.append(keep(tokens_in, tokens.at[place]))
    for c in range(chunks):
        keeps.append(keep(gate_up_in.at[c, place], gate_up.at[c, place]))
    greet(me, range(1, TEAM), others)

    started = []

    def begin(source, target, device):
        k = next(counter)
        copy = remote(source, target, send.at[k], receive.at[k], device)
        copy.start()
        started.append(copy)
        return copy

    masks = (6, 7, 2, 3, 4, 5, 1)
    swaps = [
        begin(qkv_in.at[flipped(place, m)], qkv.at[plane, place], flipped(me, m)) for m in masks
    ]
    near = [begin(small_in, small.at[me], flipped(me, m)) for m in masks]

    def line(ref):
        up, down = [next(counter) for _ in range(planes - 1)], [
            next(counter) for _ in range(planes - 1)
        ]

        def passing(step, sign, ks, source):
            block = jnp.clip(source, 0, planes - 1)
            beyond = jnp.clip(plane + sign, 0, planes - 1) * TEAM + place
            return remote(
                ref.at[block], ref.at[block], send.at[ks[step]], receive.at[ks[step]], beyond
            )

        def goes(step, sign):
            source, onward = plane - sign * step, plane + sign
            return (
                (source >= 0) & (source <= planes - 1) & (onward >= 0) & (onward <= planes - 1)
            )

        def start(step):
            for sign, ks in ((1, up), (-1, down)):
                going = passing(step, sign, ks, plane - sign * step)
                pl.when(goes(step, sign))(going.start)

        def arrive(step):
            for sign, ks in ((1, up), (-1, down)):
                source = plane - sign * (step + 1)
                coming = passing(step, sign, ks, source)
                pl.when((source >= 0) & (source <= planes - 1))(coming.wait_recv)

        def sent(step):
            for sign, ks in ((1, up), (-1, down)):
                going = passing(step, sign, ks, plane - sign * step)
                pl.when(goes(step, sign))(going.wait_send)

        return start, arrive, sent

    qkv_start, qkv_arrive, qkv_sent = line(qkv)
    out_start, out_arrive, out_sent = line(output_raw)

    for copy in swaps:
        copy.wait_recv()
    keep_qkv.wait()
    keep_output.wait()
    qkv_start(0)
    out_start(0)

    def part(ref, which):
        return ref.at[pl.ds(which * half, half)]

    def relay(slot, which, mask):
        ref = part(tokens.at[slot], which)
        return begin(ref, ref, flipped(me, mask))

    def first(which, mask):
        return begin(part(tokens_in, which), part(tokens.at[place], which), flipped(me, mask))

    by_x, by_y, by_both = flipped(place, 2), flipped(place, 4), flipped(place, 6)
    x0, y1, x1, y0 = first(0, 2), first(1, 4), first(1, 2), first(0, 4)
    late = [first(0, 1), first(1, 1)]
    for copy in near:
        copy.wait_recv()
    keep_small.wait()
    slots = small.at[pl.ds(team, TEAM)]
    far = [begin(slots, slots, other) for other in others]
    x0.wait_recv()
    d0 = relay(by_x, 0, 4)
    y1.wait_recv()
    d1 = relay(by_y, 1, 2)
    late += [relay(by_x, 0, 1), relay(by_y, 1, 1)]
    gate_ups = [
        begin(gate_up_in.at[c, flipped(place, m)], gate_up.at[c, place], flipped(me, m))
        for c in range(chunks)
        for m in masks
    ]
    for step in range(planes - 1):
        qkv_arrive(step)
        if step < planes - 2:
            qkv_start(step + 1)
        out_arrive(step)
        if step < planes - 2:
            out_start(step + 1)
        if step == 0:
            x1.wait_recv()
            late.append(relay(by_x, 1, 1))
            y0.wait_recv()
            late.append(relay(by_y, 0, 1))
            d0.wait_recv()
            late.append(relay(by_both, 0, 1))
            d1.wait_recv()
            late.append(relay(by_both, 1, 1))

    spread_send = [next(counter) for _ in range(planes)]
    spread_receive = [next(counter) for _ in range(planes)]

    spread_own = [next(locals_) for _ in range(planes)]

    def outgoing(k):
        block = TEAM * k + place
        partner, there = lax.div(block, planes), lax.rem(block, planes)
        over = remote(
            output_raw.at[k],
            output.at[there],
            send.at[spread_send[k]],
            receive.at[spread_receive[0] + there],
            team + partner,
        )
        here = pltpu.make_async_copy(output_raw.at[k], output.at[there], own.at[spread_own[k]])
        return partner, over, here

    def incoming(k):
        partner = lax.rem(planes * place + k, TEAM)
        return partner, remote(
            output_raw.at[k],
            output.at[k],
            send.at[spread_send[k]],
            receive.at[spread_receive[k]],
            team + partner,
        )

    for k in range(planes):
        partner, over, here = outgoing(k)
        pl.when(partner != place)(over.start)
        pl.when(partner == place)(here.start)
    for copy in (*far, *gate_ups, *late):
        copy.wait_recv()
    for k in range(planes):
        partner, over, here = outgoing(k)
        pl.when(partner != place)(over.wait_send)
        pl.when(partner == place)(here.wait)
        partner, arriving = incoming(k)
        pl.when(partner != place)(arriving.wait_recv)
    for step in range(planes - 1):
        qkv_sent(step)
        out_sent(step)
    for copy in started:
        copy.wait_send()
    for copy in keeps:
        copy.wait()


def opening(qkv, gate_up, output, tokens, small, planes, collective):
    links = 7 + 7 + 4 * (planes - 1) + 14 + planes - 1 + 7 * gate_up.shape[0] + 2 * planes
    anywhere = pl.BlockSpec(memory_space=pl.ANY)
    like = jax.ShapeDtypeStruct
    return pl.pallas_call(
        functools.partial(open_kernel, planes),
        out_shape=(
            like((planes, *qkv.shape), bf16),
            like(gate_up.shape, bf16),
            like((planes, *output.shape), bf16),
            like((planes, *output.shape), bf16),
            like((TEAM, *tokens.shape), bf16),
            like((planes * TEAM, *small.shape), bf16),
        ),
        in_specs=[anywhere] * 5,
        out_specs=(anywhere,) * 6,
        scratch_shapes=[
            pltpu.SemaphoreType.DMA((links,)),
            pltpu.SemaphoreType.DMA((links,)),
            pltpu.SemaphoreType.DMA((4 + gate_up.shape[0] + planes,)),
        ],
        compiler_params=params(collective),
    )(qkv, gate_up, output, tokens, small)


def total_kernel(planes, x_ref, o_ref, near_in, mid, far_in, send, receive):
    me = lax.axis_index("fsdp")
    place = lax.rem(me, TEAM)
    plane = lax.div(me, TEAM)
    others = [lax.rem(me + TEAM * k, planes * TEAM) for k in range(1, planes)]
    greet(me, range(1, TEAM), others)
    near = []
    for mask in range(1, TEAM):
        copy = remote(
            x_ref.at[flipped(place, mask)],
            near_in.at[mask - 1],
            send.at[mask - 1],
            receive.at[mask - 1],
            flipped(me, mask),
        )
        copy.start()
        near.append(copy)
    for copy in near:
        copy.wait_recv()
    summed = x_ref[place]
    for mask in range(1, TEAM):
        summed = summed + near_in[mask - 1]
    mid[...] = summed
    far = []
    for k, other in enumerate(others):
        copy = remote(
            mid.at[lax.rem(plane + k + 1, planes)],
            far_in.at[k],
            send.at[TEAM - 1 + k],
            receive.at[TEAM - 1 + k],
            other,
        )
        copy.start()
        far.append(copy)
    for copy in far:
        copy.wait_recv()
    result = mid[plane]
    for k in range(planes - 1):
        result = result + far_in[k]
    o_ref[...] = result
    for copy in (*near, *far):
        copy.wait_send()


def total(x, planes, collective):
    links = TEAM - 1 + planes - 1
    block = x.shape[2:]
    vmem = pl.BlockSpec(memory_space=pltpu.VMEM)
    return pl.pallas_call(
        functools.partial(total_kernel, planes),
        out_shape=jax.ShapeDtypeStruct(block, x.dtype),
        in_specs=[vmem],
        out_specs=vmem,
        scratch_shapes=[
            pltpu.VMEM((TEAM - 1, planes, *block), x.dtype),
            pltpu.VMEM((planes, *block), x.dtype),
            pltpu.VMEM((planes - 1, *block), x.dtype),
            pltpu.SemaphoreType.DMA((links,)),
            pltpu.SemaphoreType.DMA((links,)),
        ],
        compiler_params=params(collective),
    )(x)


def padded(rows, height, width, dtype):
    rows = [jnp.pad(r, ((0, 0), (0, width - r.shape[1]))) for r in rows]
    block = jnp.concatenate(rows, axis=0).astype(dtype)
    return jnp.pad(block, ((0, height - block.shape[0]), (0, 0)))


def local(
    devices,
    tokens,
    segments,
    micro_live,
    cotangent,
    w_query,
    key_weight,
    value_weight,
    w_output,
    attn_gain,
    query_norm_gain,
    key_gain,
    w_gate,
    w_up,
    w_down,
    mlp_gain,
):
    planes = devices // TEAM
    lines = [[place + TEAM * k for k in range(planes)] for place in range(TEAM)]
    slots, sequence = segments.shape
    token_count, width = tokens.shape
    groups = QUERY_HEADS // KEY_VALUE_HEADS
    rows = w_query.shape[0]
    ff_rows = w_down.shape[0]
    ff_part = ff_rows // CHUNKS
    team_slots = TEAM * slots
    head_width = groups * HEAD_SIZE
    me = lax.axis_index("fsdp")
    plane = me // TEAM

    def gather_line(x):
        return lax.all_gather(x, "fsdp", axis=0, tiled=True, axis_index_groups=lines)

    def sum_line(x):
        return lax.psum_scatter(
            x, "fsdp", scatter_dimension=0, tiled=True, axis_index_groups=lines
        )

    slot_live = (lax.broadcasted_iota(jnp.int32, (slots, 1), 0) < micro_live[0]).astype(f32)
    row_live = jnp.broadcast_to(slot_live, (slots, sequence)).reshape(token_count, 1)

    qkv_send = jnp.concatenate(
        [
            w.reshape(rows, TEAM, w.shape[1] // TEAM).transpose(1, 0, 2)
            for w in (w_query, key_weight, value_weight)
        ],
        axis=2,
    )
    gate_up_send = jnp.concatenate(
        [
            w.reshape(rows, planes, TEAM, CHUNKS, ff_part)
            .transpose(3, 2, 0, 1, 4)
            .reshape(CHUNKS, TEAM, rows, planes * ff_part)
            for w in (w_gate, w_up)
        ],
        axis=3,
    )
    small_send = padded(
        [
            attn_gain[None],
            mlp_gain[None],
            query_norm_gain[None],
            key_gain[None],
            segments.astype(bf16),
        ],
        16,
        128,
        bf16,
    )
    qkv_weight, gate_up_slices, _, output_weight, team_tokens, small = opening(
        qkv_send, gate_up_send, w_output, tokens, small_send, planes, 1
    )
    qkv_weight = qkv_weight.reshape(width, -1)
    output_weight = output_weight.reshape(head_width, width)
    gate_up_weights = []
    down_weights = []
    for k in range(CHUNKS):
        gate_up_weights.append(gather_line(gate_up_slices[k].reshape(TEAM * rows, -1)))
        down_rows, _ = lax.optimization_barrier(
            (w_down[k * ff_part : (k + 1) * ff_part], gate_up_slices)
        )
        down_weights.append(gather_line(down_rows))

    norm_gain = small[:, 0, : attn_gain.shape[0]].reshape(width).astype(f32)
    mlp_norm_gain = small[:, 1, : mlp_gain.shape[0]].reshape(width).astype(f32)
    qgain = small[:, 2, : query_norm_gain.shape[0]].reshape(HEAD_SIZE).astype(f32)
    kgain = small[:, 3, : key_gain.shape[0]].reshape(HEAD_SIZE).astype(f32)
    team_small = lax.dynamic_slice_in_dim(small, plane * TEAM, TEAM, axis=0)
    team_segments = (
        team_small[:, 4 : 4 + slots, :sequence].reshape(team_slots, sequence).astype(jnp.int32)
    )
    tables = rotation_tables(doc_positions(team_segments))
    visible = allowed(team_segments)

    inputs = tokens.astype(f32)
    cot_b = cotangent * row_live.astype(bf16)
    team_normalized = root_mean_square_norm(
        team_tokens.reshape(TEAM * token_count, width).astype(f32), norm_gain
    ).astype(bf16)

    projected = simple_product(team_normalized, qkv_weight)

    def head_prep(query_projected, key_projected, gain_query, gain_key):
        query_heads = query_projected.reshape(team_slots, sequence, groups, HEAD_SIZE)
        key_heads = key_projected.reshape(team_slots, sequence, 1, HEAD_SIZE)
        return (
            apply_rotation(root_mean_square_norm(query_heads, gain_query), tables),
            apply_rotation(root_mean_square_norm(key_heads, gain_key), tables),
        )

    query_projected = projected[:, :head_width]
    key_projected = projected[:, head_width : head_width + HEAD_SIZE]
    value_b = projected[:, head_width + HEAD_SIZE :].astype(bf16)
    value_b = value_b.reshape(team_slots, sequence, HEAD_SIZE)
    query_rot, key_rot = head_prep(query_projected, key_projected, qgain, kgain)
    query_b = query_rot.astype(bf16)
    key_b = key_rot.astype(bf16).reshape(team_slots, sequence, HEAD_SIZE)
    scores = jnp.einsum(
        "bigd,bjd->bgij", query_b, key_b, preferred_element_type=f32
    ) * HEAD_SIZE ** (-0.5)
    scores = jnp.where(visible[:, None], scores, -1e30)
    top = jnp.max(scores, axis=-1, keepdims=True)
    expos = jnp.exp(scores - top)
    probs = expos / jnp.sum(expos, axis=-1, keepdims=True)
    probs_b = probs.astype(bf16)
    context = jnp.einsum("bgij,bjd->bigd", probs_b, value_b, preferred_element_type=f32)
    context_b = context.astype(bf16).reshape(team_slots * sequence, head_width)
    middle = inputs + reduce(simple_product(context_b, output_weight).astype(bf16), 5)

    normed_two = root_mean_square_norm(middle, mlp_norm_gain).astype(bf16)
    team_two = gather(normed_two, 3)
    late_cot, _ = lax.optimization_barrier((cot_b, team_two))
    team_cot = gather(late_cot, 3)
    out_part = 0.0
    grad_two_part = 0.0
    grad_gate_up = []
    grad_down = []
    units = planes * ff_part
    for k in range(CHUNKS):
        both = simple_product(team_two, gate_up_weights[k])
        gate, up = both[:, :units], both[:, units:]
        sigma = jax.nn.sigmoid(gate)
        silu_gate = gate * sigma
        act_b = (silu_gate * up).astype(bf16)
        grad_act = dot_last(team_cot, down_weights[k])
        grad_both = jnp.concatenate(
            [
                (grad_act * up * (sigma * (1.0 + gate * (1.0 - sigma)))).astype(bf16),
                (grad_act * silu_gate).astype(bf16),
            ],
            axis=1,
        )
        grad_gate_up.append(sum_line(dot_first(team_two, grad_both).astype(bf16)))
        grad_down.append(sum_line(dot_first(act_b, team_cot).astype(bf16)))
        out_part = out_part + simple_product(act_b, down_weights[k])
        grad_two_part = grad_two_part + dot_last(grad_both, gate_up_weights[k])

    grad_normed_two = reduce(grad_two_part.astype(bf16), 5)
    _, pull_two = jax.vjp(root_mean_square_norm, middle, mlp_norm_gain)
    middle_part, grad_mgain = pull_two(grad_normed_two)
    grad_middle = cot_b.astype(f32) + middle_part
    team_grad = gather(grad_middle.astype(bf16), 3)

    grad_output_part = spread(
        dot_first(context_b, team_grad).astype(bf16), planes, True, 6
    )
    grad_output = sum_line(grad_output_part)
    grad_context = dot_last(team_grad, output_weight).astype(bf16)
    grad_context = grad_context.reshape(team_slots, sequence, groups, HEAD_SIZE)
    grad_value = jnp.einsum(
        "bgij,bigd->bjd", probs_b, grad_context, preferred_element_type=f32
    )
    grad_probs = jnp.einsum(
        "bigd,bjd->bgij", grad_context, value_b, preferred_element_type=f32
    )
    inner = jnp.sum(probs * grad_probs, axis=-1, keepdims=True)
    grad_scores = (probs * (grad_probs - inner)).astype(bf16)
    grad_query_rot = jnp.einsum(
        "bgij,bjd->bigd", grad_scores, key_b, preferred_element_type=f32
    ) * HEAD_SIZE ** (-0.5)
    grad_key_rot = jnp.einsum(
        "bgij,bigd->bjd", grad_scores, query_b, preferred_element_type=f32
    ) * HEAD_SIZE ** (-0.5)
    _, pull_heads = jax.vjp(head_prep, query_projected, key_projected, qgain, kgain)
    grad_query_raw, grad_key_raw, grad_qgain, grad_kgain = pull_heads(
        (grad_query_rot, grad_key_rot.reshape(team_slots, sequence, 1, HEAD_SIZE))
    )
    grad_qkv = jnp.concatenate(
        [
            grad_query_raw.astype(bf16),
            grad_key_raw.astype(bf16),
            grad_value.reshape(team_slots * sequence, HEAD_SIZE).astype(bf16),
        ],
        axis=1,
    )
    grad_qkv_weight = sum_line(dot_first(team_normalized, grad_qkv).astype(bf16))
    grad_normed = reduce(dot_last(grad_qkv, qkv_weight).astype(bf16), 5)
    _, pull_one = jax.vjp(root_mean_square_norm, inputs, norm_gain)
    input_part, grad_again = pull_one(grad_normed)
    grad_tokens = (grad_middle + input_part).astype(bf16)
    layer_out = (row_live * (middle + reduce(out_part.astype(bf16), 5))).astype(bf16)

    def by_owner(vector):
        vector = vector.reshape(devices, -1)
        return jnp.pad(vector, ((0, 0), (0, 128 - vector.shape[1])))

    gains = jnp.stack(
        [by_owner(v) for v in (grad_again, grad_mgain, grad_qgain, grad_kgain)], axis=1
    )
    gains = jnp.pad(gains, ((0, 0), (0, 4), (0, 0)))
    gains = gains.reshape(planes, TEAM, 8, 128).transpose(1, 0, 2, 3)
    gains = total(gains, planes, 7)

    grad_gate_parts, grad_up_parts = [], []
    before = grad_down[0]
    for k in range(CHUNKS):
        summed, _, _ = lax.optimization_barrier((grad_gate_up[k], grad_down[k], before))
        back = swap(summed.reshape(TEAM, rows, 2 * units), 2)
        before = back
        back = back.astype(f32)
        back = back.reshape(TEAM, rows, 2, planes, ff_part).transpose(2, 1, 3, 0, 4)
        grad_gate_parts.append(back[0])
        grad_up_parts.append(back[1])
    grad_gate = jnp.stack(grad_gate_parts, axis=3).reshape(rows, -1)
    grad_up = jnp.stack(grad_up_parts, axis=3).reshape(rows, -1)
    grad_down_w = jnp.concatenate(grad_down, axis=0).astype(f32)
    grad_qkv_weight, grad_output, _ = lax.optimization_barrier(
        (grad_qkv_weight, grad_output, before)
    )
    grad_output = grad_output.astype(f32)
    qkv_back = swap(grad_qkv_weight.reshape(TEAM, rows, -1), 0).astype(f32)
    qkv_back = qkv_back.transpose(1, 0, 2)
    grad_query = qkv_back[:, :, :head_width].reshape(rows, -1)
    grad_key = qkv_back[:, :, head_width : head_width + HEAD_SIZE].reshape(rows, -1)
    grad_value_w = qkv_back[:, :, head_width + HEAD_SIZE :].reshape(rows, -1)
    return (
        layer_out,
        grad_tokens,
        grad_query,
        grad_key,
        grad_value_w,
        grad_output,
        gains[0, : attn_gain.shape[0]],
        gains[2, : query_norm_gain.shape[0]],
        gains[3, : key_gain.shape[0]],
        grad_gate,
        grad_up,
        grad_down_w,
        gains[1, : mlp_gain.shape[0]],
    )


def solution(mesh):
    by_rows, by_entry = P("fsdp", None), P("fsdp")
    return jax.shard_map(
        functools.partial(local, mesh.shape["fsdp"]),
        mesh=mesh,
        in_specs=(
            by_rows,
            by_rows,
            by_entry,
            by_rows,
            by_rows,
            by_rows,
            by_rows,
            by_rows,
            by_entry,
            by_entry,
            by_entry,
            by_rows,
            by_rows,
            by_rows,
            by_entry,
        ),
        out_specs=(
            by_rows,
            by_rows,
            by_rows,
            by_rows,
            by_rows,
            by_rows,
            by_entry,
            by_entry,
            by_entry,
            by_rows,
            by_rows,
            by_rows,
            by_entry,
        ),
        check_vma=False,
    )
```

time: 2830 us -> 668 us (0.24)
  waiting for transfers between devices: 2450 us -> 30.7 us
  Pallas kernels: 0 us -> 360 us
  matrix products: 222 us -> 134 us
  blocking collectives: 82.4 us -> 0 us
  local copies, waits for them, and re-layouts: 28.3 us -> 64.3 us
  other arithmetic: 23 us -> 55.1 us
    reduce_scatter x7 -> x6, waiting for transfers between devices: 1800 us -> 0.03 us  [sum_line(): lax.psum_scatter(x, 'fsdp', scatter_dimension=0, tiled=True, axis_index_g...]
    all_gather x7 -> x4, waiting for transfers between devices: 646 us -> 29.3 us  [gather_line(): lax.all_gather(x, 'fsdp', axis=0, tiled=True, axis_index_groups=lines)]
    pallas_call x0 -> x13, Pallas kernels: none -> 360 us  [the longest x4 127 us: reduce(): pl.pallas_call(reduce_kernel, out_shape=jax.ShapeDtypeStruct((rows, width...]
    unnamed x2 -> x0, blocking collectives: 82.4 us -> none
    dot_general x7 -> x6, matrix products: 91.5 us -> 40.5 us  [dot_first(): lax.dot_general(left, right, (((0,), (0,)), ((), ())), preferred_element_...]
    dot_general x7 -> x6, matrix products: 68.6 us -> 48.4 us  [dot_last(): lax.dot_general(left, right, (((1,), (1,)), ((), ())), preferred_element_...]
  transfers between devices with their start and end apart: 14 -> 10, of which waited for: 13 -> 2; matrix products, arithmetic and copies ran while one was open for 7% -> 30% of each run, Pallas kernels for 0% -> 41%
where the time goes in v1:
time: 668 us; the launch traced here: 661 us
  Pallas kernels  360 us (54%)
  matrix products  134 us (20%)
  local copies, waits for them, and re-layouts  64.3 us (10%)
  other arithmetic  55.1 us (8%)
  waiting for transfers between devices  30.7 us (5%)
  between operations  16.7 us (2%)
    pallas_call x4, Pallas kernels, reduce(): pl.pallas_call(reduce_kernel, out_shape=jax.ShapeDtypeStruct((rows, width...  127 us
    pallas_call x3, Pallas kernels, gather(): pl.pallas_call(gather_kernel, out_shape=jax.ShapeDtypeStruct((TEAM, rows,...  93.1 us
    pallas_call x1, Pallas kernels, opening(): pl.pallas_call(functools.partial(open_kernel, planes), out_shape=(like((p...  80.3 us
    dot_general x6, matrix products, dot_last(): lax.dot_general(left, right, (((1,), (1,)), ((), ())), preferred_element_...  48.4 us
    dot_general x6, matrix products, dot_first(): lax.dot_general(left, right, (((0,), (0,)), ((), ())), preferred_element_...  40.5 us
    dot_general x6, matrix products, simple_product(): return jnp.dot(left, right, preferred_element_type=jnp.float32)  36.3 us
    pallas_call x3, Pallas kernels, swap(): pl.pallas_call(swap_kernel, out_shape=jax.ShapeDtypeStruct(x.shape, x.dty...  35.2 us
    all_gather x4, waiting for transfers between devices, gather_line(): lax.all_gather(x, 'fsdp', axis=0, tiled=True, axis_index_groups=lines)  29.3 us
  transfers between devices with their start and end apart: 10, of which 2 were waited for; matrix products, arithmetic and copies ran while one was open for 30% of the time, Pallas kernels for 41%

profile of v1, /device:TPU:0, one launch (start us, length us, event | category | flops | bytes accessed | tf_op | source)
XLA Modules:
  0.0 660.9 jit_solution(1394261219413918234)
XLA Ops:
  24.9 80.3 %shard_map.246 = (bf16[4,8,64,512]{3,2,1,0:T(8,128)(2,1)}, bf16[2,8,64,768]{3,2,1,0:T(8,128)(2,1)}, bf16[4,64,2048]{2,1,0:T(8,128)(2,1)}, bf16[4,64,2048]{2,1,0:...) custom-call(bf16[8,64,512]{2,1,0:T(8,128)(2,1)} %pad_maximum_fusion.13.qkv_in, ...), custom_call_target="tpu_custom_call" | custom-call | tf_op jit(solution)/shard_map/pallas_call | solution.py:574
  150.7 33.1 %shard_map.247 = f32[192,2048]{1,0:T(8,128)S(1)} custom-call(bf16[8,192,2048]{2,1,0:T(8,128)(2,1)S(1)} %bitcast.208), custom_call_target="tpu_custom_call" | custom-call | tf_op jit(solution)/shard_map/pallas_call | solution.py:302
  185.5 30.8 %shard_map.248 = bf16[8,192,2048]{2,1,0:T(8,128)(2,1)} custom-call(bf16[192,2048]{1,0:T(8,128)(2,1)} %multiply_convert_fusion.8.x_ref), custom_call_target="tpu_custom_call" | custom-call | tf_op jit(solution)/shard_map/pallas_call | solution.py:199
  217.4 31.1 %shard_map.250 = bf16[8,192,2048]{2,1,0:T(8,128)(2,1)} custom-call(bf16[192,2048]{1,0:T(8,128)(2,1)} %broadcast_multiply_fusion.x_ref), custom_call_target="tpu_custom_call" | custom-call | tf_op jit(solution)/shard_map/pallas_call | solution.py:199
  248.6 10.2 %fusion.72 = f32[1536,768]{0,1:T(8,128)} fusion(bf16[1536,2048]{1,0:T(8,128)(2,1)} %bitcast.222, bf16[2048,768]{1,0:T(8,128)(2,1)} %all-gather.5.cloned.1.call-done), kind=kOutput, calls=%fused_computation.195 | convolution fusion | flops 4831838208 | bytes 14155776 | tf_op jit(solution)/shard_map/dot_general | solution.py:71
  258.7 9.2 %multiply_convert_fusion.4 = (bf16[1536,384]{0,1:T(8,128)(2,1)S(1)}, bf16[1536,384]{0,1:T(8,128)(2,1)}, bf16[1536,384]{0,1:T(8,128)(2,1)S(1)}) fusion(f32[1536,768]{0,1:T(8,128)} %fusion.72, bf16[1536,2048]{1,0:T(8,128)(2,1)} %bitcast.226, bf16[384,2048]{1,0:T(8,128)(2,1)} %all-gather.7.cloned.1.call-done), kind=kOutput, calls=%fused_computation.30 | convolution fusion | flops 2424766464 | bytes 16121856 | tf_op jit(solution)/shard_map/dot_general | solution.py:59
  274.6 9.8 %fusion.74 = f32[1536,768]{0,1:T(8,128)} fusion(bf16[1536,2048]{1,0:T(8,128)(2,1)} %bitcast.223, bf16[2048,768]{1,0:T(8,128)(2,1)} %all-gather.9.cloned.1.call-done), kind=kOutput, calls=%fused_computation.197 | convolution fusion | flops 4831838208 | bytes 14155776 | tf_op jit(solution)/shard_map/dot_general | solution.py:71
  284.4 27.4 %all-gather.11.cloned.1.call-done = bf16[384,2048]{1,0:T(8,128)(2,1)} async-done(((bf16[96,2048]{1,0:T(8,128)(2,1)}), bf16[384,2048]{1,0:T(8,128)(2,1)}) %all-gather.11.cloned.1.call-update) | async-done | bytes 1572880 | tf_op jit(solution)/shard_map/all_gather | solution.py:697
  311.8 9.4 %multiply_convert_fusion.2 = (bf16[1536,384]{0,1:T(8,128)(2,1)}, bf16[1536,384]{0,1:T(8,128)(2,1)}, bf16[1536,384]{0,1:T(8,128)(2,1)S(1)}) fusion(f32[1536,768]{0,1:T(8,128)} %fusion.74, bf16[1536,2048]{1,0:T(8,128)(2,1)} %bitcast.227, bf16[384,2048]{1,0:T(8,128)(2,1)} %all-gather.11.cloned.1.call-done), kind=kOutput, calls=%fused_computation.28 | convolution fusion | flops 2424766464 | bytes 16121856 | tf_op jit(solution)/shard_map/dot_general | solution.py:59
  329.0 8.8 %convolution_convert_fusion.2 = bf16[2048,768]{1,0:T(8,128)(2,1)} fusion(bf16[1536,2048]{1,0:T(8,128)(2,1)} %bitcast.224, bf16[1536,384]{0,1:T(8,128)(2,1)} %get-tuple-element.54, bf16[1536,384]{0,1:T(8,128)(2,1)S(1)} %get-tuple-element.53), kind=kOutput, calls=%fused_computation.10 | convolution fusion | flops 4838129664 | bytes 11796480 | tf_op jit(solution)/shard_map/dot_general | solution.py:65
  338.0 7.0 %fusion.2 = bf16[1536,2048]{1,0:T(8,128)(2,1)} fusion(f32[2048]{0:T(1024)S(1)} %reshape.473, f32[1536]{0:T(1024)S(1)} %rsqrt.61, bf16[8,192,2048]{2,1,0:T(8,128)(2,1)} %get-tuple-element.25), kind=kLoop, calls=%fused_computation.3 | loop fusion | flops 12582912 | bytes 12597248 | tf_op jit(solution)/shard_map/convert_element_type | solution.py:764
  345.0 10.6 %convolution_convert_fusion.3 = bf16[2048,768]{1,0:T(8,128)(2,1)} fusion(bf16[1536,2048]{1,0:T(8,128)(2,1)} %bitcast.225, bf16[1536,384]{0,1:T(8,128)(2,1)S(1)} %copy-done.74, bf16[1536,384]{0,1:T(8,128)(2,1)S(1)} %copy-done.72), kind=kOutput, calls=%fused_computation.11 | convolution fusion | flops 4838129664 | bytes 11796480 | tf_op jit(solution)/shard_map/dot_general | solution.py:65
  355.8 10.0 %fusion.17 = f32[1536,2048]{1,0:T(8,128)} fusion(bf16[2048,768]{1,0:T(8,128)(2,1)} %all-gather.5.cloned.1.call-done, bf16[1536,384]{0,1:T(8,128)(2,1)} %get-tuple-element.54, bf16[1536,384]{0,1:T(8,128)(2,1)S(1)} %get-tuple-element.53), kind=kOutput, calls=%fused_computation.71 | convolution fusion | flops 4836556800 | bytes 18087936 | tf_op jit(solution)/shard_map/dot_general | solution.py:59
  365.7 8.2 %add_convert_fusion = bf16[1536,2048]{1,0:T(8,128)(2,1)S(1)} fusion(f32[1536,2048]{1,0:T(8,128)} %fusion.17, bf16[2048,768]{1,0:T(8,128)(2,1)S(1)} %copy-done.70, bf16[1536,384]{0,1:T(8,128)(2,1)S(1)} %copy-done.75, bf16[1536,384]{0,1:T(8,128)(2,1)S(1)} %copy-done.73), kind=kOutput, calls=%fused_computation.4 | convolution fusion | flops 4842848256 | bytes 24379392 | tf_op jit(solution)/shard_map/dot_general | solution.py:59
  374.0 31.9 %shard_map.251 = f32[192,2048]{1,0:T(8,128)S(1)} custom-call(bf16[8,192,2048]{2,1,0:T(8,128)(2,1)S(1)} %bitcast.210), custom_call_target="tpu_custom_call" | custom-call | tf_op jit(solution)/shard_map/pallas_call | solution.py:302
  408.4 31.2 %shard_map.252 = bf16[8,192,2048]{2,1,0:T(8,128)(2,1)} custom-call(bf16[192,2048]{1,0:T(8,128)(2,1)} %fusion.67.x_ref), custom_call_target="tpu_custom_call" | custom-call | tf_op jit(solution)/shard_map/pallas_call | solution.py:199
  451.1 13.7 %shard_map.254 = bf16[4,64,2048]{2,1,0:T(8,128)(2,1)} custom-call(bf16[4,64,2048]{2,1,0:T(8,128)(2,1)} %bitcast.234), custom_call_target="tpu_custom_call" | custom-call | tf_op jit(solution)/shard_map/pallas_call | solution.py:356
  488.9 7.0 %convolution_convert_fusion.1 = bf16[1536,2048]{1,0:T(8,128)(2,1)} fusion(bf16[2048,512]{1,0:T(8,128)(2,1)} %bitcast.255, bf16[1536,128]{1,0:T(8,128)(2,1)S(1)} %bitcast.262, bf16[1536,128]{1,0:T(8,128)(2,1)S(1)} %bitcast.249, bf16[1536,256]{1,0:T(8,128)(2,1)S(1)} %bitcast.244), kind=kOutput, calls=%fused_computation.9 | convolution fusion | flops 3229089792 | bytes 9961472 | tf_op jit(solution)/shard_map/dot_general | solution.py:59
  499.0 32.4 %shard_map.253 = f32[192,2048]{1,0:T(8,128)S(1)} custom-call(bf16[8,192,2048]{2,1,0:T(8,128)(2,1)S(1)} %bitcast.209), custom_call_target="tpu_custom_call" | custom-call | tf_op jit(solution)/shard_map/pallas_call | solution.py:302
  532.9 10.8 %shard_map.258 = f32[8,128]{1,0:T(8,128)} custom-call(f32[8,4,8,128]{3,2,1,0:T(8,128)} %bitcast.247), custom_call_target="tpu_custom_call" | custom-call | tf_op jit(solution)/shard_map/pallas_call | solution.py:643
  554.8 29.2 %shard_map.249 = f32[192,2048]{1,0:T(8,128)S(1)} custom-call(bf16[8,192,2048]{2,1,0:T(8,128)(2,1)S(1)} %bitcast.207), custom_call_target="tpu_custom_call" | custom-call | tf_op jit(solution)/shard_map/pallas_call | solution.py:302
  589.9 13.4 %shard_map.255 = bf16[8,64,768]{2,1,0:T(8,128)(2,1)} custom-call(bf16[8,64,768]{2,1,0:T(8,128)(2,1)} %bitcast.241), custom_call_target="tpu_custom_call" | custom-call | tf_op jit(solution)/shard_map/pallas_call | solution.py:134
  606.1 11.8 %shard_map.256 = bf16[8,64,768]{2,1,0:T(8,128)(2,1)} custom-call(bf16[8,64,768]{2,1,0:T(8,128)(2,1)} %bitcast.242), custom_call_target="tpu_custom_call" | custom-call | tf_op jit(solution)/shard_map/pallas_call | solution.py:134
  622.0 10.0 %shard_map.257 = bf16[8,64,512]{2,1,0:T(8,128)(2,1)} custom-call(bf16[8,64,512]{2,1,0:T(8,128)(2,1)} %bitcast.245), custom_call_target="tpu_custom_call" | custom-call | tf_op jit(solution)/shard_map/pallas_call | solution.py:134
  (314 shorter events, 167.0 us)
Async XLA Ops:
  7.2 241.4 %all-gather.5.cloned.1.call-start = ((), (), s32[]{:S(2)}) async-start(), calls=%async_computation.6 | async-start | bytes 3932160 | tf_op jit(solution)/shard_map/all_gather | solution.py:697
  108.0 150.7 %all-gather.7.cloned.1.call-start = ((), (), s32[]{:S(2)}) async-start(), calls=%async_computation.7 | async-start | bytes 1966080 | tf_op jit(solution)/shard_map/all_gather | solution.py:697
  109.0 165.6 %all-gather.9.cloned.1.call-start = ((), (), s32[]{:S(2)}) async-start(), calls=%async_computation.8 | async-start | bytes 3932160 | tf_op jit(solution)/shard_map/all_gather | solution.py:697
  109.7 202.1 %all-gather.11.cloned.1.call-start = ((), (), s32[]{:S(2)}) async-start(), calls=%async_computation.9 | async-start | bytes 1966080 | tf_op jit(solution)/shard_map/all_gather | solution.py:697
  110.3 477.1 %reduce-scatter.17.cloned.1.call-start = ((), (), s32[]{:S(2)}) async-start(), calls=%async_computation.15 | async-start | bytes 1966080 | tf_op jit(solution)/shard_map/reduce_scatter | solution.py:700
  126.7 279.6 %copy-start.64 = (bf16[192]{0:T(256)(128)(2,1)}, bf16[192]{0:T(256)(128)(2,1)S(1)}, u32[]{:S(2)}) copy-start(bf16[192]{0:T(256)(128)(2,1)S(1)} %convert_element_type.260) | copy-start | bytes 1156
  145.9 321.2 %copy-start.51 = (f32[24,2,64]{2,1,0:T(2,128)}, f32[24,2,64]{2,1,0:T(2,128)S(1)}, u32[]{:S(2)}) copy-start(f32[24,2,64]{2,1,0:T(2,128)S(1)} %get-tuple-element.86) | copy-start | bytes 36868
  150.7 33.1 %copy-start.9 = (bf16[192,2048]{1,0:T(8,128)(2,1)S(1)}, bf16[192,2048]{1,0:T(8,128)(2,1)}, u32[]{:S(2)}) copy-start(bf16[192,2048]{1,0:T(8,128)(2,1)} %tokens_in.1) | copy-start | bytes 2359300
  184.2 153.7 %copy-start.57 = (f32[192]{0:T(256)}, f32[192]{0:T(256)S(1)}, u32[]{:S(2)}) copy-start(f32[192]{0:T(256)S(1)} %get-tuple-element.77) | copy-start | bytes 2308
  184.2 222.1 %copy-start.3 = (f32[192,2048]{1,0:T(8,128)}, f32[192,2048]{1,0:T(8,128)S(1)}, u32[]{:S(2)}) copy-start(f32[192,2048]{1,0:T(8,128)S(1)} %get-tuple-element.50) | copy-start | bytes 4718596
  184.3 222.1 %copy-start.49 = (f32[192]{0:T(256)}, f32[192]{0:T(256)S(1)}, u32[]{:S(2)}) copy-start(f32[192]{0:T(256)S(1)} %fusion.52) | copy-start | bytes 2308
  185.5 30.8 %copy-start.15 = (bf16[192,2048]{1,0:T(8,128)(2,1)S(1)}, bf16[192,2048]{1,0:T(8,128)(2,1)}, u32[]{:S(2)}) copy-start(bf16[192,2048]{1,0:T(8,128)(2,1)} %param.18) | copy-start | bytes 2359300
  272.7 314.7 %reduce-scatter.13.cloned.1.call-start = ((), (), s32[]{:S(2)}) async-start(), calls=%async_computation.13 | async-start | bytes 1966080 | tf_op jit(solution)/shard_map/reduce_scatter | solution.py:700
  329.0 260.9 %reduce-scatter.15.cloned.1.call-start = ((), (), s32[]{:S(2)}) async-start(), calls=%async_computation.14 | async-start | bytes 3932160 | tf_op jit(solution)/shard_map/reduce_scatter | solution.py:700
  337.8 268.3 %reduce-scatter.11.cloned.1.call-start = ((), (), s32[]{:S(2)}) async-start(), calls=%async_computation.12 | async-start | bytes 3932160 | tf_op jit(solution)/shard_map/reduce_scatter | solution.py:700
  338.0 193.4 %copy-start.55 = (f32[192]{0:T(256)}, f32[192]{0:T(256)S(1)}, u32[]{:S(2)}) copy-start(f32[192]{0:T(256)S(1)} %fusion.53) | copy-start | bytes 2308
  355.7 266.3 %reduce-scatter.9.cloned.1.call-start = ((), (), s32[]{:S(2)}) async-start(), calls=%async_computation.11 | async-start | bytes 1310720 | tf_op jit(solution)/shard_map/reduce_scatter | solution.py:700
  408.4 31.2 %copy-start.37 = (bf16[4,64,2048]{2,1,0:T(8,128)(2,1)S(1)}, bf16[4,64,2048]{2,1,0:T(8,128)(2,1)}, u32[]{:S(2)}) copy-start(bf16[4,64,2048]{2,1,0:T(8,128)(2,1)} %get-tuple-element.28) | copy-start | bytes 3145732
  476.6 145.3 %reduce-scatter.7.cloned.1.call-start = ((), (), s32[]{:S(2)}) async-start(), calls=%async_computation.10 | async-start | bytes 2621440 | tf_op jit(solution)/shard_map/reduce_scatter | solution.py:700
  499.0 32.4 %copy-start.10 = (bf16[192,2048]{1,0:T(8,128)(2,1)S(1)}, bf16[192,2048]{1,0:T(8,128)(2,1)}, u32[]{:S(2)}) copy-start(bf16[192,2048]{1,0:T(8,128)(2,1)} %tokens_in.1) | copy-start | bytes 2359300
  554.7 30.3 %copy-start.4 = (f32[192,2048]{1,0:T(8,128)S(1)}, f32[192,2048]{1,0:T(8,128)}, u32[]{:S(2)}) copy-start(f32[192,2048]{1,0:T(8,128)} %copy-done.3) | copy-start | bytes 4718596
  554.8 30.3 %copy-start.11 = (bf16[192,2048]{1,0:T(8,128)(2,1)S(1)}, bf16[192,2048]{1,0:T(8,128)(2,1)}, u32[]{:S(2)}) copy-start(bf16[192,2048]{1,0:T(8,128)(2,1)} %tokens_in.1) | copy-start | bytes 2359300
  554.8 30.3 %copy-start.17 = (bf16[192,2048]{1,0:T(8,128)(2,1)S(1)}, bf16[192,2048]{1,0:T(8,128)(2,1)}, u32[]{:S(2)}) copy-start(bf16[192,2048]{1,0:T(8,128)(2,1)} %param.18) | copy-start | bytes 2359300
  554.8 30.3 %copy-start.50 = (f32[192]{0:T(256)S(1)}, f32[192]{0:T(256)}, u32[]{:S(2)}) copy-start(f32[192]{0:T(256)} %copy-done.49) | copy-start | bytes 2308
  (64 other events, 441.6 us)
Sparse Core Ops, SparseCore 0:
  108.1 64.5 all-gather.4
  174.3 35.7 all-gather.6
  212.2 62.3 all-gather.8
  276.0 35.7 all-gather.10
  314.0 34.1 reduce-scatter.16
  350.3 34.2 reduce-scatter.12
  386.9 59.2 reduce-scatter.14
  448.5 60.2 reduce-scatter.10
  511.1 27.1 reduce-scatter.8
  540.5 42.4 reduce-scatter.6

commit v2 on v0

v2 whole, which is shorter than its diff:
```python
import functools

import jax
import jax.numpy as jnp
import numpy as np
from jax import lax
from jax.experimental import pallas as pl
from jax.experimental.pallas import tpu as pltpu
from jax.sharding import PartitionSpec as P

QUERY_HEADS = 16
KEY_VALUE_HEADS = 8
HEAD_SIZE = 128
TEAM = 8
STEP = 256

epsilon = 1e-06
base_theta = 1000000.0
MESH = pl.DeviceIdType.MESH
LIMIT = 60 * 2**20
f32 = jnp.float32
bf16 = jnp.bfloat16


def root_mean_square_norm(values, gain):
    return values * lax.rsqrt(jnp.mean(values * values, axis=-1, keepdims=True) + epsilon) * gain


def rotation_tables(positions):
    half = HEAD_SIZE // 2
    powers = -np.arange(half, dtype=np.float32) * np.float32(2.0) / np.float32(HEAD_SIZE)
    freqs = np.power(np.float32(base_theta), powers).astype(np.float32)
    angles = np.arange(positions, dtype=np.float32)[:, None] * freqs
    cosine, sine = np.cos(angles), np.sin(angles)
    rest = np.concatenate([cosine, cosine, -sine, sine], axis=1).astype(np.float32)
    parts = []
    for _ in range(3):
        parts.append(rest.astype(jnp.bfloat16))
        rest = rest - parts[-1].astype(np.float32)
    return np.concatenate(parts, axis=1)


def dot_last(left, right):
    return lax.dot_general(
        left, right, (((1,), (1,)), ((), ())), preferred_element_type=jnp.float32
    )


def dot_first(left, right):
    return lax.dot_general(
        left, right, (((0,), (0,)), ((), ())), preferred_element_type=jnp.float32
    )


def simple_product(left, right):
    return jnp.dot(left, right, preferred_element_type=jnp.float32)


def flipped(index, mask):
    for bit in (1, 2, 4):
        if mask & bit:
            index = index + bit * (1 - 2 * lax.rem(lax.div(index, bit), 2))
    return index


def greet(me, masks, others=(), owners=()):
    barrier = pltpu.get_barrier_semaphore()

    def signal(device):
        pl.semaphore_signal(barrier, inc=1, device_id=(device,), device_id_type=MESH)

    for mask in masks:
        signal(flipped(me, mask))
    for other in others:
        signal(other)
    peers = len(masks) + len(others)
    for owner in owners:
        pl.when(owner != me)(functools.partial(signal, owner))
        peers = peers + (owner != me).astype(jnp.int32)
    pl.semaphore_wait(barrier, peers)


def head_owner(me, planes):
    to = TEAM * lax.rem(me, planes) + lax.div(me, planes)
    back = planes * lax.rem(me, TEAM) + lax.div(me, TEAM)
    return to, back


def remote(source, target, send, receive, device):
    return pltpu.make_async_remote_copy(
        src_ref=source,
        dst_ref=target,
        send_sem=send,
        recv_sem=receive,
        device_id=(device,),
        device_id_type=MESH,
    )


def params(collective, limit=None):
    if limit is None:
        return pltpu.CompilerParams(collective_id=collective, has_side_effects=True)
    return pltpu.CompilerParams(
        collective_id=collective, has_side_effects=True, vmem_limit_bytes=limit
    )


class Gather:
    def __init__(self, begin, x, o, me):
        self.begin, self.x, self.o, self.me = begin, x, o, me
        self.place = lax.rem(me, TEAM)
        self.half = x.shape[0] // 2

    def part(self, ref, which):
        return ref.at[pl.ds(which * self.half, self.half)]

    def first(self, which, mask):
        target = self.part(self.o.at[self.place], which)
        return self.begin(self.part(self.x, which), target, flipped(self.me, mask))

    def relay(self, origin, which, mask):
        ref = self.part(self.o.at[flipped(self.place, origin)], which)
        return self.begin(ref, ref, flipped(self.me, mask))

    def start(self):
        self.x0, self.y1 = self.first(0, 2), self.first(1, 4)
        self.x1, self.y0 = self.first(1, 2), self.first(0, 4)
        self.late = [self.first(0, 1), self.first(1, 1)]

    def forward(self):
        self.x0.wait_recv()
        self.d0 = self.relay(2, 0, 4)
        self.y1.wait_recv()
        self.d1 = self.relay(4, 1, 2)
        self.late += [self.relay(2, 0, 1), self.relay(4, 1, 1)]

    def across(self):
        self.x1.wait_recv()
        self.late.append(self.relay(2, 1, 1))
        self.y0.wait_recv()
        self.late.append(self.relay(4, 0, 1))

    def diagonal(self):
        self.d0.wait_recv()
        self.late.append(self.relay(6, 0, 1))
        self.d1.wait_recv()
        self.late.append(self.relay(6, 1, 1))

    def arrive(self):
        for copy in self.late:
            copy.wait_recv()


class Sender:
    def __init__(self, send, receive):
        self.send, self.receive, self.count, self.started = send, receive, 0, []

    def take(self):
        self.count += 1
        return self.count - 1

    def __call__(self, source, target, device):
        k = self.take()
        copy = remote(source, target, self.send.at[k], self.receive.at[k], device)
        copy.start()
        self.started.append(copy)
        return copy

    def finish(self):
        for copy in self.started:
            copy.wait_send()


def gather_kernel(x_ref, o_ref, send, receive, own):
    me = lax.axis_index("fsdp")
    keep = pltpu.make_async_copy(x_ref, o_ref.at[lax.rem(me, TEAM)], own)
    keep.start()
    greet(me, (1, 2, 4))
    sender = Sender(send, receive)
    moves = Gather(sender, x_ref, o_ref, me)
    moves.start()
    moves.forward()
    moves.across()
    moves.diagonal()
    moves.arrive()
    sender.finish()
    keep.wait()


def gather(x, collective):
    rows, width = x.shape
    whole = pl.pallas_call(
        gather_kernel,
        out_shape=jax.ShapeDtypeStruct((TEAM, rows, width), x.dtype),
        in_specs=[pl.BlockSpec(memory_space=pltpu.VMEM)],
        out_specs=pl.BlockSpec(memory_space=pl.ANY),
        scratch_shapes=[
            pltpu.SemaphoreType.DMA((14,)),
            pltpu.SemaphoreType.DMA((14,)),
            pltpu.SemaphoreType.DMA,
        ],
        compiler_params=params(collective),
    )(x)
    return whole.reshape(TEAM * rows, width)


TILE = 512


def reduce_kernel(turned, cut, pairs, *refs):
    lefts, rights = refs[:pairs], refs[pairs : 2 * pairs]
    out, mix, from_core, from_x, from_y, *rest = refs[2 * pairs :]
    left_here, right_here = rest[:pairs], rest[pairs : 2 * pairs]
    send, receive, own = rest[2 * pairs :]
    me = lax.axis_index("fsdp")
    place = lax.rem(me, TEAM)
    core = lax.rem(place, 2)
    rows, width = out.shape
    half = rows // 2
    step = 16
    chips = [lax.div(flipped(place, mask), 2) for mask in (6, 2, 4, 0)]

    loads = []

    def load(source, target):
        copy = pltpu.make_async_copy(source, target, own.at[len(loads)])
        copy.start()
        loads.append(copy)

    for k, (right, here) in enumerate(zip(rights, right_here)):
        if cut:
            load(right.at[pl.ds(k * here.shape[0], here.shape[0])], here)
        else:
            load(right, here)
    for left, here in zip(lefts, left_here):
        load(left, here)

    def product(j):
        @pl.loop(0, width // TILE)
        def _(t):
            at = pl.ds(pl.multiple_of(t * TILE, TILE), TILE)
            value = 0.0
            for left, right in zip(left_here, right_here):
                both = left[pl.ds(2 * chips[j], 2)].reshape(2 * rows, left.shape[2])
                if turned:
                    value = value + dot_last(both, right[at, :])
                else:
                    value = value + simple_product(both, right[:, at])
            mix[j, :, :, at] = value.astype(bf16).reshape(2, rows, TILE)

    across = []

    def cross(j):
        copy = remote(
            mix.at[j, 1 - core], from_core.at[j], send.at[j], receive.at[j], flipped(me, 1)
        )
        copy.start()
        across.append(copy)

    def combine(j):
        across[j].wait_recv()

        @pl.loop(0, rows // step)
        def _(i):
            at = pl.ds(i * step, step)
            mix[j, core, at, :] = (
                mix[j, core, at, :].astype(f32) + from_core[j, at, :].astype(f32)
            ).astype(bf16)

    def begin(j, which, ref, slot, mask, k):
        copy = remote(
            mix.at[j, core, pl.ds(which * half, half)],
            ref.at[slot],
            send.at[k],
            receive.at[k],
            flipped(me, mask),
        )
        copy.start()
        return copy

    def add_relayed(j, which, ref):
        @pl.loop(0, half // step)
        def _(i):
            at = pl.ds(which * half + i * step, step)
            mix[j, core, at, :] = (
                mix[j, core, at, :].astype(f32) + ref[0, pl.ds(i * step, step), :].astype(f32)
            ).astype(bf16)

    greet(me, (1, 2, 4))
    for copy in loads:
        copy.wait()
    product(0)
    cross(0)
    product(1)
    combine(0)
    d_x = begin(0, 0, from_x, 0, 2, 4)
    d_y = begin(0, 1, from_y, 0, 4, 5)
    cross(1)
    product(2)
    cross(2)
    combine(1)
    x_0 = begin(1, 0, from_x, 1, 2, 6)
    combine(2)
    y_1 = begin(2, 1, from_y, 1, 4, 7)
    d_x.wait_recv()
    add_relayed(2, 0, from_x)
    y_0 = begin(2, 0, from_y, 2, 4, 8)
    d_y.wait_recv()
    add_relayed(1, 1, from_y)
    x_1 = begin(1, 1, from_x, 2, 2, 9)
    product(3)
    cross(3)
    across[3].wait_recv()

    def finish(which, slot_x, slot_y):
        @pl.loop(0, half // step)
        def _(i):
            at = pl.ds(which * half + i * step, step)
            here = pl.ds(i * step, step)
            out[at, :] = (mix[3, core, at, :].astype(f32) + from_core[3, at, :].astype(f32)) + (
                from_x[slot_x, here, :].astype(f32) + from_y[slot_y, here, :].astype(f32)
            )

    x_0.wait_recv()
    y_0.wait_recv()
    finish(0, 1, 2)
    y_1.wait_recv()
    x_1.wait_recv()
    finish(1, 2, 1)
    for copy in (*across, d_x, d_y, x_0, x_1, y_0, y_1):
        copy.wait_send()


def reduce(lefts, rights, turned, collective, cut=False):
    _, rows, _ = lefts[0].shape
    pairs = len(lefts)
    width = rights[0].shape[0] if turned else rights[0].shape[-1]
    depth = sum(left.shape[2] for left in lefts)
    anywhere = pl.BlockSpec(memory_space=pl.ANY)
    here = [(width, x.shape[2]) if turned else (x.shape[2], width) for x in lefts]
    loads = 2 * pairs
    return pl.pallas_call(
        functools.partial(reduce_kernel, turned, cut, pairs),
        out_shape=jax.ShapeDtypeStruct((rows, width), f32),
        in_specs=[anywhere] * (2 * pairs),
        out_specs=pl.BlockSpec(memory_space=pltpu.VMEM),
        scratch_shapes=[
            pltpu.VMEM((4, 2, rows, width), bf16),
            pltpu.VMEM((4, rows, width), bf16),
            pltpu.VMEM((3, rows // 2, width), bf16),
            pltpu.VMEM((3, rows // 2, width), bf16),
            *(pltpu.VMEM(x.shape, x.dtype) for x in lefts),
            *(pltpu.VMEM(shape, bf16) for shape in here),
            pltpu.SemaphoreType.DMA((10,)),
            pltpu.SemaphoreType.DMA((10,)),
            pltpu.SemaphoreType.DMA((loads,)),
        ],
        compiler_params=params(collective, LIMIT),
        cost_estimate=pl.CostEstimate(
            flops=2 * TEAM * rows * depth * width,
            bytes_accessed=2 * TEAM * rows * depth + 2 * depth * width + 4 * rows * width,
            transcendentals=0,
        ),
    )(*lefts, *rights)


class Line:
    def __init__(self, sender, ref, planes, me):
        self.sender, self.ref, self.planes = sender, ref, planes
        self.plane, self.place = lax.div(me, TEAM), lax.rem(me, TEAM)
        self.flows = [(sign, [sender.take() for _ in range(planes - 1)]) for sign in (1, -1)]

    def passing(self, step, sign, ks, source):
        block = jnp.clip(source, 0, self.planes - 1)
        beyond = jnp.clip(self.plane + sign, 0, self.planes - 1) * TEAM + self.place
        ref, k = self.ref.at[block], ks[step]
        return remote(ref, ref, self.sender.send.at[k], self.sender.receive.at[k], beyond)

    def goes(self, step, sign):
        source, onward = self.plane - sign * step, self.plane + sign
        last = self.planes - 1
        return (source >= 0) & (source <= last) & (onward >= 0) & (onward <= last)

    def start(self, step):
        for sign, ks in self.flows:
            going = self.passing(step, sign, ks, self.plane - sign * step)
            pl.when(self.goes(step, sign))(going.start)

    def arrive(self, step):
        for sign, ks in self.flows:
            source = self.plane - sign * (step + 1)
            coming = self.passing(step, sign, ks, source)
            pl.when((source >= 0) & (source <= self.planes - 1))(coming.wait_recv)

    def sent(self, step):
        for sign, ks in self.flows:
            going = self.passing(step, sign, ks, self.plane - sign * step)
            pl.when(self.goes(step, sign))(going.wait_send)


SWAP_ORDER = (6, 7, 2, 3, 4, 5, 1)


def open_kernel(planes, query_in, key_in, value_in, output_in, tokens_in, cot_in, *refs):
    smalls, refs = refs[:5], refs[5:]
    qkv, output, tokens, cot, *gain_refs, numbers = refs[:9]
    small_in, small, send, receive, own = refs[9:]
    slots, sequence = smalls[4].shape
    small_in[...] = jnp.zeros_like(small_in)
    for k, ref in enumerate(smalls):
        small_in[k : k + ref.shape[0], : ref.shape[1]] = ref[...].astype(f32)
    me = lax.axis_index("fsdp")
    place = lax.rem(me, TEAM)
    plane = lax.div(me, TEAM)
    team = me - place
    others = [lax.rem(me + TEAM * k, planes * TEAM) for k in range(1, planes)]
    sender = Sender(send, receive)
    keeps = []

    def keep(source, target):
        copy = pltpu.make_async_copy(source, target, own.at[len(keeps)])
        copy.start()
        keeps.append(copy)

    qkv_parts, at = [], 0
    for ref in (query_in, key_in, value_in):
        part = ref.shape[1] // TEAM
        qkv_parts.append((ref, part, qkv.at[plane, place, :, pl.ds(at, part)]))
        at += part

    def columns(ref, part, target):
        return ref.at[:, pl.ds(pl.multiple_of(target * part, part), part)]

    for ref, part, target in qkv_parts:
        keep(columns(ref, part, place), target)
    keep(small_in, small.at[me])
    keep(tokens_in, tokens.at[place])
    keep(cot_in, cot.at[place])
    to, back = head_owner(me, planes)
    greet(me, range(1, TEAM), others, (to, back))

    k = sender.take()
    over = remote(output_in, output.at[lax.rem(me, planes)], send.at[k], receive.at[k], to)
    home = remote(output_in, output.at[plane], send.at[k], receive.at[k], back)
    here = pltpu.make_async_copy(output_in, output.at[plane], own.at[len(keeps)])
    pl.when(to != me)(over.start)
    pl.when(to == me)(here.start)
    swaps = [
        sender(columns(ref, part, flipped(place, m)), target, flipped(me, m))
        for m in SWAP_ORDER
        for ref, part, target in qkv_parts
    ]
    near = [sender(small_in, small.at[me], flipped(me, m)) for m in SWAP_ORDER]
    qkv_line = Line(sender, qkv, planes, me)
    out_line = Line(sender, output, planes, me)
    rows_tokens = Gather(sender, tokens_in, tokens, me)
    rows_cot = Gather(sender, cot_in, cot, me)

    pl.when(to != me)(home.wait_recv)
    pl.when(to == me)(here.wait)
    out_line.start(0)
    for copy in swaps:
        copy.wait_recv()
    for copy in keeps[:3]:
        copy.wait()
    qkv_line.start(0)
    rows_tokens.start()
    rows_cot.start()
    rows_tokens.forward()
    out_line.arrive(0)
    if planes > 2:
        out_line.start(1)
    for copy in near:
        copy.wait_recv()
    keeps[3].wait()
    shared = small.at[pl.ds(team, TEAM)]
    far = [sender(shared, shared, other) for other in others]
    rows_tokens.across()
    for step in range(planes - 1):
        qkv_line.arrive(step)
        if step < planes - 2:
            qkv_line.start(step + 1)
            out_line.arrive(step + 1)
        if step < planes - 3:
            out_line.start(step + 2)
        if step == 0:
            rows_tokens.diagonal()
            rows_cot.forward()
        if step == 1:
            rows_cot.across()
            rows_cot.diagonal()
            for copy in far:
                copy.wait_recv()
            for k, ref in enumerate(gain_refs):
                part = smalls[k].shape[1]
                ref[...] = jnp.concatenate(
                    [small[i, k : k + 1, :part] for i in range(planes * TEAM)], axis=1
                )
            per_step = STEP // sequence
            for i in range(numbers.shape[0]):
                pieces = []
                for m in range(i * per_step, (i + 1) * per_step):
                    row = 4 + m % slots
                    pieces.append(small[team + m // slots, row : row + 1, :sequence] + 64.0 * m)
                numbers[i] = jnp.concatenate(pieces, axis=1)
    rows_tokens.arrive()
    rows_cot.arrive()
    pl.when(to != me)(over.wait_send)
    for step in range(planes - 1):
        qkv_line.sent(step)
        out_line.sent(step)
    sender.finish()
    for copy in keeps[4:]:
        copy.wait()


def opening(query, key, value, output, tokens, cot, smalls, planes, collective):
    links = 29 + 4 * (planes - 1) + 28 + planes - 1
    anywhere = pl.BlockSpec(memory_space=pl.ANY)
    vmem = pl.BlockSpec(memory_space=pltpu.VMEM)
    like = jax.ShapeDtypeStruct
    rows = query.shape[0]
    width = (query.shape[1] + key.shape[1] + value.shape[1]) // TEAM
    devices = planes * TEAM
    return pl.pallas_call(
        functools.partial(open_kernel, planes),
        out_shape=(
            like((planes, TEAM, rows, width), bf16),
            like((planes, *output.shape), bf16),
            like((TEAM, *tokens.shape), bf16),
            like((TEAM, *cot.shape), bf16),
            *(like((1, devices * x.shape[1]), f32) for x in smalls[:4]),
            like((TEAM * tokens.shape[0] // STEP, 1, STEP), f32),
        ),
        in_specs=[vmem] * 11,
        out_specs=(anywhere,) * 4 + (vmem,) * 5,
        scratch_shapes=[
            pltpu.VMEM((8, 128), f32),
            pltpu.VMEM((devices, 8, 128), f32),
            pltpu.SemaphoreType.DMA((links,)),
            pltpu.SemaphoreType.DMA((links,)),
            pltpu.SemaphoreType.DMA((7,)),
        ],
        compiler_params=params(collective, LIMIT),
    )(query, key, value, output, tokens, cot, *smalls)


def units_kernel(planes, parts, gate_in, up_in, *refs):
    gate_up, (sorted_units, send, receive, own) = refs[:parts], refs[parts:]
    me = lax.axis_index("fsdp")
    place = lax.rem(me, TEAM)
    greet(me, range(1, TEAM))
    sender = Sender(send, receive)
    block = gate_in.shape[1] // (planes * TEAM)
    some = planes // parts
    units = some * block
    moves = []
    for k in range(parts):
        for q in range(TEAM):
            for j, ref in enumerate((gate_in, up_in)):
                starts = [(TEAM * g + q) * block for g in range(k * some, (k + 1) * some)]
                sorted_units[k, q, :, j * units : (j + 1) * units] = jnp.concatenate(
                    [ref[:, at : at + block] for at in starts], axis=1
                )
        moves += [
            sender(sorted_units.at[k, flipped(place, m)], gate_up[k].at[place], flipped(me, m))
            for m in SWAP_ORDER
        ]
    keeps = [
        pltpu.make_async_copy(sorted_units.at[k, place], gate_up[k].at[place], own.at[k])
        for k in range(parts)
    ]
    for copy in keeps:
        copy.start()
    for copy in (*moves, *keeps):
        copy.wait()


def units_out(gate, up, planes, parts, collective):
    vmem = pl.BlockSpec(memory_space=pltpu.VMEM)
    anywhere = pl.BlockSpec(memory_space=pl.ANY)
    units = (TEAM, gate.shape[0], 2 * gate.shape[1] // TEAM // parts)
    links = (TEAM - 1) * parts
    return pl.pallas_call(
        functools.partial(units_kernel, planes, parts),
        out_shape=(jax.ShapeDtypeStruct(units, bf16),) * parts,
        in_specs=[vmem, vmem],
        out_specs=(anywhere,) * parts,
        scratch_shapes=[
            pltpu.VMEM((parts, *units), bf16),
            pltpu.SemaphoreType.DMA((links,)),
            pltpu.SemaphoreType.DMA((links,)),
            pltpu.SemaphoreType.DMA((parts,)),
        ],
        compiler_params=params(collective, LIMIT),
    )(gate, up)


def units_home_kernel(planes, parts, *refs):
    x_refs, (gate_ref, up_ref, landed, send, receive, own) = refs[:parts], refs[parts:]
    me = lax.axis_index("fsdp")
    place = lax.rem(me, TEAM)
    keeps = [
        pltpu.make_async_copy(x.at[place], landed.at[k, place], own.at[k])
        for k, x in enumerate(x_refs)
    ]
    for copy in keeps:
        copy.start()
    greet(me, range(1, TEAM))
    sender = Sender(send, receive)
    moves = [
        sender(x.at[flipped(place, m)], landed.at[k, place], flipped(me, m))
        for k, x in enumerate(x_refs)
        for m in SWAP_ORDER
    ]
    for copy in moves:
        copy.wait_recv()
    for copy in keeps:
        copy.wait()
    block = gate_ref.shape[1] // (planes * TEAM)
    some = planes // parts
    span = TEAM * block
    for j, ref in enumerate((gate_ref, up_ref)):
        for g in range(planes):
            at = (j * some + g % some) * block
            ref[:, g * span : (g + 1) * span] = jnp.concatenate(
                [landed[g // some, q, :, at : at + block].astype(f32) for q in range(TEAM)],
                axis=1,
            )
    sender.finish()


def units_home(xs, planes, collective):
    parts = len(xs)
    _, rows, width = xs[0].shape
    vmem = pl.BlockSpec(memory_space=pltpu.VMEM)
    like = jax.ShapeDtypeStruct
    links = (TEAM - 1) * parts
    return pl.pallas_call(
        functools.partial(units_home_kernel, planes, parts),
        out_shape=(like((rows, TEAM * parts * width // 2), f32),) * 2,
        in_specs=[pl.BlockSpec(memory_space=pl.ANY)] * parts,
        out_specs=(vmem, vmem),
        scratch_shapes=[
            pltpu.VMEM((parts, *xs[0].shape), xs[0].dtype),
            pltpu.SemaphoreType.DMA((links,)),
            pltpu.SemaphoreType.DMA((links,)),
            pltpu.SemaphoreType.DMA((parts,)),
        ],
        compiler_params=params(collective, LIMIT),
    )(*xs)


def close_kernel(planes, x_ref, gains, *refs):
    query_ref, key_ref, value_ref, output_ref, gain_ref, *refs = refs
    landed, mine, near_in, mid, far_in, send, receive, own = refs
    from_heads = x_ref.at[pl.ds(TEAM * landed.shape[1], mine.shape[0])]
    me = lax.axis_index("fsdp")
    place = lax.rem(me, TEAM)
    plane = lax.div(me, TEAM)
    others = [lax.rem(me + TEAM * k, planes * TEAM) for k in range(1, planes)]
    rows = landed.shape[1]

    def part(target):
        return x_ref.at[pl.ds(pl.multiple_of(target * rows, rows), rows)]

    keep = pltpu.make_async_copy(part(place), landed.at[place], own.at[0])
    keep.start()
    back, to = head_owner(me, planes)
    greet(me, range(1, TEAM), others, (to, back))
    sender = Sender(send, receive)
    k = sender.take()
    over = remote(from_heads, mine, send.at[k], receive.at[k], to)
    here = pltpu.make_async_copy(from_heads, mine, own.at[1])
    pl.when(to != me)(over.start)
    pl.when(to == me)(here.start)
    near = [
        sender(gains.at[flipped(place, m)], near_in.at[m - 1], flipped(me, m)) for m in SWAP_ORDER
    ]
    moves = [
        sender(part(flipped(place, m)), landed.at[place], flipped(me, m)) for m in SWAP_ORDER
    ]
    for copy in near:
        copy.wait_recv()
    summed = gains[place]
    for mask in range(1, TEAM):
        summed = summed + near_in[mask - 1]
    mid[...] = summed
    far = [
        sender(mid.at[lax.rem(plane + k + 1, planes)], far_in.at[k], other)
        for k, other in enumerate(others)
    ]
    pl.when(to != me)(over.wait)
    pl.when(to == me)(here.wait)
    width = mine.shape[1]
    for c in range(output_ref.shape[1] // width):
        output_ref[:, c * width : (c + 1) * width] = mine[c * rows : (c + 1) * rows].astype(f32)
    for copy in moves:
        copy.wait_recv()
    keep.wait()
    at = 0
    for ref in (query_ref, key_ref, value_ref):
        part_width = ref.shape[1] // TEAM
        for q in range(TEAM):
            ref[:, q * part_width : (q + 1) * part_width] = landed[
                q, :, at : at + part_width
            ].astype(f32)
        at += part_width
    for copy in far:
        copy.wait_recv()
    result = mid[plane]
    for k in range(planes - 1):
        result = result + far_in[k]
    gain_ref[...] = result
    sender.finish()


def closing(x, gains, rows, widths, planes, collective):
    links = 2 * (TEAM - 1) + planes
    block = gains.shape[2:]
    vmem = pl.BlockSpec(memory_space=pltpu.VMEM)
    like = jax.ShapeDtypeStruct
    return pl.pallas_call(
        functools.partial(close_kernel, planes),
        out_shape=(*(like((rows, w), f32) for w in widths), like(block, f32)),
        in_specs=[pl.BlockSpec(memory_space=pl.ANY), vmem],
        out_specs=(vmem,) * 5,
        scratch_shapes=[
            pltpu.VMEM((TEAM, rows, x.shape[1]), x.dtype),
            pltpu.VMEM((x.shape[0] - TEAM * rows, x.shape[1]), x.dtype),
            pltpu.VMEM((TEAM - 1, planes, *block), f32),
            pltpu.VMEM((planes, *block), f32),
            pltpu.VMEM((planes - 1, *block), f32),
            pltpu.SemaphoreType.DMA((links,)),
            pltpu.SemaphoreType.DMA((links,)),
            pltpu.SemaphoreType.DMA((2,)),
        ],
        compiler_params=params(collective, LIMIT),
    )(x, gains)


def visible_and_tables(ids_row, table):
    rows = ids_row.shape[1]
    row_at = lax.broadcasted_iota(jnp.int32, (rows, rows), 0)
    column_at = lax.broadcasted_iota(jnp.int32, (rows, rows), 1)
    ids_column = jnp.sum(jnp.where(row_at == column_at, ids_row, 0.0), axis=1, keepdims=True)
    visible = (ids_column == ids_row) & (column_at <= row_at)
    sequence = table.shape[0]
    place = jnp.sum(visible.astype(f32), axis=1, keepdims=True) - 1.0
    at = lax.broadcasted_iota(jnp.int32, (rows, sequence), 1).astype(f32)
    chosen = (at == place).astype(bf16)
    both = simple_product(chosen, table)
    width = 2 * HEAD_SIZE
    both = (both[:, :width] + both[:, width : 2 * width]) + both[:, 2 * width :]
    return visible, both[:, :HEAD_SIZE], both[:, HEAD_SIZE:]


def softmax(query, key, visible):
    scores = dot_last(query, key) * HEAD_SIZE ** (-0.5)
    scores = jnp.where(visible, scores, -1e30)
    expos = jnp.exp(scores - jnp.max(scores, axis=1, keepdims=True))
    return expos / jnp.sum(expos, axis=1, keepdims=True)


def attend_kernel(
    x_ref, gain, weight, ids_row, table, query_gain, key_gain,
    normed_ref, raw_ref, turned_ref, value_ref, context_ref,
):
    x = x_ref[...].astype(f32)
    scale = lax.rsqrt(jnp.mean(x * x, axis=1, keepdims=True) + epsilon)
    normed = (x * scale * gain[...]).astype(bf16)
    normed_ref[...] = normed
    projected = simple_product(normed, weight[...])
    visible, cosine, sine = visible_and_tables(ids_row[0], table[...])
    heads = context_ref.shape[1] // HEAD_SIZE
    raw_ref[...] = projected[:, : (heads + 1) * HEAD_SIZE]
    value = projected[:, (heads + 1) * HEAD_SIZE :].astype(bf16)
    value_ref[...] = value
    turned = []
    for h in range(heads + 1):
        raw = projected[:, h * HEAD_SIZE : (h + 1) * HEAD_SIZE]
        head_gain = query_gain if h < heads else key_gain
        y = raw * lax.rsqrt(jnp.mean(raw * raw, axis=1, keepdims=True) + epsilon) * head_gain[...]
        y = y * cosine + pltpu.roll(y, HEAD_SIZE // 2, 1) * sine
        turned.append(y.astype(bf16))
        turned_ref[:, h * HEAD_SIZE : (h + 1) * HEAD_SIZE] = turned[-1]
    for h in range(heads):
        probs = softmax(turned[h], turned[heads], visible).astype(bf16)
        context = simple_product(probs, value)
        context_ref[:, h * HEAD_SIZE : (h + 1) * HEAD_SIZE] = context.astype(bf16)


def by_step(*shape):
    return pl.BlockSpec(shape, lambda i: (i, *(0 for _ in shape[1:])))


def fixed(*shape):
    return pl.BlockSpec(shape, lambda i: tuple(0 for _ in shape))


def attend(x, gain, weight, ids, table, query_gain, key_gain):
    rows, width = x.shape
    out = weight.shape[1]
    like = jax.ShapeDtypeStruct
    heads = out - 2 * HEAD_SIZE
    return pl.pallas_call(
        attend_kernel,
        grid=(rows // STEP,),
        out_shape=(
            like((rows, width), bf16),
            like((rows, heads + HEAD_SIZE), f32),
            like((rows, heads + HEAD_SIZE), bf16),
            like((rows, HEAD_SIZE), bf16),
            like((rows, heads), bf16),
        ),
        in_specs=[
            by_step(STEP, width),
            fixed(1, width),
            fixed(width, out),
            by_step(1, 1, STEP),
            fixed(*table.shape),
            fixed(1, HEAD_SIZE),
            fixed(1, HEAD_SIZE),
        ],
        out_specs=(
            by_step(STEP, width),
            by_step(STEP, heads + HEAD_SIZE),
            by_step(STEP, heads + HEAD_SIZE),
            by_step(STEP, HEAD_SIZE),
            by_step(STEP, heads),
        ),
        compiler_params=pltpu.CompilerParams(vmem_limit_bytes=LIMIT),
        cost_estimate=pl.CostEstimate(
            flops=2 * rows * width * out, bytes_accessed=8 * rows * width, transcendentals=0
        ),
    )(x, gain, weight, ids, table, query_gain, key_gain)


def attend_back_kernel(
    grad_ref, out_weight, context_ref, raw_ref, turned_ref, value_ref, normed_ref,
    ids_row, table, query_gain, key_gain,
    grad_raw_ref, merged_ref, grad_gains_ref, out_sum, weight_sum,
):
    step = pl.program_id(0)

    @pl.when(step == 0)
    def _():
        out_sum[...] = jnp.zeros_like(out_sum)
        weight_sum[...] = jnp.zeros_like(weight_sum)
        grad_gains_ref[...] = jnp.zeros_like(grad_gains_ref)

    grad = grad_ref[...]
    grad_context = dot_last(grad, out_weight[...]).astype(bf16)
    out_sum[...] += dot_first(context_ref[...], grad)
    visible, cosine, sine = visible_and_tables(ids_row[0], table[...])
    heads = context_ref.shape[1] // HEAD_SIZE
    value = value_ref[...]
    key = turned_ref[:, heads * HEAD_SIZE :]
    grads = []
    grad_value = 0.0
    grad_key = 0.0
    for h in range(heads):
        at = slice(h * HEAD_SIZE, (h + 1) * HEAD_SIZE)
        query = turned_ref[:, at]
        probs = softmax(query, key, visible)
        grad_value = grad_value + dot_first(probs.astype(bf16), grad_context[:, at])
        grad_probs = dot_last(grad_context[:, at], value)
        inner = jnp.sum(probs * grad_probs, axis=1, keepdims=True)
        grad_scores = (probs * (grad_probs - inner)).astype(bf16)
        grads.append(simple_product(grad_scores, key) * HEAD_SIZE ** (-0.5))
        grad_key = grad_key + dot_first(grad_scores, query) * HEAD_SIZE ** (-0.5)
    grads.append(grad_key)
    parts = []
    for h in range(heads + 1):
        raw = raw_ref[:, h * HEAD_SIZE : (h + 1) * HEAD_SIZE]
        head_gain = query_gain[...] if h < heads else key_gain[...]
        scale = lax.rsqrt(jnp.mean(raw * raw, axis=1, keepdims=True) + epsilon)
        turned = grads[h] * cosine + pltpu.roll(grads[h] * sine, HEAD_SIZE // 2, 1)
        row = 0 if h < heads else 1
        grad_gains_ref[row : row + 1, :] += jnp.sum(turned * raw * scale, axis=0, keepdims=True)
        turned = turned * head_gain
        mean = jnp.mean(turned * raw, axis=1, keepdims=True)
        parts.append((turned * scale - raw * (scale * scale * scale * mean)).astype(bf16))
    parts.append(grad_value.astype(bf16))
    grad_raw = jnp.concatenate(parts, axis=1)
    grad_raw_ref[...] = grad_raw
    weight_sum[...] += dot_first(normed_ref[...], grad_raw)

    @pl.when(step == pl.num_programs(0) - 1)
    def _():
        planes, _, width = merged_ref.shape
        rows, block = weight_sum.shape[0] // planes, out_sum.shape[0] // planes
        for g in range(planes):
            merged_ref[g, :rows] = weight_sum[g * rows : (g + 1) * rows].astype(bf16)
            for c in range(out_sum.shape[1] // width):
                at = rows + c * block
                merged_ref[g, at : at + block] = out_sum[
                    g * block : (g + 1) * block, c * width : (c + 1) * width
                ].astype(bf16)


def attend_back(
    grad, out_weight, context, raw, turned, value, normed, ids, table, query_gain, key_gain, planes
):
    rows, width = grad.shape
    heads = context.shape[1]
    out = heads + 2 * HEAD_SIZE
    merged = (planes, (width + heads * width // out) // planes, out)
    like = jax.ShapeDtypeStruct
    return pl.pallas_call(
        attend_back_kernel,
        grid=(rows // STEP,),
        out_shape=(
            like((rows, out), bf16),
            like(merged, bf16),
            like((8, HEAD_SIZE), f32),
        ),
        in_specs=[
            by_step(STEP, width),
            fixed(heads, width),
            by_step(STEP, heads),
            by_step(STEP, heads + HEAD_SIZE),
            by_step(STEP, heads + HEAD_SIZE),
            by_step(STEP, HEAD_SIZE),
            by_step(STEP, width),
            by_step(1, 1, STEP),
            fixed(*table.shape),
            fixed(1, HEAD_SIZE),
            fixed(1, HEAD_SIZE),
        ],
        out_specs=(
            by_step(STEP, out),
            fixed(*merged),
            fixed(8, HEAD_SIZE),
        ),
        scratch_shapes=[pltpu.VMEM((heads, width), f32), pltpu.VMEM((width, out), f32)],
        compiler_params=pltpu.CompilerParams(vmem_limit_bytes=LIMIT),
        cost_estimate=pl.CostEstimate(
            flops=2 * rows * width * (out + 2 * heads),
            bytes_accessed=8 * rows * width,
            transcendentals=0,
        ),
    )(grad, out_weight, context, raw, turned, value, normed, ids, table, query_gain, key_gain)


def hidden(two, weight):
    return simple_product(two, weight)


def hidden_grads(both, cot, down):
    units = both.shape[1] // 2
    gate, up = both[:, :units], both[:, units:]
    grad_act = dot_last(cot, down)
    sigma = 1.0 / (1.0 + jnp.exp(-gate))
    silu_gate = gate * sigma
    act = (silu_gate * up).astype(bf16)
    grad_gate = (grad_act * up * (sigma * (1.0 + gate * (1.0 - sigma)))).astype(bf16)
    grad_up = (grad_act * silu_gate).astype(bf16)
    return act, grad_gate, grad_up


def feed_kernel(
    two_in, cot_in, weight_in, down_in, two_out, act, grad_both,
    two, cot, weight, down, both, send, receive, own,
):
    me = lax.axis_index("fsdp")
    place = lax.rem(me, TEAM)
    keeps = []
    for source, target in (
        (two_in, two.at[place]),
        (weight_in, weight),
        (down_in.at[pl.ds(0, down.shape[0])], down),
        (cot_in, cot),
    ):
        copy = pltpu.make_async_copy(source, target, own.at[len(keeps)])
        copy.start()
        keeps.append(copy)
    greet(me, (1, 2, 4))
    sender = Sender(send, receive)
    moves = Gather(sender, two_in, two, me)
    moves.start()
    rows, units = act.shape[1:]
    outs = []

    def work(mask):
        chip = pl.ds(2 * lax.div(flipped(place, mask), 2), 2)
        copy = pltpu.make_async_copy(two.at[chip], two_out.at[chip], own.at[4 + len(outs)])
        copy.start()
        outs.append(copy)
        flat = two[chip].reshape(2 * rows, two.shape[2])
        both[...] = simple_product(flat, weight[...])
        flat = cot[chip].reshape(2 * rows, two.shape[2])
        a, grad_gate, grad_up = hidden_grads(both[...], flat, down[...])
        act[chip] = a.reshape(2, rows, units)
        grad_both[chip, :, :units] = grad_gate.reshape(2, rows, units)
        grad_both[chip, :, units:] = grad_up.reshape(2, rows, units)

    moves.forward()
    moves.across()
    for copy in keeps:
        copy.wait()
    for copy in moves.late[:2]:
        copy.wait_recv()
    work(0)
    moves.diagonal()
    for mask, first, second in ((2, 2, 4), (4, 3, 5), (6, 6, 7)):
        moves.late[first].wait_recv()
        moves.late[second].wait_recv()
        work(mask)
    sender.finish()
    for copy in outs:
        copy.wait()


def feed(two, cot, weight, down, collective):
    rows, width = two.shape
    units = weight.shape[1] // 2
    vmem = pl.BlockSpec(memory_space=pltpu.VMEM)
    anywhere = pl.BlockSpec(memory_space=pl.ANY)
    like = jax.ShapeDtypeStruct
    return pl.pallas_call(
        feed_kernel,
        out_shape=(
            like((TEAM, rows, width), bf16),
            like((TEAM, rows, units), bf16),
            like((TEAM, rows, 2 * units), bf16),
        ),
        in_specs=[anywhere] * 4,
        out_specs=(anywhere, vmem, vmem),
        scratch_shapes=[
            pltpu.VMEM((TEAM, rows, width), bf16),
            pltpu.VMEM(cot.shape, bf16),
            pltpu.VMEM(weight.shape, bf16),
            pltpu.VMEM((units, width), bf16),
            pltpu.VMEM((2 * rows, 2 * units), f32),
            pltpu.SemaphoreType.DMA((14,)),
            pltpu.SemaphoreType.DMA((14,)),
            pltpu.SemaphoreType.DMA((8,)),
        ],
        compiler_params=params(collective, LIMIT),
        cost_estimate=pl.CostEstimate(
            flops=6 * TEAM * rows * width * units,
            bytes_accessed=6 * TEAM * rows * width,
            transcendentals=0,
        ),
    )(two, cot, weight, down)


def feed_rest_kernel(two, cot, weight, down, act, grad_both):
    blocks, rows, units = act.shape
    both = simple_product(two[...].reshape(blocks * rows, -1), weight[...])
    flat = cot[...].reshape(blocks * rows, -1)
    a, grad_gate, grad_up = hidden_grads(both, flat, down[...])
    act[...] = a.reshape(blocks, rows, units)
    grad_both[:, :, :units] = grad_gate.reshape(blocks, rows, units)
    grad_both[:, :, units:] = grad_up.reshape(blocks, rows, units)


def feed_rest(two, cot, weight, down, part):
    _, rows, width = two.shape
    units = weight.shape[1] // 2
    like = jax.ShapeDtypeStruct
    return pl.pallas_call(
        feed_rest_kernel,
        grid=(TEAM // 2,),
        out_shape=(like((TEAM, rows, units), bf16), like((TEAM, rows, 2 * units), bf16)),
        in_specs=[
            by_step(2, rows, width),
            by_step(2, rows, width),
            fixed(*weight.shape),
            pl.BlockSpec((units, width), lambda i: (part, 0)),
        ],
        out_specs=(by_step(2, rows, units), by_step(2, rows, 2 * units)),
        compiler_params=pltpu.CompilerParams(vmem_limit_bytes=LIMIT),
        cost_estimate=pl.CostEstimate(
            flops=6 * TEAM * rows * width * units,
            bytes_accessed=4 * TEAM * rows * width,
            transcendentals=0,
        ),
    )(two, cot, weight, down)


def local(
    devices,
    tokens,
    segments,
    micro_live,
    cotangent,
    w_query,
    key_weight,
    value_weight,
    w_output,
    attn_gain,
    query_norm_gain,
    key_gain,
    w_gate,
    w_up,
    w_down,
    mlp_gain,
):
    planes = devices // TEAM
    lines = [[place + TEAM * k for k in range(planes)] for place in range(TEAM)]
    slots, sequence = segments.shape
    token_count, width = tokens.shape
    groups = QUERY_HEADS // KEY_VALUE_HEADS
    rows = w_query.shape[0]
    parts = 2 if planes % 2 == 0 else 1
    team_rows = TEAM * token_count
    head_width = groups * HEAD_SIZE
    me = lax.axis_index("fsdp")
    plane = me // TEAM

    def gather_line(x):
        return lax.all_gather(x, "fsdp", axis=0, tiled=True, axis_index_groups=lines)

    def sum_line(x):
        return lax.psum_scatter(
            x, "fsdp", scatter_dimension=0, tiled=True, axis_index_groups=lines
        )

    slot_live = (lax.broadcasted_iota(jnp.int32, (slots, 1), 0) < micro_live[0]).astype(f32)
    row_live = jnp.broadcast_to(slot_live, (slots, sequence)).reshape(token_count, 1)
    cot_b = cotangent * row_live.astype(bf16)

    down_weight = gather_line(w_down)
    unit_slices = units_out(w_gate, w_up, planes, parts, 3)
    query_in, *unit_slices = lax.optimization_barrier((w_query, *unit_slices))
    smalls = [x[None] for x in (attn_gain, mlp_gain, query_norm_gain, key_gain)] + [segments]
    opened = opening(
        query_in, key_weight, value_weight, w_output, tokens, cot_b, smalls, planes, 1
    )
    qkv_weight, output_weight, team_tokens, team_cot = opened[:4]
    norm_gain, mlp_norm_gain, qgain, kgain, ids = opened[4:]
    mlp_norm_gain = mlp_norm_gain.reshape(width)
    qkv_weight = qkv_weight.reshape(width, -1)
    output_weight = output_weight.reshape(head_width, width)
    *unit_slices, _ = lax.optimization_barrier((*unit_slices, qkv_weight))
    unit_weights = [gather_line(x.reshape(TEAM * rows, -1)) for x in unit_slices]
    table = jnp.asarray(rotation_tables(sequence))

    inputs = tokens.astype(f32)
    team_normed, raw, turned, value_b, context_b = attend(
        team_tokens.reshape(team_rows, width), norm_gain, qkv_weight, ids, table, qgain, kgain
    )
    middle = inputs + reduce(
        [context_b.reshape(TEAM, token_count, head_width)], [output_weight], False, 2
    )

    normed_two = root_mean_square_norm(middle, mlp_norm_gain).astype(bf16)
    team_two, act, grad_both = feed(normed_two, team_cot, unit_weights[0], down_weight, 0)
    acts, grads_both = [act], [grad_both]
    flat_two = team_two.reshape(team_rows, width)

    def unit_grads(grad_both):
        return dot_first(flat_two, grad_both.reshape(team_rows, -1)).astype(bf16)

    grad_units = [unit_grads(grad_both)]
    for k in range(1, parts):
        rest_two, grad_units[k - 1] = lax.optimization_barrier((team_two, grad_units[k - 1]))
        act, grad_both = feed_rest(rest_two, team_cot, unit_weights[k], down_weight, k)
        acts.append(act)
        grads_both.append(grad_both)
        grad_units.append(unit_grads(grad_both))
    grad_units = [sum_line(g) for g in grad_units]
    grad_down = sum_line(
        jnp.concatenate(
            [
                dot_first(a.reshape(team_rows, -1), team_cot.reshape(team_rows, width))
                for a in acts
            ],
            axis=0,
        ).astype(bf16)
    )
    grad_normed_two = reduce(grads_both, unit_weights, True, 4)
    _, pull_two = jax.vjp(root_mean_square_norm, middle, mlp_norm_gain)
    middle_part, grad_mgain = pull_two(grad_normed_two)
    grad_middle = cot_b.astype(f32) + middle_part
    team_grad = gather(grad_middle.astype(bf16), 10)

    grad_qkv, grad_attention, grad_head_gains = attend_back(
        team_grad,
        output_weight,
        context_b,
        raw,
        turned,
        value_b,
        team_normed,
        ids,
        table,
        qgain,
        kgain,
        planes,
    )
    grad_attention = sum_line(grad_attention.reshape(-1, grad_attention.shape[2]))
    grad_normed = reduce(
        [grad_qkv.reshape(TEAM, token_count, -1)], [qkv_weight], True, 5
    )
    _, pull_one = jax.vjp(root_mean_square_norm, inputs, norm_gain.reshape(width))
    input_part, grad_again = pull_one(grad_normed)
    grad_tokens = (grad_middle + input_part).astype(bf16)
    layer_out = (row_live * (middle + reduce(acts, [down_weight] * parts, False, 7, cut=True))).astype(bf16)

    def by_owner(vector):
        vector = vector.reshape(devices, -1)
        return jnp.pad(vector, ((0, 0), (0, 128 - vector.shape[1])))

    gains = jnp.stack(
        [by_owner(v) for v in (grad_again, grad_mgain, grad_head_gains[0], grad_head_gains[1])], axis=1
    )
    gains = jnp.pad(gains, ((0, 0), (0, 4), (0, 0)))
    gains = gains.reshape(planes, TEAM, 8, 128).transpose(1, 0, 2, 3)

    *grad_units, _ = lax.optimization_barrier((*grad_units, layer_out))
    grad_gate, grad_up = units_home(
        [g.reshape(TEAM, rows, -1) for g in grad_units], planes, 8
    )
    grad_attention, grad_gate, grad_up = lax.optimization_barrier(
        (grad_attention, grad_gate, grad_up)
    )
    grad_query, grad_key, grad_value_w, grad_output, gains = closing(
        grad_attention,
        gains,
        rows,
        (w_query.shape[1], key_weight.shape[1], value_weight.shape[1], width),
        planes,
        9,
    )
    grad_down, gains = lax.optimization_barrier((grad_down, gains))
    return (
        layer_out,
        grad_tokens,
        grad_query,
        grad_key,
        grad_value_w,
        grad_output,
        gains[0, : attn_gain.shape[0]],
        gains[2, : query_norm_gain.shape[0]],
        gains[3, : key_gain.shape[0]],
        grad_gate,
        grad_up,
        grad_down.astype(f32),
        gains[1, : mlp_gain.shape[0]],
    )


def solution(mesh):
    by_rows, by_entry = P("fsdp", None), P("fsdp")
    return jax.shard_map(
        functools.partial(local, mesh.shape["fsdp"]),
        mesh=mesh,
        in_specs=(
            by_rows,
            by_rows,
            by_entry,
            by_rows,
            by_rows,
            by_rows,
            by_rows,
            by_rows,
            by_entry,
            by_entry,
            by_entry,
            by_rows,
            by_rows,
            by_rows,
            by_entry,
        ),
        out_specs=(
            by_rows,
            by_rows,
            by_rows,
            by_rows,
            by_rows,
            by_rows,
            by_entry,
            by_entry,
            by_entry,
            by_rows,
            by_rows,
            by_rows,
            by_entry,
        ),
        check_vma=False,
    )
```

time: 2830 us -> 558 us (0.20)
  waiting for transfers between devices: 2450 us -> 26.3 us
  Pallas kernels: 0 us -> 447 us
  matrix products: 222 us -> 30.2 us
  blocking collectives: 82.4 us -> 0 us
    reduce_scatter x7 -> x4, waiting for transfers between devices: 1800 us -> 0.05 us  [sum_line(): lax.psum_scatter(x, 'fsdp', scatter_dimension=0, tiled=True, axis_index_g...]
    all_gather x7 -> x3, waiting for transfers between devices: 646 us -> 24.8 us  [gather_line(): lax.all_gather(x, 'fsdp', axis=0, tiled=True, axis_index_groups=lines)]
    pallas_call x0 -> x13, Pallas kernels: none -> 447 us  [the longest x4 145 us: reduce(): pl.pallas_call(functools.partial(reduce_kernel, turned, cut, pairs), out_...]
    dot_general x20 -> x0, matrix products: 131 us -> none  [the longest x7 68.6 us: dot_last(): lax.dot_general(left, right, (((1,), (1,)), ((), ())), preferred_element_...]
    unnamed x2 -> x0, blocking collectives: 82.4 us -> none
    dot_general x7 -> x4, matrix products: 91.5 us -> 30.2 us  [dot_first(): lax.dot_general(left, right, (((0,), (0,)), ((), ())), preferred_element_...]
  transfers between devices with their start and end apart: 14 -> 7, of which waited for: 13 -> 2; matrix products, arithmetic and copies ran while one was open for 7% -> 9% of each run, Pallas kernels for 0% -> 81%
where the time goes in v2:
time: 558 us; the launch traced here: 548 us
  Pallas kernels  447 us (80%)
  matrix products  30.2 us (5%)
  waiting for transfers between devices  26.3 us (5%)
  other arithmetic  18.5 us (3%)
  between operations  15.5 us (3%)
  local copies, waits for them, and re-layouts  10.9 us (2%)
    pallas_call x4, Pallas kernels, reduce(): pl.pallas_call(functools.partial(reduce_kernel, turned, cut, pairs), out_...  145 us
    pallas_call x1, Pallas kernels, opening(): pl.pallas_call(functools.partial(open_kernel, planes), out_shape=(like((p...  104 us
    pallas_call x1, Pallas kernels, feed(): pl.pallas_call(feed_kernel, out_shape=(like((TEAM, rows, width), bf16), l...  38.8 us
    pallas_call x1, Pallas kernels, gather(): pl.pallas_call(gather_kernel, out_shape=jax.ShapeDtypeStruct((TEAM, rows,...  31.7 us
    dot_general x4, matrix products, dot_first(): lax.dot_general(left, right, (((0,), (0,)), ((), ())), preferred_element_...  30.2 us
    pallas_call x1, Pallas kernels, closing(): pl.pallas_call(functools.partial(close_kernel, planes), out_shape=(*(like...  26.2 us
    pallas_call x1, Pallas kernels, attend_back(): pl.pallas_call(attend_back_kernel, grid=(rows // STEP,), out_shape=(like(...  25.2 us
    all_gather x3, waiting for transfers between devices, gather_line(): lax.all_gather(x, 'fsdp', axis=0, tiled=True, axis_index_groups=lines)  24.8 us
  transfers between devices with their start and end apart: 7, of which 2 were waited for; matrix products, arithmetic and copies ran while one was open for 9% of the time, Pallas kernels for 81%

profile of v2, /device:TPU:0, one launch (start us, length us, event | category | flops | bytes accessed | tf_op | source)
XLA Modules:
  0.0 548.4 jit_solution(16652445343202055069)
XLA Ops:
  8.8 24.2 %shard_map.255 = (bf16[8,64,768]{2,1,0:T(8,128)(2,1)}, bf16[8,64,768]{2,1,0:T(8,128)(2,1)}) custom-call(bf16[64,6144]{1,0:T(8,128)(2,1)} %gate_in.1, bf16[64,6144]{1,0:T(8,128)(2,1)} %up_in.1), custom_call_target="tpu_custom_call" | custom-call | tf_op jit(solution)/shard_map/pallas_call | solution.py:584
  34.0 103.9 %shard_map.256 = (bf16[4,8,64,512]{3,2,1,0:T(8,128)(2,1)}, bf16[4,64,2048]{2,1,0:T(8,128)(2,1)}, bf16[8,192,2048]{2,1,0:T(8,128)(2,1)}, bf16[8,192,2048]{2,1,0:T...) custom-call(bf16[64,2048]{1,0:T(8,128)(2,1)} %query_in, ...), custom_call_target="tpu_custom_call" | custom-call | tf_op jit(solution)/shard_map/pallas_call | solution.py:525
  138.7 16.0 %shard_map.257 = (bf16[1536,2048]{1,0:T(8,128)(2,1)}, f32[1536,384]{1,0:T(8,128)}, bf16[1536,384]{1,0:T(8,128)(2,1)}, bf16[1536,128]{1,0:T(8,128)(2,1)}, bf16[1536,256]{1,0:T(8,128)(2,1)}) custom-call(bf16[1536,2048]{1,0:T(8,128)(2,1)} %bitcast.73, f32[1,2048]{1,0:T(1,128)} %get-tuple-element.62.gain, bf16[2048,512]{1,0:T(8,128)(2,1)} %bitcast.74, ...), custom_call_target="tpu_custom_call" | custom-call | flops 3221225472 | bytes 25165824 | tf_op jit(solution)/shard_map/pallas_call | solution.py:806
  154.8 33.5 %shard_map.258 = f32[192,2048]{1,0:T(8,128)} custom-call(bf16[8,192,256]{2,1,0:T(8,128)(2,1)} %bitcast.79, bf16[256,2048]{1,0:T(8,128)(2,1)} %bitcast.76), custom_call_target="tpu_custom_call" | custom-call | flops 1610612736 | bytes 3407872 | tf_op jit(solution)/shard_map/pallas_call | solution.py:342
  191.2 9.4 %all-gather.4.cloned.1.call-done.weight_in.refs_2_ = bf16[2048,768]{1,0:T(8,128)(2,1)} async-done(((bf16[512,768]{1,0:T(8,128)(2,1)}), bf16[2048,768]{1,0:T(8,128)(2,1)}) %all-gather.4.cloned.1.call-update) | async-done | bytes 3145744 | tf_op jit(solution)/shard_map/all_gather | solution.py:1114
  200.5 38.8 %shard_map.259 = (bf16[8,192,2048]{2,1,0:T(8,128)(2,1)}, bf16[8,192,384]{2,1,0:T(8,128)(2,1)}, bf16[8,192,768]{2,1,0:T(8,128)(2,1)}) custom-call(bf16[192,2048]{1,0:T(8,128)(2,1)} %multiply_convert_fusion.1.two_in, bf16[8,192,2048]{2,1,0:T(8,128)(2,1)} %get-tuple-element.70.cot_in.cot, bf16[2048,768]{1,0:T(8,128)(2,1)} %all-gather.4.cloned.1.call-done.weight_in.refs_2_, ...), custom_call_target="tpu_custom_call" | custom-call | flops 7247757312 | bytes 18874368 | tf_op jit(solution)/shard_map/pallas_call | solution.py:1021
  239.4 9.4 %bitcast_convert_fusion.1 = bf16[2048,768]{1,0:T(8,128)(2,1)} fusion(bf16[8,192,2048]{2,1,0:T(8,128)(2,1)} %get-tuple-element.77.two, bf16[8,192,768]{2,1,0:T(8,128)(2,1)} %get-tuple-element.76.refs_0_), kind=kOutput, calls=%fused_computation.1 | convolution fusion | flops 4833411072 | bytes 11796480 | tf_op jit(solution)/shard_map/dot_general | solution.py:50
  248.9 15.4 %all-gather.8.cloned.1.call-done.weight.refs_3_ = bf16[2048,768]{1,0:T(8,128)(2,1)} async-done(((bf16[512,768]{1,0:T(8,128)(2,1)}), bf16[2048,768]{1,0:T(8,128)(2,1)}) %all-gather.8.cloned.1.call-update) | async-done | bytes 3145744 | tf_op jit(solution)/shard_map/all_gather | solution.py:1114
  264.3 13.6 %shard_map.260 = (bf16[8,192,384]{2,1,0:T(8,128)(2,1)}, bf16[8,192,768]{2,1,0:T(8,128)(2,1)}) custom-call(bf16[8,192,2048]{2,1,0:T(8,128)(2,1)} %get-tuple-element.77.two, bf16[8,192,2048]{2,1,0:T(8,128)(2,1)} %get-tuple-element.70.cot_in.cot, bf16[2048,768]{1,0:T(8,128)(2,1)} %all-gather.8.cloned.1.call-done.weight.refs_3_, ...), custom_call_target="tpu_custom_call" | custom-call | flops 7247757312 | bytes 12582912 | tf_op jit(solution)/shard_map/pallas_call | solution.py:1063
  277.9 9.2 %bitcast_convert_fusion = bf16[2048,768]{1,0:T(8,128)(2,1)} fusion(bf16[8,192,2048]{2,1,0:T(8,128)(2,1)} %get-tuple-element.77.two, bf16[8,192,768]{2,1,0:T(8,128)(2,1)} %get-tuple-element.80.refs_1_), kind=kOutput, calls=%fused_computation | convolution fusion | flops 4833411072 | bytes 11796480 | tf_op jit(solution)/shard_map/dot_general | solution.py:50
  287.2 39.9 %shard_map.262 = f32[192,2048]{1,0:T(8,128)} custom-call(bf16[8,192,768]{2,1,0:T(8,128)(2,1)} %get-tuple-element.76.refs_0_, bf16[8,192,768]{2,1,0:T(8,128)(2,1)} %get-tuple-element.80.refs_1_, bf16[2048,768]{1,0:T(8,128)(2,1)} %all-gather.4.cloned.1.call-done.weight_in.refs_2_, bf16[2048,768]{1,0:T(8,128)(2,1)} %all-gather.8.cloned.1.call-done.weight.refs_3_), custom_call_target="tpu_custom_call" | custom-call | flops 9663676416 | bytes 12582912 | tf_op jit(solution)/shard_map/pallas_call | solution.py:342
  327.2 1.9 multiply_reduce_fusion
  330.6 31.7 %shard_map.263 = bf16[8,192,2048]{2,1,0:T(8,128)(2,1)} custom-call(bf16[192,2048]{1,0:T(8,128)(2,1)} %fusion.10.x_ref), custom_call_target="tpu_custom_call" | custom-call | tf_op jit(solution)/shard_map/pallas_call | solution.py:192
  362.3 25.2 %shard_map.264 = (bf16[1536,512]{1,0:T(8,128)(2,1)}, bf16[4,768,512]{2,1,0:T(8,128)(2,1)}, f32[8,128]{1,0:T(8,128)}) custom-call(bf16[1536,2048]{1,0:T(8,128)(2,1)} %bitcast.56, bf16[256,2048]{1,0:T(8,128)(2,1)} %bitcast.77, bf16[1536,256]{1,0:T(8,128)(2,1)} %get-tuple-element.67.context_ref, f32[1536,384]{1,0:T(8,128)} %get-tuple-element.81.raw_ref, ...), custom_call_target="tpu_custom_call" | custom-call | flops 6442450944 | bytes 25165824 | tf_op jit(solution)/shard_map/pallas_call | solution.py:910
  387.6 5.9 %bitcast_convert_fusion.3 = bf16[384,2048]{1,0:T(8,128)(2,1)S(1)} fusion(bf16[8,192,384]{2,1,0:T(8,128)(2,1)} %get-tuple-element.74.refs_0_, bf16[8,192,2048]{2,1,0:T(8,128)(2,1)} %get-tuple-element.70.cot_in.cot), kind=kOutput, calls=%fused_computation.4 | convolution fusion | flops 2416705536 | bytes 9043968 | tf_op jit(solution)/shard_map/dot_general | solution.py:50
  393.5 5.7 %bitcast_convert_fusion.2 = bf16[384,2048]{1,0:T(8,128)(2,1)S(1)} fusion(bf16[8,192,384]{2,1,0:T(8,128)(2,1)S(1)} %copy-done.6, bf16[8,192,2048]{2,1,0:T(8,128)(2,1)} %get-tuple-element.70.cot_in.cot), kind=kOutput, calls=%fused_computation.3 | convolution fusion | flops 2416705536 | bytes 9043968 | tf_op jit(solution)/shard_map/dot_general | solution.py:50
  399.1 2.0 pad_maximum_fusion
  401.3 34.9 %shard_map.265 = f32[192,2048]{1,0:T(8,128)} custom-call(bf16[8,192,512]{2,1,0:T(8,128)(2,1)} %bitcast.78, bf16[2048,512]{1,0:T(8,128)(2,1)} %bitcast.75), custom_call_target="tpu_custom_call" | custom-call | flops 3221225472 | bytes 5242880 | tf_op jit(solution)/shard_map/pallas_call | solution.py:342
  436.2 2.2 fusion.6
  440.2 36.8 %shard_map.261 = f32[192,2048]{1,0:T(8,128)} custom-call(bf16[8,192,384]{2,1,0:T(8,128)(2,1)} %get-tuple-element.74.refs_0_, bf16[8,192,384]{2,1,0:T(8,128)(2,1)} %get-tuple-element.79.refs_1_, bf16[768,2048]{1,0:T(8,128)(2,1)} %all-gather.6.cloned.1.call-done.down_in.down.refs_2_.refs_3_, ...), custom_call_target="tpu_custom_call" | custom-call | flops 4831838208 | bytes 7077888 | tf_op jit(solution)/shard_map/pallas_call | solution.py:342
  477.0 4.5 fusion.2
  481.6 22.1 %shard_map.266 = (f32[64,6144]{1,0:T(8,128)}, f32[64,6144]{1,0:T(8,128)}) custom-call(bf16[8,64,768]{2,1,0:T(8,128)(2,1)} %bitcast.58, bf16[8,64,768]{2,1,0:T(8,128)(2,1)} %bitcast.59), custom_call_target="tpu_custom_call" | custom-call | tf_op jit(solution)/shard_map/pallas_call | solution.py:639
  503.7 26.2 %shard_map.267 = (f32[64,2048]{1,0:T(8,128)}, f32[64,1024]{1,0:T(8,128)}, f32[64,1024]{1,0:T(8,128)}, f32[64,2048]{1,0:T(8,128)}, f32[8,128]{1,0:T(8,128)}) custom-call(bf16[768,512]{1,0:T(8,128)(2,1)} %reduce-scatter.5.cloned.1.call-done.x_ref, f32[8,4,8,128]{3,2,1,0:T(8,128)} %bitcast.62), custom_call_target="tpu_custom_call" | custom-call | tf_op jit(solution)/shard_map/pallas_call | solution.py:723
  532.4 2.5 convert_element_type.62
  (75 shorter events, 18.0 us)
Async XLA Ops:
  7.2 25.8 %copy-start.2 = (bf16[192,2048]{1,0:T(8,128)(2,1)S(1)}, bf16[192,2048]{1,0:T(8,128)(2,1)}, u32[]{:S(2)}) copy-start(bf16[192,2048]{1,0:T(8,128)(2,1)} %param.19) | copy-start | bytes 2359300
  7.2 184.0 %all-gather.6.cloned.1.call-start = ((), (), s32[]{:S(2)}) async-start(), calls=%async_computation.5 | async-start | bytes 3932160 | tf_op jit(solution)/shard_map/all_gather | solution.py:1114
  7.9 192.6 %all-gather.4.cloned.1.call-start = ((), (), s32[]{:S(2)}) async-start(), calls=%async_computation.4 | async-start | bytes 3932160 | tf_op jit(solution)/shard_map/all_gather | solution.py:1114
  137.9 126.4 %all-gather.8.cloned.1.call-start = ((), (), s32[]{:S(2)}) async-start(), calls=%async_computation.6 | async-start | bytes 3932160 | tf_op jit(solution)/shard_map/all_gather | solution.py:1114
  138.7 342.9 %reduce-scatter.7.cloned.1.call-start = ((), (), s32[]{:S(2)}) async-start(), calls=%async_computation.8 | async-start | bytes 3932160 | tf_op jit(solution)/shard_map/reduce_scatter | solution.py:1117
  154.8 33.5 %copy-start.1 = (bf16[192,2048]{1,0:T(8,128)(2,1)S(1)}, bf16[192,2048]{1,0:T(8,128)(2,1)}, u32[]{:S(2)}) copy-start(bf16[192,2048]{1,0:T(8,128)(2,1)} %tokens_in.1) | copy-start | bytes 2359300
  188.3 1.8 copy-start.11
  248.8 232.8 %reduce-scatter.9.cloned.1.call-start = ((), (), s32[]{:S(2)}) async-start(), calls=%async_computation.9 | async-start | bytes 3932160 | tf_op jit(solution)/shard_map/reduce_scatter | solution.py:1117
  287.2 216.5 %reduce-scatter.5.cloned.1.call-start = ((), (), s32[]{:S(2)}) async-start(), calls=%async_computation.7 | async-start | bytes 3932160 | tf_op jit(solution)/shard_map/reduce_scatter | solution.py:1117
  327.1 2.0 copy-start
  327.1 2.1 copy-start.3
  387.5 142.4 %reduce-scatter.11.cloned.1.call-start = ((), (), s32[]{:S(2)}) async-start(), calls=%async_computation.10 | async-start | bytes 3932160 | tf_op jit(solution)/shard_map/reduce_scatter | solution.py:1117
  387.5 5.9 %copy-start.6 = (bf16[8,192,384]{2,1,0:T(8,128)(2,1)S(1)}, bf16[8,192,384]{2,1,0:T(8,128)(2,1)}, u32[]{:S(2)}) copy-start(bf16[8,192,384]{2,1,0:T(8,128)(2,1)} %get-tuple-element.79.refs_1_) | copy-start | bytes 3538948
  401.2 34.9 %copy-start.12 = (f32[1,2048]{1,0:T(1,128)S(1)}, f32[1,2048]{1,0:T(1,128)}, u32[]{:S(2)}) copy-start(f32[1,2048]{1,0:T(1,128)} %get-tuple-element.62.gain) | copy-start | bytes 24580
  529.9 5.1 copy-start.8
  532.4 3.3 copy-start.10
  532.4 4.0 copy-start.9
  535.0 2.2 copy-start.7
  535.0 3.0 copy-start.5
  538.0 2.0 copy-start.4
Sparse Core Ops, SparseCore 0:
  9.6 90.3 all-gather.5
  138.1 62.4 all-gather.3
  202.1 62.1 all-gather.7
  266.4 58.8 reduce-scatter.6
  327.5 60.2 reduce-scatter.8
  390.0 60.2 reduce-scatter.4
  452.6 60.8 reduce-scatter.10

commit v3 on v2

v3 whole, which is shorter than its diff:
```python
import functools

import jax
import jax.numpy as jnp
import numpy as np
from jax import lax
from jax.experimental import pallas as pl
from jax.experimental.pallas import tpu as pltpu
from jax.sharding import PartitionSpec as P

QUERY_HEADS = 16
KEY_VALUE_HEADS = 8
HEAD_SIZE = 128
TEAM = 8
STEP = 256

epsilon = 1e-06
base_theta = 1000000.0
MESH = pl.DeviceIdType.MESH
LIMIT = 60 * 2**20
f32 = jnp.float32
bf16 = jnp.bfloat16


def root_mean_square_norm(values, gain):
    return values * lax.rsqrt(jnp.mean(values * values, axis=-1, keepdims=True) + epsilon) * gain


def rotation_tables(positions):
    half = HEAD_SIZE // 2
    powers = -np.arange(half, dtype=np.float32) * np.float32(2.0) / np.float32(HEAD_SIZE)
    freqs = np.power(np.float32(base_theta), powers).astype(np.float32)
    angles = np.arange(positions, dtype=np.float32)[:, None] * freqs
    cosine, sine = np.cos(angles), np.sin(angles)
    rest = np.concatenate([cosine, cosine, -sine, sine], axis=1).astype(np.float32)
    parts = []
    for _ in range(3):
        parts.append(rest.astype(jnp.bfloat16))
        rest = rest - parts[-1].astype(np.float32)
    return np.concatenate(parts, axis=1)


def dot_last(left, right):
    return lax.dot_general(
        left, right, (((1,), (1,)), ((), ())), preferred_element_type=jnp.float32
    )


def dot_first(left, right):
    return lax.dot_general(
        left, right, (((0,), (0,)), ((), ())), preferred_element_type=jnp.float32
    )


def simple_product(left, right):
    return jnp.dot(left, right, preferred_element_type=jnp.float32)


def flipped(index, mask):
    for bit in (1, 2, 4):
        if mask & bit:
            index = index + bit * (1 - 2 * lax.rem(lax.div(index, bit), 2))
    return index


def greet(me, masks, others=()):
    barrier = pltpu.get_barrier_semaphore()
    for device in (*(flipped(me, mask) for mask in masks), *others):
        pl.semaphore_signal(barrier, inc=1, device_id=(device,), device_id_type=MESH)
    pl.semaphore_wait(barrier, len(masks) + len(others))


def remote(source, target, send, receive, device):
    return pltpu.make_async_remote_copy(
        src_ref=source,
        dst_ref=target,
        send_sem=send,
        recv_sem=receive,
        device_id=(device,),
        device_id_type=MESH,
    )


def params(collective, limit=None):
    if limit is None:
        return pltpu.CompilerParams(collective_id=collective, has_side_effects=True)
    return pltpu.CompilerParams(
        collective_id=collective, has_side_effects=True, vmem_limit_bytes=limit
    )


class Gather:
    def __init__(self, begin, x, o, me):
        self.begin, self.x, self.o, self.me = begin, x, o, me
        self.place = lax.rem(me, TEAM)
        self.half = x.shape[0] // 2

    def part(self, ref, which):
        return ref.at[pl.ds(which * self.half, self.half)]

    def first(self, which, mask):
        target = self.part(self.o.at[self.place], which)
        return self.begin(self.part(self.x, which), target, flipped(self.me, mask))

    def relay(self, origin, which, mask):
        ref = self.part(self.o.at[flipped(self.place, origin)], which)
        return self.begin(ref, ref, flipped(self.me, mask))

    def start(self):
        self.x0, self.y1 = self.first(0, 2), self.first(1, 4)
        self.x1, self.y0 = self.first(1, 2), self.first(0, 4)
        self.late = [self.first(0, 1), self.first(1, 1)]

    def forward(self):
        self.x0.wait_recv()
        self.d0 = self.relay(2, 0, 4)
        self.y1.wait_recv()
        self.d1 = self.relay(4, 1, 2)
        self.late += [self.relay(2, 0, 1), self.relay(4, 1, 1)]

    def across(self):
        self.x1.wait_recv()
        self.late.append(self.relay(2, 1, 1))
        self.y0.wait_recv()
        self.late.append(self.relay(4, 0, 1))

    def diagonal(self):
        self.d0.wait_recv()
        self.late.append(self.relay(6, 0, 1))
        self.d1.wait_recv()
        self.late.append(self.relay(6, 1, 1))

    def arrive(self):
        for copy in self.late:
            copy.wait_recv()


class Sender:
    def __init__(self, send, receive):
        self.send, self.receive, self.count, self.started = send, receive, 0, []

    def take(self):
        self.count += 1
        return self.count - 1

    def __call__(self, source, target, device):
        k = self.take()
        copy = remote(source, target, self.send.at[k], self.receive.at[k], device)
        copy.start()
        self.started.append(copy)
        return copy

    def finish(self):
        for copy in self.started:
            copy.wait_send()


TILE = 512
STRIP = 16


class TeamSum:
    def __init__(self, sender, me, out, buffers, lefts, rights, turned):
        self.sender, self.me, self.out = sender, me, out
        self.mix, self.from_core, self.from_x, self.from_y = buffers
        self.lefts, self.rights, self.turned = lefts, rights, turned
        place = lax.rem(me, TEAM)
        self.core = lax.rem(place, 2)
        self.rows, self.width = out.shape
        self.half = self.rows // 2
        self.chips = [lax.div(flipped(place, mask), 2) for mask in (6, 2, 4, 0)]
        self.across = []

    def product(self, j):
        @pl.loop(0, self.width // TILE)
        def _(t):
            at = pl.ds(pl.multiple_of(t * TILE, TILE), TILE)
            value = 0.0
            for left, right in zip(self.lefts, self.rights):
                both = left[pl.ds(2 * self.chips[j], 2)].reshape(2 * self.rows, left.shape[2])
                if self.turned:
                    value = value + dot_last(both, right[at, :])
                else:
                    value = value + simple_product(both, right[:, at])
            self.mix[j, :, :, at] = value.astype(bf16).reshape(2, self.rows, TILE)

        self.across.append(
            self.sender(self.mix.at[j, 1 - self.core], self.from_core.at[j], flipped(self.me, 1))
        )

    def combine(self, j):
        self.across[j].wait_recv()

        @pl.loop(0, self.rows // STRIP)
        def _(i):
            at = pl.ds(i * STRIP, STRIP)
            self.mix[j, self.core, at, :] = (
                self.mix[j, self.core, at, :].astype(f32) + self.from_core[j, at, :].astype(f32)
            ).astype(bf16)

    def begin(self, j, which, ref, slot, mask):
        source = self.mix.at[j, self.core, pl.ds(which * self.half, self.half)]
        return self.sender(source, ref.at[slot], flipped(self.me, mask))

    def add_relayed(self, j, which, ref):
        @pl.loop(0, self.half // STRIP)
        def _(i):
            at = pl.ds(which * self.half + i * STRIP, STRIP)
            self.mix[j, self.core, at, :] = (
                self.mix[j, self.core, at, :].astype(f32)
                + ref[0, pl.ds(i * STRIP, STRIP), :].astype(f32)
            ).astype(bf16)

    def start(self):
        self.product(0)
        self.product(1)
        self.combine(0)
        self.d_x = self.begin(0, 0, self.from_x, 0, 2)
        self.d_y = self.begin(0, 1, self.from_y, 0, 4)
        self.product(2)
        self.combine(1)
        self.x_0 = self.begin(1, 0, self.from_x, 1, 2)
        self.combine(2)
        self.y_1 = self.begin(2, 1, self.from_y, 1, 4)

    def own(self):
        self.product(3)

    def relay(self):
        self.d_x.wait_recv()
        self.add_relayed(2, 0, self.from_x)
        self.y_0 = self.begin(2, 0, self.from_y, 2, 4)
        self.d_y.wait_recv()
        self.add_relayed(1, 1, self.from_y)
        self.x_1 = self.begin(1, 1, self.from_x, 2, 2)

    def gather_half(self, which, slot_x, slot_y):
        @pl.loop(0, self.half // STRIP)
        def _(i):
            at = pl.ds(which * self.half + i * STRIP, STRIP)
            here = pl.ds(i * STRIP, STRIP)
            self.out[at, :] = (
                self.mix[3, self.core, at, :].astype(f32) + self.from_core[3, at, :].astype(f32)
            ) + (
                self.from_x[slot_x, here, :].astype(f32) + self.from_y[slot_y, here, :].astype(f32)
            )

    def finish(self):
        self.across[3].wait_recv()
        self.x_0.wait_recv()
        self.y_0.wait_recv()
        self.gather_half(0, 1, 2)
        self.y_1.wait_recv()
        self.x_1.wait_recv()
        self.gather_half(1, 2, 1)


SUM_COPIES = 10


def sum_buffers(rows, width):
    return [
        pltpu.VMEM((4, 2, rows, width), bf16),
        pltpu.VMEM((4, rows, width), bf16),
        pltpu.VMEM((3, rows // 2, width), bf16),
        pltpu.VMEM((3, rows // 2, width), bf16),
    ]


class Loader:
    def __init__(self, sems):
        self.sems, self.copies = sems, []

    def __call__(self, source, target):
        copy = pltpu.make_async_copy(source, target, self.sems.at[len(self.copies)])
        copy.start()
        self.copies.append(copy)
        return copy

    def wait(self):
        for copy in self.copies:
            copy.wait()


def rows_of(ref, k, rows):
    return ref.at[pl.ds(k * rows, rows)]


def turned_product(left, right, out, part, parts):
    blocks, rows, units = left.shape
    width = right.shape[2]
    tiles = width // TILE
    flat = left[...].reshape(blocks * rows, units)

    @pl.loop(part * tiles // parts, (part + 1) * tiles // parts)
    def _(t):
        at = pl.ds(pl.multiple_of(t * TILE, TILE), TILE)
        value = dot_first(flat, right[:, :, at].reshape(blocks * rows, TILE))
        out[:, at] = value.astype(bf16)


def turned_rows(left, right, out, part, parts):
    blocks, rows, width = left.shape
    tiles = width // TILE
    flat = right[...].reshape(blocks * rows, right.shape[2])

    @pl.loop(part * tiles // parts, (part + 1) * tiles // parts)
    def _(t):
        at = pl.ds(pl.multiple_of(t * TILE, TILE), TILE)
        value = dot_first(left[:, :, at].reshape(blocks * rows, TILE), flat)
        out[at, :] = value.astype(bf16)


def sum_kernel(left, right, out, *rest):
    buffers, (left_here, right_here, send, receive, own) = rest[:4], rest[4:]
    me = lax.axis_index("fsdp")
    loader = Loader(own)
    loader(right, right_here)
    loader(left, left_here)
    greet(me, (1, 2, 4))
    loader.wait()
    sender = Sender(send, receive)
    total = TeamSum(sender, me, out, buffers, [left_here], [right_here], False)
    total.start()
    total.own()
    total.relay()
    total.finish()
    sender.finish()


def team_sum(left, right, collective):
    _, rows, depth = left.shape
    width = right.shape[1]
    anywhere = pl.BlockSpec(memory_space=pl.ANY)
    return pl.pallas_call(
        sum_kernel,
        out_shape=jax.ShapeDtypeStruct((rows, width), f32),
        in_specs=[anywhere, anywhere],
        out_specs=pl.BlockSpec(memory_space=pltpu.VMEM),
        scratch_shapes=[
            *sum_buffers(rows, width),
            pltpu.VMEM(left.shape, bf16),
            pltpu.VMEM(right.shape, bf16),
            pltpu.SemaphoreType.DMA((SUM_COPIES,)),
            pltpu.SemaphoreType.DMA((SUM_COPIES,)),
            pltpu.SemaphoreType.DMA((2,)),
        ],
        compiler_params=params(collective, LIMIT),
        cost_estimate=pl.CostEstimate(
            flops=2 * TEAM * rows * depth * width,
            bytes_accessed=2 * TEAM * rows * depth + 2 * depth * width + 4 * rows * width,
            transcendentals=0,
        ),
    )(left, right)


def feed_back_kernel(parts, two, *refs):
    grads, weights, refs = refs[:parts], refs[parts : 2 * parts], refs[2 * parts :]
    out, weight_out, buffers, refs = refs[0], refs[1], refs[2:6], refs[6:]
    grads_here, weights_here = refs[:parts], refs[parts : 2 * parts]
    two_here, send, receive, own = refs[2 * parts :]
    me = lax.axis_index("fsdp")
    loader = Loader(own)
    for source, target in zip((*grads, *weights), (*grads_here, *weights_here)):
        loader(source, target)
    greet(me, (1, 2, 4))
    loader.wait()
    loader(two, two_here)
    sender = Sender(send, receive)
    total = TeamSum(sender, me, out, buffers, grads_here, weights_here, True)
    total.start()
    loader.copies[-1].wait()
    total.relay()
    total.own()
    turned_rows(two_here, grads_here[-1], weight_out, 0, 1)
    total.finish()
    sender.finish()


def feed_back(two, grads, weights, collective):
    _, rows, width = two.shape
    parts, units = len(grads), grads[0].shape[2]
    anywhere = pl.BlockSpec(memory_space=pl.ANY)
    vmem = pl.BlockSpec(memory_space=pltpu.VMEM)
    like = jax.ShapeDtypeStruct
    return pl.pallas_call(
        functools.partial(feed_back_kernel, parts),
        out_shape=(like((rows, width), f32), like((width, units), bf16)),
        in_specs=[anywhere] * (1 + 2 * parts),
        out_specs=(vmem, vmem),
        scratch_shapes=[
            *sum_buffers(rows, width),
            *(pltpu.VMEM(x.shape, bf16) for x in (*grads, *weights, two)),
            pltpu.SemaphoreType.DMA((SUM_COPIES,)),
            pltpu.SemaphoreType.DMA((SUM_COPIES,)),
            pltpu.SemaphoreType.DMA((2 * parts + 1,)),
        ],
        compiler_params=params(collective, LIMIT),
        cost_estimate=pl.CostEstimate(
            flops=2 * TEAM * rows * units * width * (parts + 1),
            bytes_accessed=2 * TEAM * rows * (units * parts + width),
            transcendentals=0,
        ),
    )(two, *grads, *weights)


def gather_down_kernel(parts, x, cot, *refs):
    acts, refs = refs[:parts], refs[parts:]
    o_ref, down_out, refs = refs[0], refs[1], refs[2:]
    acts_here, (cot_here, send, receive, own) = refs[:parts], refs[parts:]
    me = lax.axis_index("fsdp")
    loader = Loader(own)
    loader(x, o_ref.at[lax.rem(me, TEAM)])
    loader(cot, cot_here)
    for source, target in zip(acts, acts_here):
        loader(source, target)
    greet(me, (1, 2, 4))
    sender = Sender(send, receive)
    moves = Gather(sender, x, o_ref, me)
    units = acts_here[0].shape[2]

    def work(k):
        turned_product(
            acts_here[k // 2], cot_here, rows_of(down_out, k // 2, units), k % 2, 2
        )

    moves.start()
    loader.wait()
    work(0)
    moves.forward()
    work(1)
    moves.across()
    if parts > 1:
        work(2)
    moves.diagonal()
    if parts > 1:
        work(3)
    moves.arrive()
    sender.finish()


def gather_down(x, cot, acts, collective):
    rows, width = x.shape
    parts, units = len(acts), acts[0].shape[2]
    anywhere = pl.BlockSpec(memory_space=pl.ANY)
    vmem = pl.BlockSpec(memory_space=pltpu.VMEM)
    like = jax.ShapeDtypeStruct
    return pl.pallas_call(
        functools.partial(gather_down_kernel, parts),
        out_shape=(like((TEAM, rows, width), x.dtype), like((parts * units, width), bf16)),
        in_specs=[vmem, anywhere] + [anywhere] * parts,
        out_specs=(anywhere, vmem),
        scratch_shapes=[
            *(pltpu.VMEM(a.shape, bf16) for a in acts),
            pltpu.VMEM(cot.shape, bf16),
            pltpu.SemaphoreType.DMA((14,)),
            pltpu.SemaphoreType.DMA((14,)),
            pltpu.SemaphoreType.DMA((2 + parts,)),
        ],
        compiler_params=params(collective, LIMIT),
        cost_estimate=pl.CostEstimate(
            flops=2 * TEAM * rows * width * units * parts,
            bytes_accessed=6 * TEAM * rows * width,
            transcendentals=0,
        ),
    )(x, cot, *acts)


def last_sums_kernel(planes, parts, grad_qkv, qkv_weight, down, *refs):
    acts, units, refs = refs[:parts], refs[parts : 2 * parts], refs[2 * parts :]
    grad_normed, layer, gate, up, refs = *refs[:4], refs[4:]
    first, second, refs = refs[:4], refs[4:8], refs[8:]
    acts_here, downs_here, refs = refs[:parts], refs[parts : 2 * parts], refs[2 * parts :]
    grad_here, weight_here, landed, send, receive, own = refs
    me = lax.axis_index("fsdp")
    place = lax.rem(me, TEAM)
    loader = Loader(own)
    loader(grad_qkv, grad_here)
    loader(qkv_weight, weight_here)
    for k in range(parts):
        loader(units[k].at[place], landed.at[k, place])
        loader(acts[k], acts_here[k])
        loader(rows_of(down, k, downs_here[k].shape[0]), downs_here[k])
    greet(me, range(1, TEAM))
    sender = Sender(send, receive)
    moves = [
        sender(units[k].at[flipped(place, m)], landed.at[k, place], flipped(me, m))
        for k in range(parts)
        for m in SWAP_ORDER
    ]
    loader.wait()
    one = TeamSum(sender, me, grad_normed, first, [grad_here], [weight_here], True)
    two = TeamSum(sender, me, layer, second, acts_here, downs_here, False)
    one.start()
    one.own()
    two.start()
    one.relay()
    two.own()
    two.relay()
    for copy in moves:
        copy.wait_recv()
    block = gate.shape[1] // (planes * TEAM)
    some = planes // parts
    span = TEAM * block
    for j, ref in enumerate((gate, up)):
        for g in range(planes):
            at = (j * some + g % some) * block
            ref[:, g * span : (g + 1) * span] = jnp.concatenate(
                [landed[g // some, q, :, at : at + block] for q in range(TEAM)], axis=1
            )
    one.finish()
    two.finish()
    sender.finish()


def last_sums(grad_qkv, qkv_weight, acts, down, units, planes, collective):
    _, rows, depth = grad_qkv.shape
    width = qkv_weight.shape[0]
    parts = len(acts)
    anywhere = pl.BlockSpec(memory_space=pl.ANY)
    vmem = pl.BlockSpec(memory_space=pltpu.VMEM)
    like = jax.ShapeDtypeStruct
    _, own_rows, some = units[0].shape
    links = 2 * SUM_COPIES + (TEAM - 1) * parts
    home = like((own_rows, TEAM * parts * some // 2), bf16)
    return pl.pallas_call(
        functools.partial(last_sums_kernel, planes, parts),
        out_shape=(like((rows, width), f32),) * 2 + (home,) * 2,
        in_specs=[anywhere] * (3 + 2 * parts),
        out_specs=(vmem,) * 4,
        scratch_shapes=[
            *sum_buffers(rows, width),
            *sum_buffers(rows, width),
            *(pltpu.VMEM(a.shape, bf16) for a in acts),
            *(pltpu.VMEM((a.shape[2], width), bf16) for a in acts),
            pltpu.VMEM(grad_qkv.shape, bf16),
            pltpu.VMEM(qkv_weight.shape, bf16),
            pltpu.VMEM((parts, *units[0].shape), bf16),
            pltpu.SemaphoreType.DMA((links,)),
            pltpu.SemaphoreType.DMA((links,)),
            pltpu.SemaphoreType.DMA((2 + 3 * parts,)),
        ],
        compiler_params=params(collective, LIMIT),
        cost_estimate=pl.CostEstimate(
            flops=2 * TEAM * rows * width * (depth + sum(a.shape[2] for a in acts)),
            bytes_accessed=4 * TEAM * rows * depth,
            transcendentals=0,
        ),
    )(grad_qkv, qkv_weight, down, *acts, *units)


class Line:
    def __init__(self, sender, ref, planes, me):
        self.sender, self.ref, self.planes = sender, ref, planes
        self.plane, self.place = lax.div(me, TEAM), lax.rem(me, TEAM)
        self.flows = [(sign, [sender.take() for _ in range(planes - 1)]) for sign in (1, -1)]

    def passing(self, step, sign, ks, source):
        block = jnp.clip(source, 0, self.planes - 1)
        beyond = jnp.clip(self.plane + sign, 0, self.planes - 1) * TEAM + self.place
        ref, k = self.ref.at[block], ks[step]
        return remote(ref, ref, self.sender.send.at[k], self.sender.receive.at[k], beyond)

    def goes(self, step, sign):
        source, onward = self.plane - sign * step, self.plane + sign
        last = self.planes - 1
        return (source >= 0) & (source <= last) & (onward >= 0) & (onward <= last)

    def start(self, step):
        for sign, ks in self.flows:
            going = self.passing(step, sign, ks, self.plane - sign * step)
            pl.when(self.goes(step, sign))(going.start)

    def arrive(self, step):
        for sign, ks in self.flows:
            source = self.plane - sign * (step + 1)
            coming = self.passing(step, sign, ks, source)
            pl.when((source >= 0) & (source <= self.planes - 1))(coming.wait_recv)

    def sent(self, step):
        for sign, ks in self.flows:
            going = self.passing(step, sign, ks, self.plane - sign * step)
            pl.when(self.goes(step, sign))(going.wait_send)


SWAP_ORDER = (6, 7, 2, 3, 4, 5, 1)


def open_kernel(
    planes, parts, query_in, key_in, value_in, output_in, tokens_in, gate_in, up_in, *refs
):
    smalls, refs = refs[:5], refs[5:]
    gate_up, refs = refs[:parts], refs[parts:]
    qkv, output_raw, output, tokens, *gain_refs, numbers = refs[:9]
    small_in, small, sorted_units, send, receive, own = refs[9:]
    slots, sequence = smalls[4].shape
    small_in[...] = jnp.zeros_like(small_in)
    for k, ref in enumerate(smalls):
        small_in[k : k + ref.shape[0], : ref.shape[1]] = ref[...].astype(f32)
    me = lax.axis_index("fsdp")
    place = lax.rem(me, TEAM)
    plane = lax.div(me, TEAM)
    team = me - place
    others = [lax.rem(me + TEAM * k, planes * TEAM) for k in range(1, planes)]
    sender = Sender(send, receive)
    keeps = []

    def keep(source, target):
        copy = pltpu.make_async_copy(source, target, own.at[len(keeps)])
        copy.start()
        keeps.append(copy)

    qkv_parts, at = [], 0
    for ref in (query_in, key_in, value_in):
        part = ref.shape[1] // TEAM
        qkv_parts.append((ref, part, qkv.at[plane, place, :, pl.ds(at, part)]))
        at += part

    def columns(ref, part, target):
        return ref.at[:, pl.ds(pl.multiple_of(target * part, part), part)]

    for ref, part, target in qkv_parts:
        keep(columns(ref, part, place), target)
    keep(small_in, small.at[me])
    keep(tokens_in, tokens.at[place])
    keep(output_in, output_raw.at[plane])
    greet(me, range(1, TEAM), others)

    qkv_line = Line(sender, qkv, planes, me)
    out_line = Line(sender, output_raw, planes, me)
    rows_tokens = Gather(sender, tokens_in, tokens, me)
    spread_send = [sender.take() for _ in range(planes)]
    spread_own = len(keeps)

    def outgoing(k):
        number = TEAM * k + place
        partner, there = lax.div(number, planes), lax.rem(number, planes)
        s, r = send.at[spread_send[0] + k], receive.at[spread_send[0] + there]
        over = remote(output_raw.at[k], output.at[there], s, r, team + partner)
        here = pltpu.make_async_copy(output_raw.at[k], output.at[there], own.at[spread_own + k])
        return partner, over, here

    def incoming(k):
        partner = lax.rem(planes * place + k, TEAM)
        s, r = send.at[spread_send[k]], receive.at[spread_send[k]]
        return partner, remote(output_raw.at[k], output.at[k], s, r, team + partner)

    def spread_one(k, inside):
        partner, over, here = outgoing(jnp.clip(k, 0, planes - 1))
        pl.when(inside & (partner != place))(over.start)
        pl.when(inside & (partner == place))(here.start)

    def step_out(step):
        out_line.arrive(step)
        if step < planes - 2:
            out_line.start(step + 1)
        spread_one(plane - step - 1, plane - step - 1 >= 0)
        spread_one(plane + step + 1, plane + step + 1 <= planes - 1)

    swaps = [
        sender(columns(ref, part, flipped(place, m)), target, flipped(me, m))
        for m in SWAP_ORDER
        for ref, part, target in qkv_parts
    ]
    near = [sender(small_in, small.at[me], flipped(me, m)) for m in SWAP_ORDER]
    keeps[-1].wait()
    out_line.start(0)
    block = gate_in.shape[1] // (planes * TEAM)
    some = planes // parts
    units = some * block
    for k in range(parts):
        for q in range(TEAM):
            for j, ref in enumerate((gate_in, up_in)):
                starts = [(TEAM * g + q) * block for g in range(k * some, (k + 1) * some)]
                sorted_units[k, q, :, j * units : (j + 1) * units] = jnp.concatenate(
                    [ref[:, at : at + block] for at in starts], axis=1
                )
    for copy in swaps:
        copy.wait_recv()
    for copy in keeps[:3]:
        copy.wait()
    qkv_line.start(0)
    rows_tokens.start()
    moves = [
        sender(sorted_units.at[k, flipped(place, m)], gate_up[k].at[place], flipped(me, m))
        for k in range(parts)
        for m in SWAP_ORDER
    ]
    kept_units = [
        pltpu.make_async_copy(
            sorted_units.at[k, place], gate_up[k].at[place], own.at[spread_own + planes + k]
        )
        for k in range(parts)
    ]
    for copy in kept_units:
        copy.start()
    spread_one(plane, True)
    rows_tokens.forward()
    step_out(0)
    for copy in near:
        copy.wait_recv()
    keeps[3].wait()
    shared = small.at[pl.ds(team, TEAM)]
    far = [sender(shared, shared, other) for other in others]
    rows_tokens.across()
    for step in range(planes - 1):
        qkv_line.arrive(step)
        if step < planes - 2:
            qkv_line.start(step + 1)
            step_out(step + 1)
        if step == 0:
            rows_tokens.diagonal()
        if step == 1:
            for copy in far:
                copy.wait_recv()
            for k, ref in enumerate(gain_refs):
                part = smalls[k].shape[1]
                ref[...] = jnp.concatenate(
                    [small[i, k : k + 1, :part] for i in range(planes * TEAM)], axis=1
                )
            per_step = STEP // sequence
            for i in range(numbers.shape[0]):
                pieces = []
                for m in range(i * per_step, (i + 1) * per_step):
                    row = 4 + m % slots
                    pieces.append(small[team + m // slots, row : row + 1, :sequence] + 64.0 * m)
                numbers[i] = jnp.concatenate(pieces, axis=1)
    rows_tokens.arrive()
    for copy in moves:
        copy.wait_recv()
    for copy in kept_units:
        copy.wait()
    for k in range(planes):
        partner, over, here = outgoing(k)
        pl.when(partner != place)(over.wait_send)
        pl.when(partner == place)(here.wait)
        partner, arriving = incoming(k)
        pl.when(partner != place)(arriving.wait_recv)
    for step in range(planes - 1):
        qkv_line.sent(step)
        out_line.sent(step)
    sender.finish()
    for copy in keeps[4:-1]:
        copy.wait()


def opening(query, key, value, output, tokens, gate, up, smalls, planes, parts, collective):
    links = 28 + 4 * (planes - 1) + 14 + planes - 1 + planes + parts * (TEAM - 1)
    anywhere = pl.BlockSpec(memory_space=pl.ANY)
    vmem = pl.BlockSpec(memory_space=pltpu.VMEM)
    like = jax.ShapeDtypeStruct
    rows = query.shape[0]
    width = (query.shape[1] + key.shape[1] + value.shape[1]) // TEAM
    units = (TEAM, rows, 2 * gate.shape[1] // TEAM // parts)
    devices = planes * TEAM
    return pl.pallas_call(
        functools.partial(open_kernel, planes, parts),
        out_shape=(
            *((like(units, bf16),) * parts),
            like((planes, TEAM, rows, width), bf16),
            like((planes, *output.shape), bf16),
            like((planes, *output.shape), bf16),
            like((TEAM, *tokens.shape), bf16),
            *(like((1, devices * x.shape[1]), f32) for x in smalls[:4]),
            like((TEAM * tokens.shape[0] // STEP, 1, STEP), f32),
        ),
        in_specs=[vmem] * 12,
        out_specs=(anywhere,) * (4 + parts) + (vmem,) * 5,
        scratch_shapes=[
            pltpu.VMEM((8, 128), f32),
            pltpu.VMEM((devices, 8, 128), f32),
            pltpu.VMEM((parts, *units), bf16),
            pltpu.SemaphoreType.DMA((links,)),
            pltpu.SemaphoreType.DMA((links,)),
            pltpu.SemaphoreType.DMA((6 + planes + parts,)),
        ],
        compiler_params=params(collective, LIMIT),
    )(query, key, value, output, tokens, gate, up, *smalls)


def close_kernel(planes, x_ref, gains, *refs):
    query_ref, key_ref, value_ref, output_ref, gain_ref, *refs = refs
    landed, mine, near_in, mid, far_in, send, receive, own = refs
    me = lax.axis_index("fsdp")
    place = lax.rem(me, TEAM)
    plane = lax.div(me, TEAM)
    others = [lax.rem(me + TEAM * k, planes * TEAM) for k in range(1, planes)]
    rows = landed.shape[1]

    def part(target):
        return x_ref.at[pl.ds(pl.multiple_of(target * rows, rows), rows)]

    keep = pltpu.make_async_copy(part(place), landed.at[place], own.at[0])
    keep.start()
    keep_mine = pltpu.make_async_copy(
        x_ref.at[pl.ds(TEAM * rows, mine.shape[0])], mine, own.at[1]
    )
    keep_mine.start()
    greet(me, range(1, TEAM), others)
    sender = Sender(send, receive)
    near = [
        sender(gains.at[flipped(place, m)], near_in.at[m - 1], flipped(me, m)) for m in SWAP_ORDER
    ]
    moves = [
        sender(part(flipped(place, m)), landed.at[place], flipped(me, m)) for m in SWAP_ORDER
    ]
    for copy in near:
        copy.wait_recv()
    summed = gains[place]
    for mask in range(1, TEAM):
        summed = summed + near_in[mask - 1]
    mid[...] = summed
    far = [
        sender(mid.at[lax.rem(plane + k + 1, planes)], far_in.at[k], other)
        for k, other in enumerate(others)
    ]
    keep_mine.wait()
    width = mine.shape[1]
    for c in range(output_ref.shape[1] // width):
        output_ref[:, c * width : (c + 1) * width] = mine[c * rows : (c + 1) * rows]
    for copy in moves:
        copy.wait_recv()
    keep.wait()
    at = 0
    for ref in (query_ref, key_ref, value_ref):
        part_width = ref.shape[1] // TEAM
        for q in range(TEAM):
            ref[:, q * part_width : (q + 1) * part_width] = landed[q, :, at : at + part_width]
        at += part_width
    for copy in far:
        copy.wait_recv()
    result = mid[plane]
    for k in range(planes - 1):
        result = result + far_in[k]
    gain_ref[...] = result
    sender.finish()


def closing(x, gains, rows, widths, planes, collective):
    links = 2 * (TEAM - 1) + planes - 1
    block = gains.shape[2:]
    vmem = pl.BlockSpec(memory_space=pltpu.VMEM)
    like = jax.ShapeDtypeStruct
    return pl.pallas_call(
        functools.partial(close_kernel, planes),
        out_shape=(*(like((rows, w), bf16) for w in widths), like(block, f32)),
        in_specs=[pl.BlockSpec(memory_space=pl.ANY), vmem],
        out_specs=(vmem,) * 5,
        scratch_shapes=[
            pltpu.VMEM((TEAM, rows, x.shape[1]), x.dtype),
            pltpu.VMEM((x.shape[0] - TEAM * rows, x.shape[1]), x.dtype),
            pltpu.VMEM((TEAM - 1, planes, *block), f32),
            pltpu.VMEM((planes, *block), f32),
            pltpu.VMEM((planes - 1, *block), f32),
            pltpu.SemaphoreType.DMA((links,)),
            pltpu.SemaphoreType.DMA((links,)),
            pltpu.SemaphoreType.DMA((2,)),
        ],
        compiler_params=params(collective, LIMIT),
    )(x, gains)


def visible_and_tables(ids_row, table):
    rows = ids_row.shape[1]
    row_at = lax.broadcasted_iota(jnp.int32, (rows, rows), 0)
    column_at = lax.broadcasted_iota(jnp.int32, (rows, rows), 1)
    ids_column = jnp.sum(jnp.where(row_at == column_at, ids_row, 0.0), axis=1, keepdims=True)
    visible = (ids_column == ids_row) & (column_at <= row_at)
    sequence = table.shape[0]
    place = jnp.sum(visible.astype(f32), axis=1, keepdims=True) - 1.0
    at = lax.broadcasted_iota(jnp.int32, (rows, sequence), 1).astype(f32)
    chosen = (at == place).astype(bf16)
    both = simple_product(chosen, table)
    width = 2 * HEAD_SIZE
    both = (both[:, :width] + both[:, width : 2 * width]) + both[:, 2 * width :]
    return visible, both[:, :HEAD_SIZE], both[:, HEAD_SIZE:]


def softmax(query, key, visible):
    scores = dot_last(query, key) * HEAD_SIZE ** (-0.5)
    scores = jnp.where(visible, scores, -1e30)
    expos = jnp.exp(scores - jnp.max(scores, axis=1, keepdims=True))
    return expos / jnp.sum(expos, axis=1, keepdims=True)


def attend_kernel(
    x_ref, gain, weight, ids_row, table, query_gain, key_gain,
    normed_ref, raw_ref, turned_ref, value_ref, context_ref,
):
    x = x_ref[...].astype(f32)
    scale = lax.rsqrt(jnp.mean(x * x, axis=1, keepdims=True) + epsilon)
    normed = (x * scale * gain[...]).astype(bf16)
    normed_ref[...] = normed
    projected = simple_product(normed, weight[...])
    visible, cosine, sine = visible_and_tables(ids_row[0], table[...])
    heads = context_ref.shape[1] // HEAD_SIZE
    raw_ref[...] = projected[:, : (heads + 1) * HEAD_SIZE]
    value = projected[:, (heads + 1) * HEAD_SIZE :].astype(bf16)
    value_ref[...] = value
    turned = []
    for h in range(heads + 1):
        raw = projected[:, h * HEAD_SIZE : (h + 1) * HEAD_SIZE]
        head_gain = query_gain if h < heads else key_gain
        y = raw * lax.rsqrt(jnp.mean(raw * raw, axis=1, keepdims=True) + epsilon) * head_gain[...]
        y = y * cosine + pltpu.roll(y, HEAD_SIZE // 2, 1) * sine
        turned.append(y.astype(bf16))
        turned_ref[:, h * HEAD_SIZE : (h + 1) * HEAD_SIZE] = turned[-1]
    for h in range(heads):
        probs = softmax(turned[h], turned[heads], visible).astype(bf16)
        context = simple_product(probs, value)
        context_ref[:, h * HEAD_SIZE : (h + 1) * HEAD_SIZE] = context.astype(bf16)


def by_step(*shape):
    return pl.BlockSpec(shape, lambda i: (i, *(0 for _ in shape[1:])))


def fixed(*shape):
    return pl.BlockSpec(shape, lambda i: tuple(0 for _ in shape))


def attend(x, gain, weight, ids, table, query_gain, key_gain):
    rows, width = x.shape
    out = weight.shape[1]
    like = jax.ShapeDtypeStruct
    heads = out - 2 * HEAD_SIZE
    return pl.pallas_call(
        attend_kernel,
        grid=(rows // STEP,),
        out_shape=(
            like((rows, width), bf16),
            like((rows, heads + HEAD_SIZE), f32),
            like((rows, heads + HEAD_SIZE), bf16),
            like((rows, HEAD_SIZE), bf16),
            like((rows, heads), bf16),
        ),
        in_specs=[
            by_step(STEP, width),
            fixed(1, width),
            fixed(width, out),
            by_step(1, 1, STEP),
            fixed(*table.shape),
            fixed(1, HEAD_SIZE),
            fixed(1, HEAD_SIZE),
        ],
        out_specs=(
            by_step(STEP, width),
            by_step(STEP, heads + HEAD_SIZE),
            by_step(STEP, heads + HEAD_SIZE),
            by_step(STEP, HEAD_SIZE),
            by_step(STEP, heads),
        ),
        compiler_params=pltpu.CompilerParams(vmem_limit_bytes=LIMIT),
        cost_estimate=pl.CostEstimate(
            flops=2 * rows * width * out, bytes_accessed=8 * rows * width, transcendentals=0
        ),
    )(x, gain, weight, ids, table, query_gain, key_gain)


def attend_back_kernel(planes, grad_in, out_weight, context, raw_in, turned_in, value_in, normed_in,
    ids_row, table, query_gain, key_gain, grad_raw_ref, merged, grad_gains_ref,
    grad_ref, raw_ref, turned_ref, value_ref, normed_ref, out_sum, weight_sum, send, receive, own,
):
    me = lax.axis_index("fsdp")
    place = lax.rem(me, TEAM)
    team = me - place
    loader = Loader(own)
    loader(grad_in, grad_ref)
    for source, target in (
        (raw_in, raw_ref), (turned_in, turned_ref), (value_in, value_ref), (normed_in, normed_ref)
    ):
        loader(source, target)
    greet(me, range(1, TEAM))
    loader.copies[0].wait()

    total, width = grad_ref.shape
    heads = context.shape[1] // HEAD_SIZE
    out = weight_sum.shape[1]
    rows, block = weight_sum.shape[0] // planes, out_sum.shape[0] // planes
    cuts = width // out

    def source(k, c):
        return out_sum.at[pl.ds(k * block, block), pl.ds(c * out, out)]

    def target(k, c):
        return merged.at[k, pl.ds(rows + c * block, block)]

    def outgoing(k, c):
        number = planes * place + k
        partner, there = lax.rem(number, TEAM), lax.div(number, TEAM)
        s, r = send.at[k * cuts + c], receive.at[there * cuts + c]
        over = remote(source(k, c), target(there, c), s, r, team + partner)
        here = pltpu.make_async_copy(source(k, c), target(there, c), own.at[5 + k * cuts + c])
        return partner, over, here

    def incoming(k, c):
        partner = lax.div(TEAM * k + place, planes)
        s, r = send.at[k * cuts + c], receive.at[k * cuts + c]
        return partner, remote(source(k, c), target(k, c), s, r, team + partner)

    for c in range(cuts):
        at = slice(c * out, (c + 1) * out)
        out_sum[:, at] = dot_first(context[...], grad_ref[:, at]).astype(bf16)
        for k in range(planes):
            partner, over, here = outgoing(k, c)
            pl.when(partner != place)(over.start)
            pl.when(partner == place)(here.start)

    grad_gains_ref[...] = jnp.zeros_like(grad_gains_ref)
    for copy in loader.copies[1:]:
        copy.wait()

    @pl.loop(0, total // STEP)
    def _(i):
        here = pl.ds(pl.multiple_of(i * STEP, STEP), STEP)
        grad_context = dot_last(grad_ref[here, :], out_weight[...]).astype(bf16)
        visible, cosine, sine = visible_and_tables(ids_row[i], table[...])
        value = value_ref[here, :]
        key = turned_ref[here, heads * HEAD_SIZE :]
        grads = []
        grad_value = 0.0
        grad_key = 0.0
        for h in range(heads):
            at = slice(h * HEAD_SIZE, (h + 1) * HEAD_SIZE)
            query = turned_ref[here, at]
            probs = softmax(query, key, visible)
            grad_value = grad_value + dot_first(probs.astype(bf16), grad_context[:, at])
            grad_probs = dot_last(grad_context[:, at], value)
            inner = jnp.sum(probs * grad_probs, axis=1, keepdims=True)
            grad_scores = (probs * (grad_probs - inner)).astype(bf16)
            grads.append(simple_product(grad_scores, key) * HEAD_SIZE ** (-0.5))
            grad_key = grad_key + dot_first(grad_scores, query) * HEAD_SIZE ** (-0.5)
        grads.append(grad_key)
        parts = []
        for h in range(heads + 1):
            raw = raw_ref[here, h * HEAD_SIZE : (h + 1) * HEAD_SIZE]
            head_gain = query_gain[...] if h < heads else key_gain[...]
            scale = lax.rsqrt(jnp.mean(raw * raw, axis=1, keepdims=True) + epsilon)
            turned = grads[h] * cosine + pltpu.roll(grads[h] * sine, HEAD_SIZE // 2, 1)
            row = 0 if h < heads else 1
            grad_gains_ref[row : row + 1, :] += jnp.sum(turned * raw * scale, axis=0, keepdims=True)
            turned = turned * head_gain
            mean = jnp.mean(turned * raw, axis=1, keepdims=True)
            parts.append((turned * scale - raw * (scale * scale * scale * mean)).astype(bf16))
        parts.append(grad_value.astype(bf16))
        grad_raw_ref[here, :] = jnp.concatenate(parts, axis=1)

    @pl.loop(0, planes)
    def _(g):
        at = pl.ds(pl.multiple_of(g * rows, rows), rows)
        weight_sum[at, :] = dot_first(normed_ref[:, at], grad_raw_ref[...]).astype(bf16)

    homes = []
    for g in range(planes):
        copy = pltpu.make_async_copy(
            weight_sum.at[pl.ds(g * rows, rows)],
            merged.at[g, pl.ds(0, rows)],
            own.at[5 + planes * cuts + g],
        )
        copy.start()
        homes.append(copy)
    for k in range(planes):
        for c in range(cuts):
            partner, over, here = outgoing(k, c)
            pl.when(partner != place)(over.wait_send)
            pl.when(partner == place)(here.wait)
            partner, arriving = incoming(k, c)
            pl.when(partner != place)(arriving.wait_recv)
    for copy in homes:
        copy.wait()


def attend_back(
    grad, out_weight, context, raw, turned, value, normed, ids, table, query_gain, key_gain,
    planes, collective,
):
    rows, width = grad.shape
    heads = context.shape[1]
    out = heads + 2 * HEAD_SIZE
    merged = (planes, (width + heads * width // out) // planes, out)
    copies = planes * (width // out)
    anywhere = pl.BlockSpec(memory_space=pl.ANY)
    vmem = pl.BlockSpec(memory_space=pltpu.VMEM)
    like = jax.ShapeDtypeStruct
    return pl.pallas_call(
        functools.partial(attend_back_kernel, planes),
        out_shape=(like((rows, out), bf16), like(merged, bf16), like((8, HEAD_SIZE), f32)),
        in_specs=[anywhere, vmem, vmem] + [anywhere] * 4 + [vmem] * 4,
        out_specs=(vmem, anywhere, vmem),
        scratch_shapes=[
            *(pltpu.VMEM(x.shape, x.dtype) for x in (grad, raw, turned, value, normed)),
            pltpu.VMEM((heads, width), bf16),
            pltpu.VMEM((width, out), bf16),
            pltpu.SemaphoreType.DMA((copies,)),
            pltpu.SemaphoreType.DMA((copies,)),
            pltpu.SemaphoreType.DMA((5 + copies + planes,)),
        ],
        compiler_params=params(collective, LIMIT),
        cost_estimate=pl.CostEstimate(
            flops=2 * rows * width * (out + 2 * heads),
            bytes_accessed=8 * rows * width,
            transcendentals=0,
        ),
    )(grad, out_weight, context, raw, turned, value, normed, ids, table, query_gain, key_gain)


def hidden(two, weight):
    return simple_product(two, weight)


def hidden_grads(both, cot, down):
    units = both.shape[1] // 2
    gate, up = both[:, :units], both[:, units:]
    grad_act = dot_last(cot, down)
    sigma = 1.0 / (1.0 + jnp.exp(-gate))
    silu_gate = gate * sigma
    act = (silu_gate * up).astype(bf16)
    grad_gate = (grad_act * up * (sigma * (1.0 + gate * (1.0 - sigma)))).astype(bf16)
    grad_up = (grad_act * silu_gate).astype(bf16)
    return act, grad_gate, grad_up


def feed_kernel(
    two_in, cot_in, weight_in, down_in, two_out, cot_out, act, grad_both, grad_weight,
    two, cot, weight, down, both, weight_sum, send, receive, own,
):
    me = lax.axis_index("fsdp")
    place = lax.rem(me, TEAM)
    loader = Loader(own)
    loader(two_in, two.at[place])
    loader(cot_in, cot.at[place])
    loader(weight_in, weight)
    loader(rows_of(down_in, 0, down.shape[0]), down)
    greet(me, (1, 2, 4))
    sender = Sender(send, receive)
    rows_two = Gather(sender, two_in, two, me)
    rows_cot = Gather(sender, cot_in, cot, me)
    rows_two.start()
    rows_cot.start()
    rows, units = act.shape[1:]
    width = two.shape[2]
    weight_sum[...] = jnp.zeros_like(weight_sum)

    crossed = {0: (0, 1), 2: (2, 4), 4: (3, 5), 6: (6, 7)}

    def chip_rows(moves, mask, target):
        for k in crossed[mask]:
            moves.late[k].wait_recv()
        chip = pl.ds(2 * lax.div(flipped(place, mask), 2), 2)
        loader(moves.o.at[chip], target.at[chip])
        return chip, moves.o[chip].reshape(2 * rows, width)

    def forward(mask):
        _, flat = chip_rows(rows_two, mask, two_out)
        both[mask // 2] = simple_product(flat, weight[...])

    def backward(mask):
        chip, flat = chip_rows(rows_cot, mask, cot_out)
        a, grad_gate, grad_up = hidden_grads(both[mask // 2], flat, down[...])
        act[chip] = a.reshape(2, rows, units)
        grads = jnp.concatenate([grad_gate, grad_up], axis=1)
        grad_both[chip] = grads.reshape(2, rows, 2 * units)
        for t in range(width // TILE):
            at = slice(t * TILE, (t + 1) * TILE)
            left = two[chip, :, at].reshape(2 * rows, TILE)
            weight_sum[at, :] += dot_first(left, grads)

    rows_two.forward()
    rows_two.across()
    loader.wait()
    forward(0)
    backward(0)
    rows_cot.forward()
    forward(2)
    forward(4)
    rows_cot.across()
    backward(2)
    rows_two.diagonal()
    backward(4)
    forward(6)
    rows_cot.diagonal()
    backward(6)
    grad_weight[...] = weight_sum[...].astype(bf16)
    sender.finish()
    for copy in loader.copies[4:]:
        copy.wait()


def feed(two, cot, weight, down, collective):
    rows, width = two.shape
    units = weight.shape[1] // 2
    vmem = pl.BlockSpec(memory_space=pltpu.VMEM)
    anywhere = pl.BlockSpec(memory_space=pl.ANY)
    like = jax.ShapeDtypeStruct
    return pl.pallas_call(
        feed_kernel,
        out_shape=(
            like((TEAM, rows, width), bf16),
            like((TEAM, rows, width), bf16),
            like((TEAM, rows, units), bf16),
            like((TEAM, rows, 2 * units), bf16),
            like(weight.shape, bf16),
        ),
        in_specs=[anywhere] * 4,
        out_specs=(anywhere, anywhere, vmem, vmem, vmem),
        scratch_shapes=[
            pltpu.VMEM((TEAM, rows, width), bf16),
            pltpu.VMEM((TEAM, rows, width), bf16),
            pltpu.VMEM(weight.shape, bf16),
            pltpu.VMEM((units, width), bf16),
            pltpu.VMEM((TEAM // 2, 2 * rows, 2 * units), f32),
            pltpu.VMEM(weight.shape, f32),
            pltpu.SemaphoreType.DMA((28,)),
            pltpu.SemaphoreType.DMA((28,)),
            pltpu.SemaphoreType.DMA((12,)),
        ],
        compiler_params=params(collective, LIMIT),
        cost_estimate=pl.CostEstimate(
            flops=10 * TEAM * rows * width * units,
            bytes_accessed=8 * TEAM * rows * width,
            transcendentals=0,
        ),
    )(two, cot, weight, down)


def feed_rest_kernel(two, cot, weight, down, act, grad_both):
    blocks, rows, units = act.shape
    both = simple_product(two[...].reshape(blocks * rows, -1), weight[...])
    flat = cot[...].reshape(blocks * rows, -1)
    a, grad_gate, grad_up = hidden_grads(both, flat, down[...])
    act[...] = a.reshape(blocks, rows, units)
    grad_both[:, :, :units] = grad_gate.reshape(blocks, rows, units)
    grad_both[:, :, units:] = grad_up.reshape(blocks, rows, units)


def feed_rest(two, cot, weight, down, part):
    _, rows, width = two.shape
    units = weight.shape[1] // 2
    like = jax.ShapeDtypeStruct
    return pl.pallas_call(
        feed_rest_kernel,
        grid=(TEAM // 2,),
        out_shape=(like((TEAM, rows, units), bf16), like((TEAM, rows, 2 * units), bf16)),
        in_specs=[
            by_step(2, rows, width),
            by_step(2, rows, width),
            fixed(*weight.shape),
            pl.BlockSpec((units, width), lambda i: (part, 0)),
        ],
        out_specs=(by_step(2, rows, units), by_step(2, rows, 2 * units)),
        compiler_params=pltpu.CompilerParams(vmem_limit_bytes=LIMIT),
        cost_estimate=pl.CostEstimate(
            flops=6 * TEAM * rows * width * units,
            bytes_accessed=4 * TEAM * rows * width,
            transcendentals=0,
        ),
    )(two, cot, weight, down)


def local(
    devices,
    tokens,
    segments,
    micro_live,
    cotangent,
    w_query,
    key_weight,
    value_weight,
    w_output,
    attn_gain,
    query_norm_gain,
    key_gain,
    w_gate,
    w_up,
    w_down,
    mlp_gain,
):
    planes = devices // TEAM
    lines = [[place + TEAM * k for k in range(planes)] for place in range(TEAM)]
    slots, sequence = segments.shape
    token_count, width = tokens.shape
    groups = QUERY_HEADS // KEY_VALUE_HEADS
    rows = w_query.shape[0]
    parts = 2 if planes % 2 == 0 else 1
    team_rows = TEAM * token_count
    head_width = groups * HEAD_SIZE
    me = lax.axis_index("fsdp")
    plane = me // TEAM

    def gather_line(x):
        return lax.all_gather(x, "fsdp", axis=0, tiled=True, axis_index_groups=lines)

    def sum_line(x):
        return lax.psum_scatter(
            x, "fsdp", scatter_dimension=0, tiled=True, axis_index_groups=lines
        )

    slot_live = (lax.broadcasted_iota(jnp.int32, (slots, 1), 0) < micro_live[0]).astype(f32)
    row_live = jnp.broadcast_to(slot_live, (slots, sequence)).reshape(token_count, 1)
    cot_b = cotangent * row_live.astype(bf16)

    down_weight = gather_line(w_down)
    smalls = [x[None] for x in (attn_gain, mlp_gain, query_norm_gain, key_gain)] + [segments]
    opened = opening(
        w_query,
        key_weight,
        value_weight,
        w_output,
        tokens,
        w_gate,
        w_up,
        smalls,
        planes,
        parts,
        1,
    )
    unit_slices, opened = opened[:parts], opened[parts:]
    qkv_weight, _, output_weight, team_tokens = opened[:4]
    norm_gain, mlp_norm_gain, qgain, kgain, ids = opened[4:]
    mlp_norm_gain = mlp_norm_gain.reshape(width)
    qkv_weight = qkv_weight.reshape(width, -1)
    output_weight = output_weight.reshape(head_width, width)
    unit_weights = [gather_line(x.reshape(TEAM * rows, -1)) for x in unit_slices]
    table = jnp.asarray(rotation_tables(sequence))

    inputs = tokens.astype(f32)
    team_normed, raw, turned, value_b, context_b = attend(
        team_tokens.reshape(team_rows, width), norm_gain, qkv_weight, ids, table, qgain, kgain
    )
    middle = inputs + team_sum(
        context_b.reshape(TEAM, token_count, head_width), output_weight, 2
    )

    normed_two = root_mean_square_norm(middle, mlp_norm_gain).astype(bf16)
    team_two, team_cot, act, grad_both, first_units = feed(
        normed_two, cot_b, unit_weights[0], down_weight, 0
    )
    acts, grads_both, grad_units = [act], [grad_both], [first_units]
    for k in range(1, parts):
        act, grad_both = feed_rest(team_two, team_cot, unit_weights[k], down_weight, k)
        acts.append(act)
        grads_both.append(grad_both)
    grad_normed_two, last_units = feed_back(team_two, grads_both, unit_weights, 4)
    grad_units = [sum_line(g) for g in (*grad_units, last_units)[:parts]]
    _, pull_two = jax.vjp(root_mean_square_norm, middle, mlp_norm_gain)
    middle_part, grad_mgain = pull_two(grad_normed_two)
    grad_middle = cot_b.astype(f32) + middle_part
    team_grad, grad_down = gather_down(grad_middle.astype(bf16), team_cot, acts, 10)
    team_grad = team_grad.reshape(team_rows, width)
    grad_down = sum_line(grad_down)

    grad_qkv, grad_attention, grad_head_gains = attend_back(
        team_grad,
        output_weight,
        context_b,
        raw,
        turned,
        value_b,
        team_normed,
        ids,
        table,
        qgain,
        kgain,
        planes,
        6,
    )
    grad_attention = sum_line(grad_attention.reshape(-1, grad_attention.shape[2]))
    grad_normed, summed_out, grad_gate, grad_up = last_sums(
        grad_qkv.reshape(TEAM, token_count, -1),
        qkv_weight,
        acts,
        down_weight,
        [g.reshape(TEAM, rows, -1) for g in grad_units],
        planes,
        5,
    )
    grad_gate, grad_up = grad_gate.astype(f32), grad_up.astype(f32)
    _, pull_one = jax.vjp(root_mean_square_norm, inputs, norm_gain.reshape(width))
    input_part, grad_again = pull_one(grad_normed)
    grad_tokens = (grad_middle + input_part).astype(bf16)
    layer_out = (row_live * (middle + summed_out)).astype(bf16)

    def by_owner(vector):
        vector = vector.reshape(devices, -1)
        return jnp.pad(vector, ((0, 0), (0, 128 - vector.shape[1])))

    gains = jnp.stack(
        [by_owner(v) for v in (grad_again, grad_mgain, grad_head_gains[0], grad_head_gains[1])], axis=1
    )
    gains = jnp.pad(gains, ((0, 0), (0, 4), (0, 0)))
    gains = gains.reshape(planes, TEAM, 8, 128).transpose(1, 0, 2, 3)

    grad_attention, grad_gate, grad_up, layer_out, grad_tokens = lax.optimization_barrier(
        (grad_attention, grad_gate, grad_up, layer_out, grad_tokens)
    )
    grad_query, grad_key, grad_value_w, grad_output, gains = closing(
        grad_attention,
        gains,
        rows,
        (w_query.shape[1], key_weight.shape[1], value_weight.shape[1], width),
        planes,
        9,
    )
    attention_grads = tuple(
        g.astype(f32) for g in (grad_query, grad_key, grad_value_w, grad_output)
    )
    gains = (
        gains[0, : attn_gain.shape[0]],
        gains[2, : query_norm_gain.shape[0]],
        gains[3, : key_gain.shape[0]],
        gains[1, : mlp_gain.shape[0]],
    )
    grad_down, attention_grads, gains = lax.optimization_barrier(
        (grad_down, attention_grads, gains)
    )
    return (
        layer_out,
        grad_tokens,
        *attention_grads,
        *gains[:3],
        grad_gate,
        grad_up,
        grad_down.astype(f32),
        gains[3],
    )


def solution(mesh):
    by_rows, by_entry = P("fsdp", None), P("fsdp")
    return jax.shard_map(
        functools.partial(local, mesh.shape["fsdp"]),
        mesh=mesh,
        in_specs=(
            by_rows,
            by_rows,
            by_entry,
            by_rows,
            by_rows,
            by_rows,
            by_rows,
            by_rows,
            by_entry,
            by_entry,
            by_entry,
            by_rows,
            by_rows,
            by_rows,
            by_entry,
        ),
        out_specs=(
            by_rows,
            by_rows,
            by_rows,
            by_rows,
            by_rows,
            by_rows,
            by_entry,
            by_entry,
            by_entry,
            by_rows,
            by_rows,
            by_rows,
            by_entry,
        ),
        check_vma=False,
    )
```

time: 558 us -> 513 us (0.919); the launches traced: 548 us -> 509 us
  matrix products: 30.2 us -> 0 us
  Pallas kernels: 447 us -> 433 us
  local copies, waits for them, and re-layouts: 10.9 us -> 5.13 us
    dot_general x4 -> x0, matrix products: 30.2 us -> none  [dot_first(): lax.dot_general(left, right, (((0,), (0,)), ((), ())), preferred_element_...]
    pallas_call x9 -> x6, Pallas kernels: 352 us -> 328 us  [the longest x1 115 us: opening(): pl.pallas_call(functools.partial(open_kernel, planes, parts), out_shape=(...]
    pallas_call x1, Pallas kernels: 38.8 us -> 61.7 us  [feed(): pl.pallas_call(feed_kernel, out_shape=(like((TEAM, rows, width), bf16), l...]
    reduce_scatter x4, waiting for transfers between devices: 0.05 us -> 21.3 us  [sum_line(): lax.psum_scatter(x, 'fsdp', scatter_dimension=0, tiled=True, axis_index_g...]
    all_gather x3, waiting for transfers between devices: 24.8 us -> 8.39 us  [gather_line(): lax.all_gather(x, 'fsdp', axis=0, tiled=True, axis_index_groups=lines)]
    pallas_call x1, Pallas kernels: 26.2 us -> 13.1 us  [closing(): pl.pallas_call(functools.partial(close_kernel, planes), out_shape=(*(like...]
    convert_element_type x1 -> x7, other arithmetic: 1.41 us -> 12.3 us  [the longest x4 5.89 us: local(): g.astype(f32)]
  transfers between devices with their start and end apart: 7 -> 7, of which waited for: 2 -> 4; matrix products, arithmetic and copies ran while one was open for 9% -> 5% of each run, Pallas kernels for 81% -> 85%
where the time goes in v3:
time: 513 us; the launch traced here: 509 us
  Pallas kernels  433 us (84%)
  waiting for transfers between devices  31.8 us (6%)
  other arithmetic  23.6 us (5%)
  between operations  15.3 us (3%)
  local copies, waits for them, and re-layouts  5.13 us (1%)
    pallas_call x1, Pallas kernels, opening(): pl.pallas_call(functools.partial(open_kernel, planes, parts), out_shape=(...  115 us
    pallas_call x1, Pallas kernels, last_sums(): pl.pallas_call(functools.partial(last_sums_kernel, planes, parts), out_sh...  74.9 us
    pallas_call x1, Pallas kernels, feed(): pl.pallas_call(feed_kernel, out_shape=(like((TEAM, rows, width), bf16), l...  61.7 us
    pallas_call x1, Pallas kernels, feed_back(): pl.pallas_call(functools.partial(feed_back_kernel, parts), out_shape=(lik...  40.9 us
    pallas_call x1, Pallas kernels, team_sum(): pl.pallas_call(sum_kernel, out_shape=jax.ShapeDtypeStruct((rows, width),...  35.8 us
    pallas_call x1, Pallas kernels, gather_down(): pl.pallas_call(functools.partial(gather_down_kernel, parts), out_shape=(l...  33.3 us
    pallas_call x1, Pallas kernels, attend_back(): pl.pallas_call(functools.partial(attend_back_kernel, planes), out_shape=(...  28.7 us
    reduce_scatter x4, waiting for transfers between devices, sum_line(): lax.psum_scatter(x, 'fsdp', scatter_dimension=0, tiled=True, axis_index_g...  21.3 us
  transfers between devices with their start and end apart: 7, of which 4 were waited for; matrix products, arithmetic and copies ran while one was open for 5% of the time, Pallas kernels for 85%

profile of v3, /device:TPU:0, one launch (start us, length us, event | category | flops | bytes accessed | tf_op | source)
XLA Modules:
  0.0 509.0 jit_solution(10766544042640990951)
XLA Ops:
  8.0 115.0 %shard_map.255 = (bf16[8,64,768]{2,1,0:T(8,128)(2,1)}, bf16[8,64,768]{2,1,0:T(8,128)(2,1)}, bf16[4,8,64,512]{3,2,1,0:T(8,128)(2,1)}, bf16[4,64,2048]{2,1,0:T(8,1...) custom-call(bf16[64,2048]{1,0:T(8,128)(2,1)} %query_in.1, ...), custom_call_target="tpu_custom_call" | custom-call | tf_op jit(solution)/shard_map/pallas_call | solution.py:756
  124.6 16.0 %shard_map.256 = (bf16[1536,2048]{1,0:T(8,128)(2,1)}, f32[1536,384]{1,0:T(8,128)}, bf16[1536,384]{1,0:T(8,128)(2,1)}, bf16[1536,128]{1,0:T(8,128)(2,1)}, bf16[1536,256]{1,0:T(8,128)(2,1)}) custom-call(bf16[1536,2048]{1,0:T(8,128)(2,1)} %bitcast.54, f32[1,2048]{1,0:T(1,128)} %get-tuple-element.66.gain, bf16[2048,512]{1,0:T(8,128)(2,1)} %bitcast.55, ...), custom_call_target="tpu_custom_call" | custom-call | flops 3221225472 | bytes 25165824 | tf_op jit(solution)/shard_map/pallas_call | solution.py:927
  140.6 35.8 %shard_map.257 = f32[192,2048]{1,0:T(8,128)} custom-call(bf16[8,192,256]{2,1,0:T(8,128)(2,1)} %bitcast.63, bf16[256,2048]{1,0:T(8,128)(2,1)} %bitcast.57), custom_call_target="tpu_custom_call" | custom-call | flops 1610612736 | bytes 3407872 | tf_op jit(solution)/shard_map/pallas_call | solution.py:335
  176.4 1.9 multiply_reduce_fusion.2
  180.4 6.4 %all-gather.4.cloned.1.call-done.weight_in.refs_2_ = bf16[2048,768]{1,0:T(8,128)(2,1)} async-done(((bf16[512,768]{1,0:T(8,128)(2,1)}), bf16[2048,768]{1,0:T(8,128)(2,1)}) %all-gather.4.cloned.1.call-update) | async-done | bytes 3145744 | tf_op jit(solution)/shard_map/all_gather | solution.py:1291
  186.8 61.7 %shard_map.258 = (bf16[8,192,2048]{2,1,0:T(8,128)(2,1)}, bf16[8,192,2048]{2,1,0:T(8,128)(2,1)}, bf16[8,192,384]{2,1,0:T(8,128)(2,1)}, bf16[8,192,768]{2,1,0:T(8,128)(2,1)}, bf16[2048,768]{1,0:T(8,128)(2,1)}) custom-call(bf16[192,2048]{1,0:T(8,128)(2,1)} %multiply_convert_fusion.1.two_in, bf16[192,2048]{1,0:T(8,128)(2,1)} %broadcast_multiply_fusion.cot_in, ...), custom_call_target="tpu_custom_call" | custom-call | flops 12079595520 | bytes 25165824 | tf_op jit(solution)/shard_map/pallas_call | solution.py:1195
  248.5 2.0 all-gather.8.cloned.1.call-done.weight.refs_3_
  250.5 13.6 %shard_map.259 = (bf16[8,192,384]{2,1,0:T(8,128)(2,1)}, bf16[8,192,768]{2,1,0:T(8,128)(2,1)}) custom-call(bf16[8,192,2048]{2,1,0:T(8,128)(2,1)} %get-tuple-element.75.two, bf16[8,192,2048]{2,1,0:T(8,128)(2,1)} %get-tuple-element.77.cot, bf16[2048,768]{1,0:T(8,128)(2,1)} %all-gather.8.cloned.1.call-done.weight.refs_3_, ...), custom_call_target="tpu_custom_call" | custom-call | flops 7247757312 | bytes 12582912 | tf_op jit(solution)/shard_map/pallas_call | solution.py:1240
  264.2 40.9 %shard_map.260 = (f32[192,2048]{1,0:T(8,128)}, bf16[2048,768]{1,0:T(8,128)(2,1)}) custom-call(bf16[8,192,2048]{2,1,0:T(8,128)(2,1)} %get-tuple-element.75.two, bf16[8,192,768]{2,1,0:T(8,128)(2,1)} %get-tuple-element.76.refs_0_, bf16[8,192,768]{2,1,0:T(8,128)(2,1)} %get-tuple-element.79.refs_1_, ...), custom_call_target="tpu_custom_call" | custom-call | flops 14495514624 | bytes 11010048 | tf_op jit(solution)/shard_map/pallas_call | solution.py:386
  305.1 1.3 copy-done
  307.6 1.4 fusion.10.x
  309.0 33.3 %shard_map.261 = (bf16[8,192,2048]{2,1,0:T(8,128)(2,1)}, bf16[768,2048]{1,0:T(8,128)(2,1)}) custom-call(bf16[192,2048]{1,0:T(8,128)(2,1)} %fusion.10.x, bf16[8,192,2048]{2,1,0:T(8,128)(2,1)} %get-tuple-element.77.cot, bf16[8,192,384]{2,1,0:T(8,128)(2,1)} %get-tuple-element.81.refs_0_, bf16[8,192,384]{2,1,0:T(8,128)(2,1)} %get-tuple-element.82.refs_1_), custom_call_target="tpu_custom_call" | custom-call | flops 4831838208 | bytes 18874368 | tf_op jit(solution)/shard_map/pallas_call | solution.py:448
  342.3 28.7 %shard_map.262 = (bf16[1536,512]{1,0:T(8,128)(2,1)}, bf16[4,768,512]{2,1,0:T(8,128)(2,1)}, f32[8,128]{1,0:T(8,128)}) custom-call(bf16[1536,2048]{1,0:T(8,128)(2,1)} %bitcast.61, bf16[256,2048]{1,0:T(8,128)(2,1)} %bitcast.58, bf16[1536,256]{1,0:T(8,128)(2,1)} %get-tuple-element.71.context, f32[1536,384]{1,0:T(8,128)} %get-tuple-element.84.raw_in, ...), custom_call_target="tpu_custom_call" | custom-call | flops 6442450944 | bytes 25165824 | tf_op jit(solution)/shard_map/pallas_call | solution.py:1085
  374.1 74.9 %shard_map.263 = (f32[192,2048]{1,0:T(8,128)}, f32[192,2048]{1,0:T(8,128)}, bf16[64,6144]{1,0:T(8,128)(2,1)}, bf16[64,6144]{1,0:T(8,128)(2,1)}) custom-call(bf16[8,192,512]{2,1,0:T(8,128)(2,1)} %bitcast.62, bf16[2048,512]{1,0:T(8,128)(2,1)} %bitcast.56, bf16[768,2048]{1,0:T(8,128)(2,1)} %all-gather.6.cloned.1.call-done.down_in.down, ...), custom_call_target="tpu_custom_call" | custom-call | flops 8053063680 | bytes 3145728 | tf_op jit(solution)/shard_map/pallas_call | solution.py:526
  449.0 2.1 fusion.6
  452.0 2.5 convert_element_type.69
  454.5 2.5 convert_element_type.70
  457.0 2.3 fusion.2
  459.3 13.1 %shard_map.264 = (bf16[64,2048]{1,0:T(8,128)(2,1)}, bf16[64,1024]{1,0:T(8,128)(2,1)}, bf16[64,1024]{1,0:T(8,128)(2,1)}, bf16[64,2048]{1,0:T(8,128)(2,1)}, f32[8,128]{1,0:T(8,128)}) custom-call(bf16[768,512]{1,0:T(8,128)(2,1)} %reduce-scatter.5.cloned.1.call-done.x_ref, f32[8,4,8,128]{3,2,1,0:T(8,128)} %bitcast.43), custom_call_target="tpu_custom_call" | custom-call | tf_op jit(solution)/shard_map/pallas_call | solution.py:844
  472.4 1.8 convert_element_type.73
  474.2 1.6 convert_element_type.74
  475.8 1.6 convert_element_type.75
  479.3 20.1 %reduce-scatter.11.cloned.1.call-done = bf16[192,2048]{1,0:T(8,128)(2,1)} async-done(((bf16[768,2048]{1,0:T(8,128)(2,1)}), bf16[192,2048]{1,0:T(8,128)(2,1)}) %reduce-scatter.11.cloned.1.call-update) | async-done | bytes 786448 | tf_op jit(solution)/shard_map/reduce_scatter | solution.py:1294
  499.4 2.5 convert_element_type.77
  (65 shorter events, 10.8 us)
Async XLA Ops:
  7.2 173.2 %all-gather.6.cloned.1.call-start = ((), (), s32[]{:S(2)}) async-start(), calls=%async_computation.5 | async-start | bytes 3932160 | tf_op jit(solution)/shard_map/all_gather | solution.py:1291
  7.9 178.9 %all-gather.4.cloned.1.call-start = ((), (), s32[]{:S(2)}) async-start(), calls=%async_computation.4 | async-start | bytes 3932160 | tf_op jit(solution)/shard_map/all_gather | solution.py:1291
  123.0 127.6 %all-gather.8.cloned.1.call-start = ((), (), s32[]{:S(2)}) async-start(), calls=%async_computation.6 | async-start | bytes 3932160 | tf_op jit(solution)/shard_map/all_gather | solution.py:1291
  123.7 249.2 %reduce-scatter.7.cloned.1.call-start = ((), (), s32[]{:S(2)}) async-start(), calls=%async_computation.8 | async-start | bytes 3932160 | tf_op jit(solution)/shard_map/reduce_scatter | solution.py:1294
  140.6 35.8 %copy-start.1 = (bf16[192,2048]{1,0:T(8,128)(2,1)S(1)}, bf16[192,2048]{1,0:T(8,128)(2,1)}, u32[]{:S(2)}) copy-start(bf16[192,2048]{1,0:T(8,128)(2,1)} %tokens_in.1) | copy-start | bytes 2359300
  176.4 1.9 copy-start.3
  178.3 1.0 copy-start.9
  248.5 125.6 %reduce-scatter.9.cloned.1.call-start = ((), (), s32[]{:S(2)}) async-start(), calls=%async_computation.9 | async-start | bytes 3932160 | tf_op jit(solution)/shard_map/reduce_scatter | solution.py:1294
  305.0 1.4 copy-start
  305.1 154.2 %reduce-scatter.5.cloned.1.call-start = ((), (), s32[]{:S(2)}) async-start(), calls=%async_computation.7 | async-start | bytes 3932160 | tf_op jit(solution)/shard_map/reduce_scatter | solution.py:1294
  306.4 1.2 copy-start.4
  371.0 128.4 %reduce-scatter.11.cloned.1.call-start = ((), (), s32[]{:S(2)}) async-start(), calls=%async_computation.10 | async-start | bytes 3932160 | tf_op jit(solution)/shard_map/reduce_scatter | solution.py:1294
  374.1 74.9 %copy-start.10 = (f32[1,2048]{1,0:T(1,128)S(1)}, f32[1,2048]{1,0:T(1,128)}, u32[]{:S(2)}) copy-start(f32[1,2048]{1,0:T(1,128)} %get-tuple-element.66.gain) | copy-start | bytes 24580
  451.9 5.1 copy-start.6
  451.9 5.1 copy-start.7
  454.5 2.5 copy-start.2
  454.5 2.5 copy-start.5
  472.4 5.1 copy-start.8
  472.4 5.9 %copy-start.11 = (f32[8,128]{1,0:T(8,128)S(1)}, f32[8,128]{1,0:T(8,128)}, u32[]{:S(2)}) copy-start(f32[8,128]{1,0:T(8,128)} %get-tuple-element.105) | copy-start | bytes 12292
Sparse Core Ops, SparseCore 0:
  9.6 92.4 all-gather.5
  123.1 63.6 all-gather.3
  188.4 62.1 all-gather.7
  252.7 58.8 reduce-scatter.6
  313.8 60.2 reduce-scatter.8
  376.3 60.2 reduce-scatter.4
  438.9 60.4 reduce-scatter.10

commit v4 on v3

--- a/solution.py
+++ b/solution.py
@@ -155,6 +155,52 @@
             copy.wait_send()
 
 
+class Line:
+    def __init__(self, sender, ref, planes, me):
+        self.sender, self.ref, self.planes = sender, ref, planes
+        self.plane, self.place = lax.div(me, TEAM), lax.rem(me, TEAM)
+        self.flows = [(sign, [sender.take() for _ in range(planes - 1)]) for sign in (1, -1)]
+
+    def passing(self, step, sign, ks, source):
+        block = jnp.clip(source, 0, self.planes - 1)
+        beyond = jnp.clip(self.plane + sign, 0, self.planes - 1) * TEAM + self.place
+        ref, k = self.ref.at[block], ks[step]
+        return remote(ref, ref, self.sender.send.at[k], self.sender.receive.at[k], beyond)
+
+    def goes(self, step, sign):
+        source, onward = self.plane - sign * step, self.plane + sign
+        last = self.planes - 1
+        return (source >= 0) & (source <= last) & (onward >= 0) & (onward <= last)
+
+    def start(self, step):
+        for sign, ks in self.flows:
+            going = self.passing(step, sign, ks, self.plane - sign * step)
+            pl.when(self.goes(step, sign))(going.start)
+
+    def arrive(self, step):
+        for sign, ks in self.flows:
+            source = self.plane - sign * (step + 1)
+            coming = self.passing(step, sign, ks, source)
+            pl.when((source >= 0) & (source <= self.planes - 1))(coming.wait_recv)
+
+    def sent(self, step):
+        for sign, ks in self.flows:
+            going = self.passing(step, sign, ks, self.plane - sign * step)
+            pl.when(self.goes(step, sign))(going.wait_send)
+
+    def through(self, first, last):
+        for step in range(first, last):
+            self.arrive(step)
+            if step + 1 < last:
+                self.start(step + 1)
+        for step in range(first, last):
+            self.sent(step)
+
+
+def line_peers(me, planes):
+    return [lax.rem(me + TEAM * k, planes * TEAM) for k in range(1, planes)]
+
+
 TILE = 512
 STRIP = 16
 
@@ -177,7 +223,11 @@
             at = pl.ds(pl.multiple_of(t * TILE, TILE), TILE)
             value = 0.0
             for left, right in zip(self.lefts, self.rights):
-                both = left[pl.ds(2 * self.chips[j], 2)].reshape(2 * self.rows, left.shape[2])
+                if len(left.shape) == 2:
+                    first = pl.multiple_of(self.chips[j] * 2 * self.rows, 2 * self.rows)
+                    both = left[pl.ds(first, 2 * self.rows), :]
+                else:
+                    both = left[pl.ds(2 * self.chips[j], 2)].reshape(2 * self.rows, left.shape[2])
                 if self.turned:
                     value = value + dot_last(both, right[at, :])
                 else:
@@ -309,49 +359,6 @@
         at = pl.ds(pl.multiple_of(t * TILE, TILE), TILE)
         value = dot_first(left[:, :, at].reshape(blocks * rows, TILE), flat)
         out[at, :] = value.astype(bf16)
-
-
-def sum_kernel(left, right, out, *rest):
-    buffers, (left_here, right_here, send, receive, own) = rest[:4], rest[4:]
-    me = lax.axis_index("fsdp")
-    loader = Loader(own)
-    loader(right, right_here)
-    loader(left, left_here)
-    greet(me, (1, 2, 4))
-    loader.wait()
-    sender = Sender(send, receive)
-    total = TeamSum(sender, me, out, buffers, [left_here], [right_here], False)
-    total.start()
-    total.own()
-    total.relay()
-    total.finish()
-    sender.finish()
-
-
-def team_sum(left, right, collective):
-    _, rows, depth = left.shape
-    width = right.shape[1]
-    anywhere = pl.BlockSpec(memory_space=pl.ANY)
-    return pl.pallas_call(
-        sum_kernel,
-        out_shape=jax.ShapeDtypeStruct((rows, width), f32),
-        in_specs=[anywhere, anywhere],
-        out_specs=pl.BlockSpec(memory_space=pltpu.VMEM),
-        scratch_shapes=[
-            *sum_buffers(rows, width),
-            pltpu.VMEM(left.shape, bf16),
-            pltpu.VMEM(right.shape, bf16),
-            pltpu.SemaphoreType.DMA((SUM_COPIES,)),
-            pltpu.SemaphoreType.DMA((SUM_COPIES,)),
-            pltpu.SemaphoreType.DMA((2,)),
-        ],
-        compiler_params=params(collective, LIMIT),
-        cost_estimate=pl.CostEstimate(
-            flops=2 * TEAM * rows * depth * width,
-            bytes_accessed=2 * TEAM * rows * depth + 2 * depth * width + 4 * rows * width,
-            transcendentals=0,
-        ),
-    )(left, right)
 
 
 def feed_back_kernel(parts, two, *refs):
@@ -549,50 +556,16 @@
     )(grad_qkv, qkv_weight, down, *acts, *units)
 
 
-class Line:
-    def __init__(self, sender, ref, planes, me):
-        self.sender, self.ref, self.planes = sender, ref, planes
-        self.plane, self.place = lax.div(me, TEAM), lax.rem(me, TEAM)
-        self.flows = [(sign, [sender.take() for _ in range(planes - 1)]) for sign in (1, -1)]
-
-    def passing(self, step, sign, ks, source):
-        block = jnp.clip(source, 0, self.planes - 1)
-        beyond = jnp.clip(self.plane + sign, 0, self.planes - 1) * TEAM + self.place
-        ref, k = self.ref.at[block], ks[step]
-        return remote(ref, ref, self.sender.send.at[k], self.sender.receive.at[k], beyond)
-
-    def goes(self, step, sign):
-        source, onward = self.plane - sign * step, self.plane + sign
-        last = self.planes - 1
-        return (source >= 0) & (source <= last) & (onward >= 0) & (onward <= last)
-
-    def start(self, step):
-        for sign, ks in self.flows:
-            going = self.passing(step, sign, ks, self.plane - sign * step)
-            pl.when(self.goes(step, sign))(going.start)
-
-    def arrive(self, step):
-        for sign, ks in self.flows:
-            source = self.plane - sign * (step + 1)
-            coming = self.passing(step, sign, ks, source)
-            pl.when((source >= 0) & (source <= self.planes - 1))(coming.wait_recv)
-
-    def sent(self, step):
-        for sign, ks in self.flows:
-            going = self.passing(step, sign, ks, self.plane - sign * step)
-            pl.when(self.goes(step, sign))(going.wait_send)
-
-
 SWAP_ORDER = (6, 7, 2, 3, 4, 5, 1)
 
 
 def open_kernel(
-    planes, parts, query_in, key_in, value_in, output_in, tokens_in, gate_in, up_in, *refs
+    planes, parts, query_in, key_in, value_in, output_in, tokens_in, gate_in, up_in, down_in, *refs
 ):
     smalls, refs = refs[:5], refs[5:]
     gate_up, refs = refs[:parts], refs[parts:]
-    qkv, output_raw, output, tokens, *gain_refs, numbers = refs[:9]
-    small_in, small, sorted_units, send, receive, own = refs[9:]
+    qkv, output_raw, output, tokens, down, *gain_refs, numbers = refs[:10]
+    small_in, small, sorted_units, send, receive, own = refs[10:]
     slots, sequence = smalls[4].shape
     small_in[...] = jnp.zeros_like(small_in)
     for k, ref in enumerate(smalls):
@@ -623,11 +596,13 @@
         keep(columns(ref, part, place), target)
     keep(small_in, small.at[me])
     keep(tokens_in, tokens.at[place])
+    keep(down_in, down.at[plane])
     keep(output_in, output_raw.at[plane])
     greet(me, range(1, TEAM), others)
 
     qkv_line = Line(sender, qkv, planes, me)
     out_line = Line(sender, output_raw, planes, me)
+    down_line = Line(sender, down, planes, me)
     rows_tokens = Gather(sender, tokens_in, tokens, me)
     spread_send = [sender.take() for _ in range(planes)]
     spread_own = len(keeps)
@@ -665,6 +640,8 @@
     near = [sender(small_in, small.at[me], flipped(me, m)) for m in SWAP_ORDER]
     keeps[-1].wait()
     out_line.start(0)
+    keeps[-2].wait()
+    down_line.start(0)
     block = gate_in.shape[1] // (planes * TEAM)
     some = planes // parts
     units = some * block
@@ -682,13 +659,13 @@
     qkv_line.start(0)
     rows_tokens.start()
     moves = [
-        sender(sorted_units.at[k, flipped(place, m)], gate_up[k].at[place], flipped(me, m))
+        sender(sorted_units.at[k, flipped(place, m)], gate_up[k].at[plane, place], flipped(me, m))
         for k in range(parts)
         for m in SWAP_ORDER
     ]
     kept_units = [
         pltpu.make_async_copy(
-            sorted_units.at[k, place], gate_up[k].at[place], own.at[spread_own + planes + k]
+            sorted_units.at[k, place], gate_up[k].at[plane, place], own.at[spread_own + planes + k]
         )
         for k in range(parts)
     ]
@@ -708,6 +685,9 @@
         if step < planes - 2:
             qkv_line.start(step + 1)
             step_out(step + 1)
+        down_line.arrive(step)
+        if step < planes - 2:
+            down_line.start(step + 1)
         if step == 0:
             rows_tokens.diagonal()
         if step == 1:
@@ -739,13 +719,14 @@
     for step in range(planes - 1):
         qkv_line.sent(step)
         out_line.sent(step)
+        down_line.sent(step)
     sender.finish()
-    for copy in keeps[4:-1]:
+    for copy in keeps[4:-2]:
         copy.wait()
 
 
-def opening(query, key, value, output, tokens, gate, up, smalls, planes, parts, collective):
-    links = 28 + 4 * (planes - 1) + 14 + planes - 1 + planes + parts * (TEAM - 1)
+def opening(query, key, value, output, tokens, gate, up, down, smalls, planes, parts, collective):
+    links = 28 + 6 * (planes - 1) + 14 + planes - 1 + planes + parts * (TEAM - 1)
     anywhere = pl.BlockSpec(memory_space=pl.ANY)
     vmem = pl.BlockSpec(memory_space=pltpu.VMEM)
     like = jax.ShapeDtypeStruct
@@ -756,26 +737,27 @@
     return pl.pallas_call(
         functools.partial(open_kernel, planes, parts),
         out_shape=(
-            *((like(units, bf16),) * parts),
+            *((like((planes, *units), bf16),) * parts),
             like((planes, TEAM, rows, width), bf16),
             like((planes, *output.shape), bf16),
             like((planes, *output.shape), bf16),
             like((TEAM, *tokens.shape), bf16),
+            like((planes, *down.shape), bf16),
             *(like((1, devices * x.shape[1]), f32) for x in smalls[:4]),
             like((TEAM * tokens.shape[0] // STEP, 1, STEP), f32),
         ),
-        in_specs=[vmem] * 12,
-        out_specs=(anywhere,) * (4 + parts) + (vmem,) * 5,
+        in_specs=[vmem] * 13,
+        out_specs=(anywhere,) * (5 + parts) + (vmem,) * 5,
         scratch_shapes=[
             pltpu.VMEM((8, 128), f32),
             pltpu.VMEM((devices, 8, 128), f32),
             pltpu.VMEM((parts, *units), bf16),
             pltpu.SemaphoreType.DMA((links,)),
             pltpu.SemaphoreType.DMA((links,)),
-            pltpu.SemaphoreType.DMA((6 + planes + parts,)),
+            pltpu.SemaphoreType.DMA((7 + planes + parts,)),
         ],
         compiler_params=params(collective, LIMIT),
-    )(query, key, value, output, tokens, gate, up, *smalls)
+    )(query, key, value, output, tokens, gate, up, down, *smalls)
 
 
 def close_kernel(planes, x_ref, gains, *refs):
@@ -883,34 +865,6 @@
     return expos / jnp.sum(expos, axis=1, keepdims=True)
 
 
-def attend_kernel(
-    x_ref, gain, weight, ids_row, table, query_gain, key_gain,
-    normed_ref, raw_ref, turned_ref, value_ref, context_ref,
-):
-    x = x_ref[...].astype(f32)
-    scale = lax.rsqrt(jnp.mean(x * x, axis=1, keepdims=True) + epsilon)
-    normed = (x * scale * gain[...]).astype(bf16)
-    normed_ref[...] = normed
-    projected = simple_product(normed, weight[...])
-    visible, cosine, sine = visible_and_tables(ids_row[0], table[...])
-    heads = context_ref.shape[1] // HEAD_SIZE
-    raw_ref[...] = projected[:, : (heads + 1) * HEAD_SIZE]
-    value = projected[:, (heads + 1) * HEAD_SIZE :].astype(bf16)
-    value_ref[...] = value
-    turned = []
-    for h in range(heads + 1):
-        raw = projected[:, h * HEAD_SIZE : (h + 1) * HEAD_SIZE]
-        head_gain = query_gain if h < heads else key_gain
-        y = raw * lax.rsqrt(jnp.mean(raw * raw, axis=1, keepdims=True) + epsilon) * head_gain[...]
-        y = y * cosine + pltpu.roll(y, HEAD_SIZE // 2, 1) * sine
-        turned.append(y.astype(bf16))
-        turned_ref[:, h * HEAD_SIZE : (h + 1) * HEAD_SIZE] = turned[-1]
-    for h in range(heads):
-        probs = softmax(turned[h], turned[heads], visible).astype(bf16)
-        context = simple_product(probs, value)
-        context_ref[:, h * HEAD_SIZE : (h + 1) * HEAD_SIZE] = context.astype(bf16)
-
-
 def by_step(*shape):
     return pl.BlockSpec(shape, lambda i: (i, *(0 for _ in shape[1:])))
 
@@ -919,42 +873,151 @@
     return pl.BlockSpec(shape, lambda i: tuple(0 for _ in shape))
 
 
-def attend(x, gain, weight, ids, table, query_gain, key_gain):
+def attend_kernel(
+    planes, x_in, gain, weight, ids_row, table, query_gain, key_gain, right_in, tokens, cot_in, live,
+    mlp_gain, _, normed_out, raw_out, turned_out, value_out, context_out, out, two, cot, units,
+    x_ref, normed_ref, raw_ref, turned_ref, value_ref, context_ref, cot_own,
+    mix, from_core, from_x, from_y, right, send, receive, own,
+):
+    me = lax.axis_index("fsdp")
+    loader = Loader(own)
+    steps = x_ref.shape[0] // STEP
+    for i in range(steps):
+        loader(rows_of(x_in, i, STEP), rows_of(x_ref, i, STEP))
+    load_right = loader(right_in, right)
+    cot_own[...] = cot_in[...] * live[...]
+    keep = loader(cot_own, cot.at[lax.rem(me, TEAM)])
+    greet(me, (1, 2, 4), line_peers(me, planes))
+    sender = Sender(send, receive)
+    line = Line(sender, units, planes, me)
+    rows_cot = Gather(sender, cot_own, cot, me)
+    line.start(0)
+    rows_cot.start()
+    heads = context_ref.shape[1] // HEAD_SIZE
+    homes = []
+
+    def attention(i):
+        loader.copies[i].wait()
+        here = slice(i * STEP, (i + 1) * STEP)
+        x = x_ref[here].astype(f32)
+        scale = lax.rsqrt(jnp.mean(x * x, axis=1, keepdims=True) + epsilon)
+        normed = (x * scale * gain[...]).astype(bf16)
+        normed_ref[here] = normed
+        projected = simple_product(normed, weight[...])
+        visible, cosine, sine = visible_and_tables(ids_row[i], table[...])
+        raw_ref[here] = projected[:, : (heads + 1) * HEAD_SIZE]
+        value = projected[:, (heads + 1) * HEAD_SIZE :].astype(bf16)
+        value_ref[here] = value
+        turned = []
+        for h in range(heads + 1):
+            at = slice(h * HEAD_SIZE, (h + 1) * HEAD_SIZE)
+            raw = projected[:, at]
+            head_gain = query_gain if h < heads else key_gain
+            scale = lax.rsqrt(jnp.mean(raw * raw, axis=1, keepdims=True) + epsilon)
+            y = raw * scale * head_gain[...]
+            y = y * cosine + pltpu.roll(y, HEAD_SIZE // 2, 1) * sine
+            turned.append(y.astype(bf16))
+            turned_ref[here, at] = turned[-1]
+        for h in range(heads):
+            probs = softmax(turned[h], turned[heads], visible).astype(bf16)
+            context = simple_product(probs, value)
+            context_ref[here, h * HEAD_SIZE : (h + 1) * HEAD_SIZE] = context.astype(bf16)
+        for ref, home in (
+            (normed_ref, normed_out), (raw_ref, raw_out), (turned_ref, turned_out),
+            (value_ref, value_out), (context_ref, context_out),
+        ):
+            homes.append(loader(rows_of(ref, i, STEP), rows_of(home, i, STEP)))
+
+    for i in range(steps):
+        attention(i)
+        if i == steps // 2 - 1:
+            rows_cot.forward()
+    rows_cot.across()
+    line.arrive(0)
+    if planes > 2:
+        line.start(1)
+    load_right.wait()
+    buffers = [mix, from_core, from_x, from_y]
+    total = TeamSum(sender, me, out, buffers, [context_ref], [right], False)
+    total.start()
+    rows_cot.diagonal()
+    total.own()
+    total.relay()
+    if planes > 2:
+        line.arrive(1)
+    if planes > 3:
+        line.start(2)
+    total.finish()
+
+    @pl.loop(0, out.shape[0] // STRIP)
+    def _(i):
+        at = pl.ds(i * STRIP, STRIP)
+        middle = tokens[at, :].astype(f32) + out[at, :]
+        out[at, :] = middle
+        scale = lax.rsqrt(jnp.mean(middle * middle, axis=1, keepdims=True) + epsilon)
+        two[at, :] = (middle * scale * mlp_gain[...]).astype(bf16)
+
+    rows_cot.arrive()
+    if planes > 3:
+        line.through(2, planes - 1)
+    for step in range(min(2, planes - 1)):
+        line.sent(step)
+    sender.finish()
+    for copy in (keep, *homes):
+        copy.wait()
+
+
+def attend(
+    x, gain, weight, ids, table, query_gain, key_gain, right, tokens, cot, live, mlp_gain, units,
+    planes, collective,
+):
     rows, width = x.shape
     out = weight.shape[1]
+    heads = out - 2 * HEAD_SIZE
+    own_rows = tokens.shape[0]
+    steps = rows // STEP
     like = jax.ShapeDtypeStruct
-    heads = out - 2 * HEAD_SIZE
+    anywhere = pl.BlockSpec(memory_space=pl.ANY)
+    vmem = pl.BlockSpec(memory_space=pltpu.VMEM)
+    kept = (
+        like((rows, width), bf16),
+        like((rows, heads + HEAD_SIZE), f32),
+        like((rows, heads + HEAD_SIZE), bf16),
+        like((rows, HEAD_SIZE), bf16),
+        like((rows, heads), bf16),
+    )
+    links = SUM_COPIES + 14 + 2 * (planes - 1)
     return pl.pallas_call(
-        attend_kernel,
-        grid=(rows // STEP,),
+        functools.partial(attend_kernel, planes),
         out_shape=(
-            like((rows, width), bf16),
-            like((rows, heads + HEAD_SIZE), f32),
-            like((rows, heads + HEAD_SIZE), bf16),
-            like((rows, HEAD_SIZE), bf16),
-            like((rows, heads), bf16),
+            *kept,
+            like((own_rows, width), f32),
+            like((own_rows, width), bf16),
+            like((TEAM, own_rows, width), bf16),
+            like(units.shape, bf16),
         ),
-        in_specs=[
-            by_step(STEP, width),
-            fixed(1, width),
-            fixed(width, out),
-            by_step(1, 1, STEP),
-            fixed(*table.shape),
-            fixed(1, HEAD_SIZE),
-            fixed(1, HEAD_SIZE),
+        in_specs=[anywhere] + [vmem] * 6 + [anywhere] + [vmem] * 4 + [anywhere],
+        out_specs=(*([anywhere] * 5), vmem, vmem, anywhere, anywhere),
+        input_output_aliases={12: 8},
+        scratch_shapes=[
+            pltpu.VMEM((rows, width), bf16),
+            *(pltpu.VMEM(x.shape, x.dtype) for x in kept),
+            pltpu.VMEM((own_rows, width), bf16),
+            *sum_buffers(own_rows, width),
+            pltpu.VMEM(right.shape, bf16),
+            pltpu.SemaphoreType.DMA((links,)),
+            pltpu.SemaphoreType.DMA((links,)),
+            pltpu.SemaphoreType.DMA((6 * steps + 2,)),
         ],
-        out_specs=(
-            by_step(STEP, width),
-            by_step(STEP, heads + HEAD_SIZE),
-            by_step(STEP, heads + HEAD_SIZE),
-            by_step(STEP, HEAD_SIZE),
-            by_step(STEP, heads),
+        compiler_params=params(collective, LIMIT),
+        cost_estimate=pl.CostEstimate(
+            flops=2 * rows * width * (out + heads),
+            bytes_accessed=8 * rows * width,
+            transcendentals=0,
         ),
-        compiler_params=pltpu.CompilerParams(vmem_limit_bytes=LIMIT),
-        cost_estimate=pl.CostEstimate(
-            flops=2 * rows * width * out, bytes_accessed=8 * rows * width, transcendentals=0
-        ),
-    )(x, gain, weight, ids, table, query_gain, key_gain)
+    )(
+        x, gain, weight, ids, table, query_gain, key_gain, right, tokens, cot, live, mlp_gain, units
+    )
 
 
 def attend_back_kernel(planes, grad_in, out_weight, context, raw_in, turned_in, value_in, normed_in,
@@ -1121,98 +1184,111 @@
 
 
 def feed_kernel(
-    two_in, cot_in, weight_in, down_in, two_out, cot_out, act, grad_both, grad_weight,
-    two, cot, weight, down, both, weight_sum, send, receive, own,
+    planes, two_in, cot_in, weight_in, down_in, _, two_out, act_out, grad_both_out,
+    weight_out, units_ref, two, cot, weight, down, both, weight_sum, act, grad_both, grad_weight,
+    send, receive, own,
 ):
     me = lax.axis_index("fsdp")
     place = lax.rem(me, TEAM)
     loader = Loader(own)
     loader(two_in, two.at[place])
-    loader(cot_in, cot.at[place])
+    loader(cot_in, cot)
     loader(weight_in, weight)
     loader(rows_of(down_in, 0, down.shape[0]), down)
-    greet(me, (1, 2, 4))
+    greet(me, (1, 2, 4), line_peers(me, planes))
     sender = Sender(send, receive)
     rows_two = Gather(sender, two_in, two, me)
-    rows_cot = Gather(sender, cot_in, cot, me)
+    line = Line(sender, units_ref, planes, me)
     rows_two.start()
-    rows_cot.start()
+    line.start(0)
     rows, units = act.shape[1:]
     width = two.shape[2]
-    weight_sum[...] = jnp.zeros_like(weight_sum)
 
     crossed = {0: (0, 1), 2: (2, 4), 4: (3, 5), 6: (6, 7)}
 
-    def chip_rows(moves, mask, target):
+    def chip_of(mask):
+        return pl.ds(2 * lax.div(flipped(place, mask), 2), 2)
+
+    def work(mask):
         for k in crossed[mask]:
-            moves.late[k].wait_recv()
-        chip = pl.ds(2 * lax.div(flipped(place, mask), 2), 2)
-        loader(moves.o.at[chip], target.at[chip])
-        return chip, moves.o[chip].reshape(2 * rows, width)
-
-    def forward(mask):
-        _, flat = chip_rows(rows_two, mask, two_out)
-        both[mask // 2] = simple_product(flat, weight[...])
-
-    def backward(mask):
-        chip, flat = chip_rows(rows_cot, mask, cot_out)
-        a, grad_gate, grad_up = hidden_grads(both[mask // 2], flat, down[...])
+            rows_two.late[k].wait_recv()
+        chip = chip_of(mask)
+        loader(two.at[chip], two_out.at[chip])
+        both[...] = simple_product(two[chip].reshape(2 * rows, width), weight[...])
+        flat = cot[chip].reshape(2 * rows, width)
+        a, grad_gate, grad_up = hidden_grads(both[...], flat, down[...])
         act[chip] = a.reshape(2, rows, units)
+        loader(act.at[chip], act_out.at[chip])
         grads = jnp.concatenate([grad_gate, grad_up], axis=1)
         grad_both[chip] = grads.reshape(2, rows, 2 * units)
+        loader(grad_both.at[chip], grad_both_out.at[chip])
         for t in range(width // TILE):
             at = slice(t * TILE, (t + 1) * TILE)
             left = two[chip, :, at].reshape(2 * rows, TILE)
-            weight_sum[at, :] += dot_first(left, grads)
+            term = dot_first(left, grads)
+            if mask == 0:
+                weight_sum[at, :] = term
+            elif mask != 6:
+                weight_sum[at, :] += term
+            else:
+                tile = pl.ds(t * TILE, TILE)
+                grad_weight[at, :] = (weight_sum[at, :] + term).astype(bf16)
+                loader(grad_weight.at[tile], weight_out.at[tile])
 
     rows_two.forward()
+    loader.wait()
+    work(0)
     rows_two.across()
-    loader.wait()
-    forward(0)
-    backward(0)
-    rows_cot.forward()
-    forward(2)
-    forward(4)
-    rows_cot.across()
-    backward(2)
+    line.arrive(0)
+    if planes > 2:
+        line.start(1)
+    work(2)
     rows_two.diagonal()
-    backward(4)
-    forward(6)
-    rows_cot.diagonal()
-    backward(6)
-    grad_weight[...] = weight_sum[...].astype(bf16)
+    work(4)
+    if planes > 2:
+        line.arrive(1)
+    if planes > 3:
+        line.start(2)
+    work(6)
+    if planes > 3:
+        line.through(2, planes - 1)
+    for step in range(min(2, planes - 1)):
+        line.sent(step)
     sender.finish()
     for copy in loader.copies[4:]:
         copy.wait()
 
 
-def feed(two, cot, weight, down, collective):
+def feed(two, cot, weight, down, next_units, planes, collective):
     rows, width = two.shape
     units = weight.shape[1] // 2
-    vmem = pl.BlockSpec(memory_space=pltpu.VMEM)
     anywhere = pl.BlockSpec(memory_space=pl.ANY)
     like = jax.ShapeDtypeStruct
     return pl.pallas_call(
-        feed_kernel,
+        functools.partial(feed_kernel, planes),
         out_shape=(
-            like((TEAM, rows, width), bf16),
             like((TEAM, rows, width), bf16),
             like((TEAM, rows, units), bf16),
             like((TEAM, rows, 2 * units), bf16),
             like(weight.shape, bf16),
+            like(next_units.shape, bf16),
         ),
-        in_specs=[anywhere] * 4,
-        out_specs=(anywhere, anywhere, vmem, vmem, vmem),
+        in_specs=[anywhere] * 5,
+        out_specs=(anywhere,) * 5,
+        input_output_aliases={4: 4},
         scratch_shapes=[
             pltpu.VMEM((TEAM, rows, width), bf16),
             pltpu.VMEM((TEAM, rows, width), bf16),
             pltpu.VMEM(weight.shape, bf16),
             pltpu.VMEM((units, width), bf16),
-            pltpu.VMEM((TEAM // 2, 2 * rows, 2 * units), f32),
+            pltpu.VMEM((2 * rows, 2 * units), f32),
             pltpu.VMEM(weight.shape, f32),
-            pltpu.SemaphoreType.DMA((28,)),
-            pltpu.SemaphoreType.DMA((28,)),
-            pltpu.SemaphoreType.DMA((12,)),
+            pltpu.VMEM((TEAM, rows, units), bf16),
+            pltpu.VMEM((TEAM, rows, 2 * units), bf16),
+            pltpu.VMEM(weight.shape, bf16),
+            pltpu.SemaphoreType.DMA((14 + 2 * (planes - 1),)),
+            pltpu.SemaphoreType.DMA((14 + 2 * (planes - 1),)),
+            pltpu.SemaphoreType.DMA((16 + width // TILE,)),
         ],
         compiler_params=params(collective, LIMIT),
         cost_estimate=pl.CostEstimate(
@@ -1220,7 +1296,7 @@
             bytes_accessed=8 * TEAM * rows * width,
             transcendentals=0,
         ),
-    )(two, cot, weight, down)
+    )(two, cot, weight, down, next_units)
 
 
 def feed_rest_kernel(two, cot, weight, down, act, grad_both):
@@ -1281,15 +1357,12 @@
     token_count, width = tokens.shape
     groups = QUERY_HEADS // KEY_VALUE_HEADS
     rows = w_query.shape[0]
-    parts = 2 if planes % 2 == 0 else 1
+    parts = 2
     team_rows = TEAM * token_count
     head_width = groups * HEAD_SIZE
     me = lax.axis_index("fsdp")
     plane = me // TEAM
 
-    def gather_line(x):
-        return lax.all_gather(x, "fsdp", axis=0, tiled=True, axis_index_groups=lines)
-
     def sum_line(x):
         return lax.psum_scatter(
             x, "fsdp", scatter_dimension=0, tiled=True, axis_index_groups=lines
@@ -1297,9 +1370,7 @@
 
     slot_live = (lax.broadcasted_iota(jnp.int32, (slots, 1), 0) < micro_live[0]).astype(f32)
     row_live = jnp.broadcast_to(slot_live, (slots, sequence)).reshape(token_count, 1)
-    cot_b = cotangent * row_live.astype(bf16)
-
-    down_weight = gather_line(w_down)
+
     smalls = [x[None] for x in (attn_gain, mlp_gain, query_norm_gain, key_gain)] + [segments]
     opened = opening(
         w_query,
@@ -1309,32 +1380,46 @@
         tokens,
         w_gate,
         w_up,
+        w_down,
         smalls,
         planes,
         parts,
         1,
     )
     unit_slices, opened = opened[:parts], opened[parts:]
-    qkv_weight, _, output_weight, team_tokens = opened[:4]
-    norm_gain, mlp_norm_gain, qgain, kgain, ids = opened[4:]
+    qkv_weight, _, output_weight, team_tokens, down_weight = opened[:5]
+    norm_gain, mlp_norm_gain, qgain, kgain, ids = opened[5:]
     mlp_norm_gain = mlp_norm_gain.reshape(width)
     qkv_weight = qkv_weight.reshape(width, -1)
     output_weight = output_weight.reshape(head_width, width)
-    unit_weights = [gather_line(x.reshape(TEAM * rows, -1)) for x in unit_slices]
+    down_weight = down_weight.reshape(-1, width)
     table = jnp.asarray(rotation_tables(sequence))
 
     inputs = tokens.astype(f32)
-    team_normed, raw, turned, value_b, context_b = attend(
-        team_tokens.reshape(team_rows, width), norm_gain, qkv_weight, ids, table, qgain, kgain
-    )
-    middle = inputs + team_sum(
-        context_b.reshape(TEAM, token_count, head_width), output_weight, 2
-    )
-
-    normed_two = root_mean_square_norm(middle, mlp_norm_gain).astype(bf16)
-    team_two, team_cot, act, grad_both, first_units = feed(
-        normed_two, cot_b, unit_weights[0], down_weight, 0
-    )
+    first, second = unit_slices
+    team_normed, raw, turned, value_b, context_b, middle, normed_two, team_cot, first = attend(
+        team_tokens.reshape(team_rows, width),
+        norm_gain,
+        qkv_weight,
+        ids,
+        table,
+        qgain,
+        kgain,
+        output_weight,
+        tokens,
+        cotangent,
+        row_live.astype(bf16),
+        mlp_norm_gain.reshape(1, width),
+        first,
+        planes,
+        2,
+    )
+
+    unit_weights = [first.reshape(width, -1)]
+    team_two, act, grad_both, first_units, second = feed(
+        normed_two, team_cot, unit_weights[0], down_weight, second, planes, 0
+    )
+    unit_weights.append(second.reshape(width, -1))
     acts, grads_both, grad_units = [act], [grad_both], [first_units]
     for k in range(1, parts):
         act, grad_both = feed_rest(team_two, team_cot, unit_weights[k], down_weight, k)
@@ -1344,7 +1429,7 @@
     grad_units = [sum_line(g) for g in (*grad_units, last_units)[:parts]]
     _, pull_two = jax.vjp(root_mean_square_norm, middle, mlp_norm_gain)
     middle_part, grad_mgain = pull_two(grad_normed_two)
-    grad_middle = cot_b.astype(f32) + middle_part
+    grad_middle = (cotangent * row_live.astype(bf16)).astype(f32) + middle_part
     team_grad, grad_down = gather_down(grad_middle.astype(bf16), team_cot, acts, 10)
     team_grad = team_grad.reshape(team_rows, width)
     grad_down = sum_line(grad_down)

time: 513 us -> 504 us (0.982)
  waiting for transfers between devices: 31.8 us -> 19.3 us
    all_gather x3 -> x0, waiting for transfers between devices: 8.39 us -> none  [gather_line(): lax.all_gather(x, 'fsdp', axis=0, tiled=True, axis_index_groups=lines)]
    pallas_call x3 -> x2, Pallas kernels: 113 us -> 116 us  [the longest x1 60.3 us: attend(): pl.pallas_call(functools.partial(attend_kernel, planes), out_shape=(*kept...]
  transfers between devices with their start and end apart: 7 -> 4, of which waited for: 4 -> 1; matrix products, arithmetic and copies ran while one was open for 5% -> 4% of each run, Pallas kernels for 85% -> 41%
where the time goes in v4:
time: 504 us; the launch traced here: 495 us
  Pallas kernels  433 us (86%)
  other arithmetic  19.3 us (4%)
  waiting for transfers between devices  19.3 us (4%)
  between operations  14.9 us (3%)
  local copies, waits for them, and re-layouts  7.86 us (2%)
    pallas_call x1, Pallas kernels, opening(): pl.pallas_call(functools.partial(open_kernel, planes, parts), out_shape=(...  115 us
    pallas_call x1, Pallas kernels, last_sums(): pl.pallas_call(functools.partial(last_sums_kernel, planes, parts), out_sh...  74.1 us
    pallas_call x1, Pallas kernels, attend(): pl.pallas_call(functools.partial(attend_kernel, planes), out_shape=(*kept...  60.3 us
    pallas_call x1, Pallas kernels, feed(): pl.pallas_call(functools.partial(feed_kernel, planes), out_shape=(like((T...  55.5 us
    pallas_call x1, Pallas kernels, feed_back(): pl.pallas_call(functools.partial(feed_back_kernel, parts), out_shape=(lik...  39.8 us
    pallas_call x1, Pallas kernels, gather_down(): pl.pallas_call(functools.partial(gather_down_kernel, parts), out_shape=(l...  33.3 us
    pallas_call x1, Pallas kernels, attend_back(): pl.pallas_call(functools.partial(attend_back_kernel, planes), out_shape=(...  28.7 us
    reduce_scatter x4, waiting for transfers between devices, sum_line(): lax.psum_scatter(x, 'fsdp', scatter_dimension=0, tiled=True, axis_index_g...  18.7 us
  transfers between devices with their start and end apart: 4, of which 1 were waited for; matrix products, arithmetic and copies ran while one was open for 4% of the time, Pallas kernels for 41%

profile of v4, /device:TPU:0, one launch (start us, length us, event | category | flops | bytes accessed | tf_op | source)
XLA Modules:
  0.0 494.9 jit_solution(16817055272514117277)
XLA Ops:
  8.0 0.8 convert_element_type.76.live
  8.7 114.7 %shard_map.255 = (bf16[4,8,64,768]{3,2,1,0:T(8,128)(2,1)}, bf16[4,8,64,768]{3,2,1,0:T(8,128)(2,1)}, bf16[4,8,64,512]{3,2,1,0:T(8,128)(2,1)}, bf16[4,64,2048]{2,1...) custom-call(bf16[64,2048]{1,0:T(8,128)(2,1)} %query_in.1, ...), custom_call_target="tpu_custom_call" | custom-call | tf_op jit(solution)/shard_map/pallas_call | solution.py:737
  123.4 60.3 %shard_map.256 = (bf16[1536,2048]{1,0:T(8,128)(2,1)}, f32[1536,384]{1,0:T(8,128)}, bf16[1536,384]{1,0:T(8,128)(2,1)}, bf16[1536,128]{1,0:T(8,128)(2,1)}, bf16[15...) custom-call(bf16[1536,2048]{1,0:T(8,128)(2,1)} %bitcast.50, ...), custom_call_target="tpu_custom_call", output_to_operand_aliasing={{8}: (12, {})} | custom-call | flops 4831838208 | bytes 25165824 | tf_op jit(solution)/shard_map/pallas_call | solution.py:990
  183.7 55.5 %shard_map.257 = (bf16[8,192,2048]{2,1,0:T(8,128)(2,1)}, bf16[8,192,384]{2,1,0:T(8,128)(2,1)}, bf16[8,192,768]{2,1,0:T(8,128)(2,1)}, bf16[2048,768]{1,0:T(8,128)(2,1)}, bf16[4,8,64,768]{3,2,1,0:T(8,128)(2,1)}) custom-call(bf16[192,2048]{1,0:T(8,128)(2,1)} %get-tuple-element.79.two_in, ...), custom_call_target="tpu_custom_call", output_to_operand_aliasing={{4}: (4, {})} | custom-call | flops 12079595520 | bytes 25165824 | tf_op jit(solution)/shard_map/pallas_call | solution.py:1267
  239.2 13.2 %shard_map.258 = (bf16[8,192,384]{2,1,0:T(8,128)(2,1)}, bf16[8,192,768]{2,1,0:T(8,128)(2,1)}) custom-call(bf16[8,192,2048]{2,1,0:T(8,128)(2,1)} %get-tuple-element.84.two, bf16[8,192,2048]{2,1,0:T(8,128)(2,1)} %get-tuple-element.80.cot_in.cot, bf16[2048,768]{1,0:T(8,128)(2,1)} %bitcast.54, bf16[768,2048]{1,0:T(8,128)(2,1)} %bitcast.52), custom_call_target="tpu_custom_call" | custom-call | flops 7247757312 | bytes 12582912 | tf_op jit(solution)/shard_map/pallas_call | solution.py:1316
  252.5 39.8 %shard_map.259 = (f32[192,2048]{1,0:T(8,128)}, bf16[2048,768]{1,0:T(8,128)(2,1)}) custom-call(bf16[8,192,2048]{2,1,0:T(8,128)(2,1)} %get-tuple-element.84.two, bf16[8,192,768]{2,1,0:T(8,128)(2,1)} %get-tuple-element.85.refs_0_, bf16[8,192,768]{2,1,0:T(8,128)(2,1)} %get-tuple-element.87.refs_1_, bf16[2048,768]{1,0:T(8,128)(2,1)} %bitcast.57, ...), custom_call_target="tpu_custom_call" | custom-call | flops 14495514624 | bytes 11010048 | tf_op jit(solution)/shard_map/pallas_call | solution.py:393
  292.6 1.2 copy-done
  295.4 1.9 fusion.11
  297.3 33.3 %shard_map.260 = (bf16[8,192,2048]{2,1,0:T(8,128)(2,1)}, bf16[768,2048]{1,0:T(8,128)(2,1)}) custom-call(bf16[192,2048]{1,0:T(8,128)(2,1)} %get-tuple-element.133.x, bf16[8,192,2048]{2,1,0:T(8,128)(2,1)} %get-tuple-element.80.cot_in.cot, bf16[8,192,384]{2,1,0:T(8,128)(2,1)} %get-tuple-element.90.refs_0_, bf16[8,192,384]{2,1,0:T(8,128)(2,1)} %get-tuple-element.91.refs_1_), custom_call_target="tpu_custom_call" | custom-call | flops 4831838208 | bytes 18874368 | tf_op jit(solution)/shard_map/pallas_call | solution.py:455
  330.7 28.7 %shard_map.261 = (bf16[1536,512]{1,0:T(8,128)(2,1)}, bf16[4,768,512]{2,1,0:T(8,128)(2,1)}, f32[8,128]{1,0:T(8,128)}) custom-call(bf16[1536,2048]{1,0:T(8,128)(2,1)} %bitcast.64, bf16[256,2048]{1,0:T(8,128)(2,1)} %bitcast.61, bf16[1536,256]{1,0:T(8,128)(2,1)} %get-tuple-element.93.context, f32[1536,384]{1,0:T(8,128)} %get-tuple-element.94.raw_in, ...), custom_call_target="tpu_custom_call" | custom-call | flops 6442450944 | bytes 25165824 | tf_op jit(solution)/shard_map/pallas_call | solution.py:1148
  360.0 0.8 slice_reduce_fusion.1
  361.4 74.1 %shard_map.262 = (f32[192,2048]{1,0:T(8,128)}, f32[192,2048]{1,0:T(8,128)}, bf16[64,6144]{1,0:T(8,128)(2,1)}, bf16[64,6144]{1,0:T(8,128)(2,1)}) custom-call(bf16[8,192,512]{2,1,0:T(8,128)(2,1)} %bitcast.65, bf16[2048,512]{1,0:T(8,128)(2,1)} %bitcast.59, bf16[768,2048]{1,0:T(8,128)(2,1)} %bitcast.53, bf16[8,192,384]{2,1,0:T(8,128)(2,1)} %get-tuple-element.90.refs_0_, ...), custom_call_target="tpu_custom_call" | custom-call | flops 8053063680 | bytes 3145728 | tf_op jit(solution)/shard_map/pallas_call | solution.py:533
  435.5 1.9 fusion.6
  438.3 2.4 convert_element_type.66
  440.7 1.2 convert_element_type.67
  442.7 1.2 multiply_convert_fusion
  444.9 1.4 fusion.2
  446.2 13.8 %shard_map.263 = (bf16[64,2048]{1,0:T(8,128)(2,1)}, bf16[64,1024]{1,0:T(8,128)(2,1)}, bf16[64,1024]{1,0:T(8,128)(2,1)}, bf16[64,2048]{1,0:T(8,128)(2,1)}, f32[8,128]{1,0:T(8,128)}) custom-call(bf16[768,512]{1,0:T(8,128)(2,1)} %reduce-scatter.5.cloned.1.call-done.x_ref, f32[8,4,8,128]{3,2,1,0:T(8,128)} %bitcast.41), custom_call_target="tpu_custom_call" | custom-call | tf_op jit(solution)/shard_map/pallas_call | solution.py:826
  460.1 1.8 convert_element_type.71
  461.9 1.6 convert_element_type.72
  463.5 1.6 convert_element_type.73
  465.2 0.8 convert_element_type.74
  467.0 18.7 %reduce-scatter.11.cloned.1.call-done = bf16[192,2048]{1,0:T(8,128)(2,1)} async-done(((bf16[768,2048]{1,0:T(8,128)(2,1)}), bf16[192,2048]{1,0:T(8,128)(2,1)}) %reduce-scatter.11.cloned.1.call-update) | async-done | bytes 786448 | tf_op jit(solution)/shard_map/reduce_scatter | solution.py:1367
  485.7 2.5 convert_element_type.75
  (58 shorter events, 6.8 us)
Async XLA Ops:
  7.2 354.2 %reduce-scatter.7.cloned.1.call-start = ((), (), s32[]{:S(2)}) async-start(), calls=%async_computation.5 | async-start | bytes 3932160 | tf_op jit(solution)/shard_map/reduce_scatter | solution.py:1367
  239.2 122.2 %reduce-scatter.9.cloned.1.call-start = ((), (), s32[]{:S(2)}) async-start(), calls=%async_computation.6 | async-start | bytes 3932160 | tf_op jit(solution)/shard_map/reduce_scatter | solution.py:1367
  292.3 1.4 copy-start
  292.3 1.9 copy-start.4
  292.3 1.9 copy-start.10
  292.3 153.9 %reduce-scatter.5.cloned.1.call-start = ((), (), s32[]{:S(2)}) async-start(), calls=%async_computation.4 | async-start | bytes 3932160 | tf_op jit(solution)/shard_map/reduce_scatter | solution.py:1367
  294.3 1.1 copy-start.6
  359.4 126.3 %reduce-scatter.11.cloned.1.call-start = ((), (), s32[]{:S(2)}) async-start(), calls=%async_computation.7 | async-start | bytes 3932160 | tf_op jit(solution)/shard_map/reduce_scatter | solution.py:1367
  359.4 1.6 copy-start.1
  361.4 74.2 %copy-start.9 = (f32[1,2048]{1,0:T(1,128)S(1)}, f32[1,2048]{1,0:T(1,128)}, u32[]{:S(2)}) copy-start(f32[1,2048]{1,0:T(1,128)} %get-tuple-element.71.gain) | copy-start | bytes 24580
  437.5 3.2 copy-start.7
  440.7 2.0 copy-start.5
  442.7 1.7 copy-start.2
  442.7 2.2 copy-start.3
  460.1 5.1 %copy-start.8 = (bf16[64,2048]{1,0:T(8,128)(2,1)S(1)}, bf16[64,2048]{1,0:T(8,128)(2,1)}, u32[]{:S(2)}) copy-start(bf16[64,2048]{1,0:T(8,128)(2,1)} %get-tuple-element.114) | copy-start | bytes 786436
  460.1 5.9 %copy-start.11 = (f32[8,128]{1,0:T(8,128)S(1)}, f32[8,128]{1,0:T(8,128)}, u32[]{:S(2)}) copy-start(f32[8,128]{1,0:T(8,128)} %get-tuple-element.115) | copy-start | bytes 12292
Sparse Core Ops, SparseCore 0:
  239.3 58.4 reduce-scatter.6
  300.1 60.2 reduce-scatter.8
  362.7 60.2 reduce-scatter.4
  425.2 60.4 reduce-scatter.10

commit v5 on v4

--- a/solution.py
+++ b/solution.py
@@ -473,12 +473,12 @@
     )(x, cot, *acts)
 
 
-def last_sums_kernel(planes, parts, grad_qkv, qkv_weight, down, *refs):
+def last_sums_kernel(planes, parts, grad_qkv, qkv_weight, down, out_blocks, before, *refs):
     acts, units, refs = refs[:parts], refs[parts : 2 * parts], refs[2 * parts :]
-    grad_normed, layer, gate, up, refs = *refs[:4], refs[4:]
+    grad_normed, layer, gate, up, output, after, *refs = refs
     first, second, refs = refs[:4], refs[4:8], refs[8:]
     acts_here, downs_here, refs = refs[:parts], refs[parts : 2 * parts], refs[2 * parts :]
-    grad_here, weight_here, landed, send, receive, own = refs
+    grad_here, weight_here, landed, mine, there, sems, out_sum, send, receive, own = refs
     me = lax.axis_index("fsdp")
     place = lax.rem(me, TEAM)
     loader = Loader(own)
@@ -488,8 +488,10 @@
         loader(units[k].at[place], landed.at[k, place])
         loader(acts[k], acts_here[k])
         loader(rows_of(down, k, downs_here[k].shape[0]), downs_here[k])
-    greet(me, range(1, TEAM))
+    greet(me, range(1, TEAM), line_peers(me, planes))
     sender = Sender(send, receive)
+    line = LineSum(sender, out_blocks, before.at[0], after, mine, there, sems, planes, me, 1)
+    line.start(0)
     moves = [
         sender(units[k].at[flipped(place, m)], landed.at[k, place], flipped(me, m))
         for k in range(parts)
@@ -503,6 +505,9 @@
     two.start()
     one.relay()
     two.own()
+    line.wait(0)
+    if planes > 3:
+        line.start(1)
     two.relay()
     for copy in moves:
         copy.wait_recv()
@@ -517,10 +522,18 @@
             )
     one.finish()
     two.finish()
+    for k in range(1, planes - 2):
+        if k > 1:
+            line.start(k)
+        line.wait(k)
+    line.total(out_sum)
+    width, rows = out_sum.shape[1], output.shape[0]
+    for c in range(output.shape[1] // width):
+        output[:, c * width : (c + 1) * width] = out_sum[c * rows : (c + 1) * rows]
     sender.finish()
 
 
-def last_sums(grad_qkv, qkv_weight, acts, down, units, planes, collective):
+def last_sums(grad_qkv, qkv_weight, acts, down, units, out_blocks, before, planes, collective):
     _, rows, depth = grad_qkv.shape
     width = qkv_weight.shape[0]
     parts = len(acts)
@@ -528,13 +541,17 @@
     vmem = pl.BlockSpec(memory_space=pltpu.VMEM)
     like = jax.ShapeDtypeStruct
     _, own_rows, some = units[0].shape
-    links = 2 * SUM_COPIES + (TEAM - 1) * parts
+    steps = planes - 2
+    links = 2 * SUM_COPIES + (TEAM - 1) * parts + 2 * steps
+    _, block, block_width = out_blocks.shape
     home = like((own_rows, TEAM * parts * some // 2), bf16)
     return pl.pallas_call(
         functools.partial(last_sums_kernel, planes, parts),
-        out_shape=(like((rows, width), f32),) * 2 + (home,) * 2,
-        in_specs=[anywhere] * (3 + 2 * parts),
-        out_specs=(vmem,) * 4,
+        out_shape=(like((rows, width), f32),) * 2
+        + (home,) * 2
+        + (like((own_rows, width), f32), like((steps, 2, block, block_width), bf16),),
+        in_specs=[anywhere] * (5 + 2 * parts),
+        out_specs=(vmem,) * 5 + (anywhere,),
         scratch_shapes=[
             *sum_buffers(rows, width),
             *sum_buffers(rows, width),
@@ -543,6 +560,8 @@
             pltpu.VMEM(grad_qkv.shape, bf16),
             pltpu.VMEM(qkv_weight.shape, bf16),
             pltpu.VMEM((parts, *units[0].shape), bf16),
+            *line_scratch(block, block_width),
+            pltpu.VMEM((block, block_width), f32),
             pltpu.SemaphoreType.DMA((links,)),
             pltpu.SemaphoreType.DMA((links,)),
             pltpu.SemaphoreType.DMA((2 + 3 * parts,)),
@@ -553,7 +572,116 @@
             bytes_accessed=4 * TEAM * rows * depth,
             transcendentals=0,
         ),
-    )(grad_qkv, qkv_weight, down, *acts, *units)
+    )(grad_qkv, qkv_weight, down, out_blocks, before, *acts, *units)
+
+
+class LineSum:
+    def __init__(self, sender, own, before, after, mine, there, sems, planes, me, first):
+        self.sender, self.own, self.before, self.after = sender, own, before, after
+        self.mine, self.there, self.sems = mine, there, sems
+        self.planes, self.me, self.first = planes, me, first
+        self.plane = lax.div(me, TEAM)
+        self.flows = [(sign, [sender.take() for _ in range(after.shape[0])]) for sign in (1, -1)]
+
+    def rank(self, sign):
+        return self.plane if sign > 0 else self.planes - 1 - self.plane
+
+    def block(self, sign, step):
+        rank = jnp.clip(self.planes - 1 - (step - self.rank(sign)), 0, self.planes - 1)
+        return rank if sign > 0 else self.planes - 1 - rank
+
+    def sends(self, sign, step):
+        rank = self.rank(sign)
+        return (rank <= step) & (rank < self.planes - 1)
+
+    def comes(self, sign, step):
+        rank = self.rank(sign)
+        return (rank >= 1) & (rank - 1 <= step)
+
+    def copy(self, sign, k):
+        d = 0 if sign > 0 else 1
+        beyond = jnp.clip(self.plane + sign, 0, self.planes - 1) * TEAM + lax.rem(self.me, TEAM)
+        sem = dict((sign, ks[k]) for sign, ks in self.flows)[sign]
+        target = self.after.at[k, d]
+        send, receive = self.sender.send.at[sem], self.sender.receive.at[sem]
+        return remote(self.mine.at[d], target, send, receive, beyond)
+
+    def start(self, k):
+        step = self.first + k
+        for d, (sign, _) in enumerate(self.flows):
+
+            @pl.when(self.sends(sign, step))
+            def _():
+                load = pltpu.make_async_copy(
+                    self.own.at[self.block(sign, step)], self.mine.at[d], self.sems.at[0]
+                )
+                load.start()
+                load.wait()
+                if step > 0:
+
+                    @pl.when(self.rank(sign) >= 1)
+                    def _():
+                        source = self.after.at[k - 1, d] if k else self.before.at[d]
+                        load = pltpu.make_async_copy(source, self.there, self.sems.at[1])
+                        load.start()
+                        load.wait()
+                        self.add(d)
+
+                self.copy(sign, k).start()
+
+    def add(self, d):
+        @pl.loop(0, self.there.shape[0] // STRIP)
+        def _(i):
+            at = pl.ds(i * STRIP, STRIP)
+            self.mine[d, at, :] = (
+                self.mine[d, at, :].astype(f32) + self.there[at, :].astype(f32)
+            ).astype(bf16)
+
+    def wait(self, k):
+        step = self.first + k
+        for sign, _ in self.flows:
+            copy = self.copy(sign, k)
+            pl.when(self.sends(sign, step))(copy.wait_send)
+            pl.when(self.comes(sign, step))(copy.wait_recv)
+
+    def rest(self):
+        for k in range(self.after.shape[0]):
+            if k:
+                self.start(k)
+            self.wait(k)
+
+    def total(self, out):
+        load = pltpu.make_async_copy(self.own.at[self.plane], self.mine.at[0], self.sems.at[0])
+        load.start()
+        load.wait()
+
+        @pl.loop(0, out.shape[0] // STRIP)
+        def _(i):
+            at = pl.ds(i * STRIP, STRIP)
+            out[at, :] = self.mine[0, at, :].astype(f32)
+
+        for d, (sign, _) in enumerate(self.flows):
+
+            @pl.when(self.rank(sign) >= 1)
+            def _():
+                load = pltpu.make_async_copy(
+                    self.after.at[self.after.shape[0] - 1, d], self.there, self.sems.at[1]
+                )
+                load.start()
+                load.wait()
+
+                @pl.loop(0, out.shape[0] // STRIP)
+                def _(i):
+                    at = pl.ds(i * STRIP, STRIP)
+                    out[at, :] = out[at, :] + self.there[at, :].astype(f32)
+
+
+def line_scratch(rows, width):
+    return [
+        pltpu.VMEM((2, rows, width), bf16),
+        pltpu.VMEM((rows, width), bf16),
+        pltpu.SemaphoreType.DMA((2,)),
+    ]
 
 
 SWAP_ORDER = (6, 7, 2, 3, 4, 5, 1)
@@ -761,8 +889,8 @@
 
 
 def close_kernel(planes, x_ref, gains, *refs):
-    query_ref, key_ref, value_ref, output_ref, gain_ref, *refs = refs
-    landed, mine, near_in, mid, far_in, send, receive, own = refs
+    query_ref, key_ref, value_ref, gain_ref, *refs = refs
+    landed, near_in, mid, far_in, send, receive, own = refs
     me = lax.axis_index("fsdp")
     place = lax.rem(me, TEAM)
     plane = lax.div(me, TEAM)
@@ -774,10 +902,6 @@
 
     keep = pltpu.make_async_copy(part(place), landed.at[place], own.at[0])
     keep.start()
-    keep_mine = pltpu.make_async_copy(
-        x_ref.at[pl.ds(TEAM * rows, mine.shape[0])], mine, own.at[1]
-    )
-    keep_mine.start()
     greet(me, range(1, TEAM), others)
     sender = Sender(send, receive)
     near = [
@@ -796,10 +920,6 @@
         sender(mid.at[lax.rem(plane + k + 1, planes)], far_in.at[k], other)
         for k, other in enumerate(others)
     ]
-    keep_mine.wait()
-    width = mine.shape[1]
-    for c in range(output_ref.shape[1] // width):
-        output_ref[:, c * width : (c + 1) * width] = mine[c * rows : (c + 1) * rows]
     for copy in moves:
         copy.wait_recv()
     keep.wait()
@@ -827,10 +947,9 @@
         functools.partial(close_kernel, planes),
         out_shape=(*(like((rows, w), bf16) for w in widths), like(block, f32)),
         in_specs=[pl.BlockSpec(memory_space=pl.ANY), vmem],
-        out_specs=(vmem,) * 5,
+        out_specs=(vmem,) * 4,
         scratch_shapes=[
             pltpu.VMEM((TEAM, rows, x.shape[1]), x.dtype),
-            pltpu.VMEM((x.shape[0] - TEAM * rows, x.shape[1]), x.dtype),
             pltpu.VMEM((TEAM - 1, planes, *block), f32),
             pltpu.VMEM((planes, *block), f32),
             pltpu.VMEM((planes - 1, *block), f32),
@@ -1021,7 +1140,8 @@
 
 
 def attend_back_kernel(planes, grad_in, out_weight, context, raw_in, turned_in, value_in, normed_in,
-    ids_row, table, query_gain, key_gain, grad_raw_ref, merged, grad_gains_ref,
+    ids_row, table, query_gain, key_gain, grad_raw_ref, weight_out, merged, grad_gains_ref, after,
+    mine, there, sems,
     grad_ref, raw_ref, turned_ref, value_ref, normed_ref, out_sum, weight_sum, send, receive, own,
 ):
     me = lax.axis_index("fsdp")
@@ -1033,7 +1153,7 @@
         (raw_in, raw_ref), (turned_in, turned_ref), (value_in, value_ref), (normed_in, normed_ref)
     ):
         loader(source, target)
-    greet(me, range(1, TEAM))
+    greet(me, range(1, TEAM), line_peers(me, planes))
     loader.copies[0].wait()
 
     total, width = grad_ref.shape
@@ -1046,7 +1166,7 @@
         return out_sum.at[pl.ds(k * block, block), pl.ds(c * out, out)]
 
     def target(k, c):
-        return merged.at[k, pl.ds(rows + c * block, block)]
+        return merged.at[k, pl.ds(c * block, block)]
 
     def outgoing(k, c):
         number = planes * place + k
@@ -1108,20 +1228,6 @@
         parts.append(grad_value.astype(bf16))
         grad_raw_ref[here, :] = jnp.concatenate(parts, axis=1)
 
-    @pl.loop(0, planes)
-    def _(g):
-        at = pl.ds(pl.multiple_of(g * rows, rows), rows)
-        weight_sum[at, :] = dot_first(normed_ref[:, at], grad_raw_ref[...]).astype(bf16)
-
-    homes = []
-    for g in range(planes):
-        copy = pltpu.make_async_copy(
-            weight_sum.at[pl.ds(g * rows, rows)],
-            merged.at[g, pl.ds(0, rows)],
-            own.at[5 + planes * cuts + g],
-        )
-        copy.start()
-        homes.append(copy)
     for k in range(planes):
         for c in range(cuts):
             partner, over, here = outgoing(k, c)
@@ -1129,6 +1235,26 @@
             pl.when(partner == place)(here.wait)
             partner, arriving = incoming(k, c)
             pl.when(partner != place)(arriving.wait_recv)
+    sender = Sender(send, receive)
+    sender.count = planes * cuts
+    line = LineSum(sender, merged, None, after, mine, there, sems, planes, me, 0)
+    line.start(0)
+
+    @pl.loop(0, planes)
+    def _(g):
+        at = pl.ds(pl.multiple_of(g * rows, rows), rows)
+        weight_sum[at, :] = dot_first(normed_ref[:, at], grad_raw_ref[...]).astype(bf16)
+
+    homes = []
+    for g in range(planes):
+        copy = pltpu.make_async_copy(
+            weight_sum.at[pl.ds(g * rows, rows)],
+            weight_out.at[g],
+            own.at[5 + planes * cuts + g],
+        )
+        copy.start()
+        homes.append(copy)
+    line.wait(0)
     for copy in homes:
         copy.wait()
 
@@ -1140,22 +1266,30 @@
     rows, width = grad.shape
     heads = context.shape[1]
     out = heads + 2 * HEAD_SIZE
-    merged = (planes, (width + heads * width // out) // planes, out)
+    by_plane = (planes, width // planes, out)
+    merged = (planes, heads * width // out // planes, out)
     copies = planes * (width // out)
     anywhere = pl.BlockSpec(memory_space=pl.ANY)
     vmem = pl.BlockSpec(memory_space=pltpu.VMEM)
     like = jax.ShapeDtypeStruct
     return pl.pallas_call(
         functools.partial(attend_back_kernel, planes),
-        out_shape=(like((rows, out), bf16), like(merged, bf16), like((8, HEAD_SIZE), f32)),
+        out_shape=(
+            like((rows, out), bf16),
+            like(by_plane, bf16),
+            like(merged, bf16),
+            like((8, HEAD_SIZE), f32),
+            like((1, 2, *merged[1:]), bf16),
+        ),
         in_specs=[anywhere, vmem, vmem] + [anywhere] * 4 + [vmem] * 4,
-        out_specs=(vmem, anywhere, vmem),
+        out_specs=(vmem, anywhere, anywhere, vmem, anywhere),
         scratch_shapes=[
+            *line_scratch(*merged[1:]),
             *(pltpu.VMEM(x.shape, x.dtype) for x in (grad, raw, turned, value, normed)),
             pltpu.VMEM((heads, width), bf16),
             pltpu.VMEM((width, out), bf16),
-            pltpu.SemaphoreType.DMA((copies,)),
-            pltpu.SemaphoreType.DMA((copies,)),
+            pltpu.SemaphoreType.DMA((copies + 2,)),
+            pltpu.SemaphoreType.DMA((copies + 2,)),
             pltpu.SemaphoreType.DMA((5 + copies + planes,)),
         ],
         compiler_params=params(collective, LIMIT),
@@ -1434,7 +1568,7 @@
     team_grad = team_grad.reshape(team_rows, width)
     grad_down = sum_line(grad_down)
 
-    grad_qkv, grad_attention, grad_head_gains = attend_back(
+    grad_qkv, grad_attention, out_blocks, grad_head_gains, out_line = attend_back(
         team_grad,
         output_weight,
         context_b,
@@ -1450,12 +1584,14 @@
         6,
     )
     grad_attention = sum_line(grad_attention.reshape(-1, grad_attention.shape[2]))
-    grad_normed, summed_out, grad_gate, grad_up = last_sums(
+    grad_normed, summed_out, grad_gate, grad_up, grad_output, _ = last_sums(
         grad_qkv.reshape(TEAM, token_count, -1),
         qkv_weight,
         acts,
         down_weight,
         [g.reshape(TEAM, rows, -1) for g in grad_units],
+        out_blocks,
+        out_line,
         planes,
         5,
     )
@@ -1478,11 +1614,11 @@
     grad_attention, grad_gate, grad_up, layer_out, grad_tokens = lax.optimization_barrier(
         (grad_attention, grad_gate, grad_up, layer_out, grad_tokens)
     )
-    grad_query, grad_key, grad_value_w, grad_output, gains = closing(
+    grad_query, grad_key, grad_value_w, gains = closing(
         grad_attention,
         gains,
         rows,
-        (w_query.shape[1], key_weight.shape[1], value_weight.shape[1], width),
+        (w_query.shape[1], key_weight.shape[1], value_weight.shape[1]),
         planes,
         9,
     )

time: 504 us -> 503 us (level)
  waiting for transfers between devices: 19.3 us -> 2.93 us
  Pallas kernels: 433 us -> 448 us
    reduce_scatter x4, waiting for transfers between devices: 18.7 us -> 2.37 us  [sum_line(): lax.psum_scatter(x, 'fsdp', scatter_dimension=0, tiled=True, axis_index_g...]
    pallas_call x1, Pallas kernels: 74.1 us -> 81.4 us  [last_sums(): pl.pallas_call(functools.partial(last_sums_kernel, planes, parts), out_sh...]
  transfers between devices with their start and end apart: 4 -> 4, of which waited for: 1 -> 1; matrix products, arithmetic and copies ran while one was open for 4% -> 4% of each run, Pallas kernels for 41% -> 44%
where the time goes in v5:
time: 503 us; the launch traced here: 493 us
  Pallas kernels  448 us (89%)
  other arithmetic  18.5 us (4%)
  between operations  14.9 us (3%)
  local copies, waits for them, and re-layouts  8.63 us (2%)
    pallas_call x1, Pallas kernels, opening(): pl.pallas_call(functools.partial(open_kernel, planes, parts), out_shape=(...  115 us
    pallas_call x1, Pallas kernels, last_sums(): pl.pallas_call(functools.partial(last_sums_kernel, planes, parts), out_sh...  81.4 us
    pallas_call x1, Pallas kernels, attend(): pl.pallas_call(functools.partial(attend_kernel, planes), out_shape=(*kept...  60.3 us
    pallas_call x1, Pallas kernels, feed(): pl.pallas_call(functools.partial(feed_kernel, planes), out_shape=(like((T...  55.5 us
    pallas_call x1, Pallas kernels, feed_back(): pl.pallas_call(functools.partial(feed_back_kernel, parts), out_shape=(lik...  39.8 us
    pallas_call x1, Pallas kernels, attend_back(): pl.pallas_call(functools.partial(attend_back_kernel, planes), out_shape=(...  33.7 us
    pallas_call x1, Pallas kernels, gather_down(): pl.pallas_call(functools.partial(gather_down_kernel, parts), out_shape=(l...  33.3 us
    pallas_call x1, Pallas kernels, closing(): pl.pallas_call(functools.partial(close_kernel, planes), out_shape=(*(like...  16.2 us
  transfers between devices with their start and end apart: 4, of which 1 were waited for; matrix products, arithmetic and copies ran while one was open for 4% of the time, Pallas kernels for 44%

profile of v5, /device:TPU:0, one launch (start us, length us, event | category | flops | bytes accessed | tf_op | source)
XLA Modules:
  0.0 493.3 jit_solution(9938232818294667097)
XLA Ops:
  8.0 0.8 convert_element_type.72.live
  8.7 114.7 %shard_map.255 = (bf16[4,8,64,768]{3,2,1,0:T(8,128)(2,1)}, bf16[4,8,64,768]{3,2,1,0:T(8,128)(2,1)}, bf16[4,8,64,512]{3,2,1,0:T(8,128)(2,1)}, bf16[4,64,2048]{2,1...) custom-call(bf16[64,2048]{1,0:T(8,128)(2,1)} %query_in.1, ...), custom_call_target="tpu_custom_call" | custom-call | tf_op jit(solution)/shard_map/pallas_call | solution.py:865
  123.4 60.3 %shard_map.256 = (bf16[1536,2048]{1,0:T(8,128)(2,1)}, f32[1536,384]{1,0:T(8,128)}, bf16[1536,384]{1,0:T(8,128)(2,1)}, bf16[1536,128]{1,0:T(8,128)(2,1)}, bf16[15...) custom-call(bf16[1536,2048]{1,0:T(8,128)(2,1)} %bitcast.50, ...), custom_call_target="tpu_custom_call", output_to_operand_aliasing={{8}: (12, {})} | custom-call | flops 4831838208 | bytes 25165824 | tf_op jit(solution)/shard_map/pallas_call | solution.py:1109
  183.7 55.5 %shard_map.257 = (bf16[8,192,2048]{2,1,0:T(8,128)(2,1)}, bf16[8,192,384]{2,1,0:T(8,128)(2,1)}, bf16[8,192,768]{2,1,0:T(8,128)(2,1)}, bf16[2048,768]{1,0:T(8,128)(2,1)}, bf16[4,8,64,768]{3,2,1,0:T(8,128)(2,1)}) custom-call(bf16[192,2048]{1,0:T(8,128)(2,1)} %get-tuple-element.81.two_in, ...), custom_call_target="tpu_custom_call", output_to_operand_aliasing={{4}: (4, {})} | custom-call | flops 12079595520 | bytes 25165824 | tf_op jit(solution)/shard_map/pallas_call | solution.py:1401
  239.3 13.2 %shard_map.258 = (bf16[8,192,384]{2,1,0:T(8,128)(2,1)}, bf16[8,192,768]{2,1,0:T(8,128)(2,1)}) custom-call(bf16[8,192,2048]{2,1,0:T(8,128)(2,1)} %get-tuple-element.86.two, bf16[8,192,2048]{2,1,0:T(8,128)(2,1)} %get-tuple-element.82.cot_in.cot, bf16[2048,768]{1,0:T(8,128)(2,1)} %bitcast.54, bf16[768,2048]{1,0:T(8,128)(2,1)} %bitcast.52), custom_call_target="tpu_custom_call" | custom-call | flops 7247757312 | bytes 12582912 | tf_op jit(solution)/shard_map/pallas_call | solution.py:1450
  252.5 39.8 %shard_map.259 = (f32[192,2048]{1,0:T(8,128)}, bf16[2048,768]{1,0:T(8,128)(2,1)}) custom-call(bf16[8,192,2048]{2,1,0:T(8,128)(2,1)} %get-tuple-element.86.two, bf16[8,192,768]{2,1,0:T(8,128)(2,1)} %get-tuple-element.87.refs_0_, bf16[8,192,768]{2,1,0:T(8,128)(2,1)} %get-tuple-element.89.refs_1_, bf16[2048,768]{1,0:T(8,128)(2,1)} %bitcast.57, ...), custom_call_target="tpu_custom_call" | custom-call | flops 14495514624 | bytes 11010048 | tf_op jit(solution)/shard_map/pallas_call | solution.py:393
  292.6 1.2 copy-done
  295.4 1.9 fusion.11
  297.3 33.3 %shard_map.260 = (bf16[8,192,2048]{2,1,0:T(8,128)(2,1)}, bf16[768,2048]{1,0:T(8,128)(2,1)}) custom-call(bf16[192,2048]{1,0:T(8,128)(2,1)} %get-tuple-element.137.x, bf16[8,192,2048]{2,1,0:T(8,128)(2,1)} %get-tuple-element.82.cot_in.cot, bf16[8,192,384]{2,1,0:T(8,128)(2,1)} %get-tuple-element.92.refs_0_, bf16[8,192,384]{2,1,0:T(8,128)(2,1)} %get-tuple-element.93.refs_1_), custom_call_target="tpu_custom_call" | custom-call | flops 4831838208 | bytes 18874368 | tf_op jit(solution)/shard_map/pallas_call | solution.py:455
  330.7 33.7 %shard_map.261 = (bf16[1536,512]{1,0:T(8,128)(2,1)}, bf16[4,512,512]{2,1,0:T(8,128)(2,1)}, bf16[4,256,512]{2,1,0:T(8,128)(2,1)}, f32[8,128]{1,0:T(8,128)}, bf16[1,2,256,512]{3,2,1,0:T(8,128)(2,1)}) custom-call(bf16[1536,2048]{1,0:T(8,128)(2,1)} %bitcast.64, bf16[256,2048]{1,0:T(8,128)(2,1)} %bitcast.61, bf16[1536,256]{1,0:T(8,128)(2,1)} %get-tuple-element.95.context, ...), custom_call_target="tpu_custom_call" | custom-call | flops 6442450944 | bytes 25165824 | tf_op jit(solution)/shard_map/pallas_call | solution.py:1275
  365.1 0.8 slice_reduce_fusion.1
  366.4 81.4 %shard_map.262 = (f32[192,2048]{1,0:T(8,128)}, f32[192,2048]{1,0:T(8,128)}, bf16[64,6144]{1,0:T(8,128)(2,1)}, bf16[64,6144]{1,0:T(8,128)(2,1)}, f32[64,2048]{1,0:T(8,128)}, /*index=5*/bf16[2,2,256,512]{3,2,1,0:T(8,128)(2,1)}) custom-call(bf16[8,192,512]{2,1,0:T(8,128)(2,1)} %bitcast.65, bf16[2048,512]{1,0:T(8,128)(2,1)} %bitcast.59, ...), custom_call_target="tpu_custom_call" | custom-call | flops 8053063680 | bytes 3145728 | tf_op jit(solution)/shard_map/pallas_call | solution.py:548
  447.9 1.9 fusion.6
  450.6 2.4 convert_element_type.63
  453.0 1.2 convert_element_type.64
  455.0 1.2 multiply_convert_fusion
  457.2 1.4 fusion.2
  458.6 16.2 %shard_map.263 = (bf16[64,2048]{1,0:T(8,128)(2,1)}, bf16[64,1024]{1,0:T(8,128)(2,1)}, bf16[64,1024]{1,0:T(8,128)(2,1)}, f32[8,128]{1,0:T(8,128)}) custom-call(bf16[512,512]{1,0:T(8,128)(2,1)} %reduce-scatter.5.cloned.1.call-done.x_ref, f32[8,4,8,128]{3,2,1,0:T(8,128)} %bitcast.41), custom_call_target="tpu_custom_call" | custom-call | tf_op jit(solution)/shard_map/pallas_call | solution.py:946
  474.8 1.8 convert_element_type.68
  476.6 1.7 convert_element_type.69
  478.3 1.6 convert_element_type.70
  480.9 2.3 reduce-scatter.11.cloned.1.call-done
  483.3 2.5 convert_element_type.71
  485.7 0.8 copy.42
  (58 shorter events, 6.8 us)
Async XLA Ops:
  7.2 359.2 %reduce-scatter.7.cloned.1.call-start = ((), (), s32[]{:S(2)}) async-start(), calls=%async_computation.5 | async-start | bytes 3932160 | tf_op jit(solution)/shard_map/reduce_scatter | solution.py:1501
  239.2 127.2 %reduce-scatter.9.cloned.1.call-start = ((), (), s32[]{:S(2)}) async-start(), calls=%async_computation.6 | async-start | bytes 3932160 | tf_op jit(solution)/shard_map/reduce_scatter | solution.py:1501
  292.3 1.4 copy-start
  292.3 1.9 copy-start.4
  292.3 1.9 copy-start.10
  292.4 166.2 %reduce-scatter.5.cloned.1.call-start = ((), (), s32[]{:S(2)}) async-start(), calls=%async_computation.4 | async-start | bytes 2621440 | tf_op jit(solution)/shard_map/reduce_scatter | solution.py:1501
  294.3 1.1 copy-start.6
  364.4 118.9 %reduce-scatter.11.cloned.1.call-start = ((), (), s32[]{:S(2)}) async-start(), calls=%async_computation.7 | async-start | bytes 3932160 | tf_op jit(solution)/shard_map/reduce_scatter | solution.py:1501
  364.5 1.6 copy-start.1
  366.4 81.5 %copy-start.9 = (f32[1,2048]{1,0:T(1,128)S(1)}, f32[1,2048]{1,0:T(1,128)}, u32[]{:S(2)}) copy-start(f32[1,2048]{1,0:T(1,128)} %get-tuple-element.73.gain) | copy-start | bytes 24580
  449.8 3.2 copy-start.7
  453.0 2.0 copy-start.5
  455.0 1.7 copy-start.2
  455.0 2.2 copy-start.3
  474.8 5.1 %copy-start.11 = (f32[8,128]{1,0:T(8,128)S(1)}, f32[8,128]{1,0:T(8,128)}, u32[]{:S(2)}) copy-start(f32[8,128]{1,0:T(8,128)} %get-tuple-element.119) | copy-start | bytes 12292
  476.6 9.1 %copy-start.8 = (f32[64,2048]{1,0:T(8,128)S(1)}, f32[64,2048]{1,0:T(8,128)}, u32[]{:S(2)}) copy-start(f32[64,2048]{1,0:T(8,128)} %get-tuple-element.163) | copy-start | bytes 1572868
Sparse Core Ops, SparseCore 0:
  239.3 58.4 reduce-scatter.6
  300.1 62.9 reduce-scatter.8
  365.3 54.4 reduce-scatter.4
  422.1 61.1 reduce-scatter.10

commit v6 on v5

--- a/solution.py
+++ b/solution.py
@@ -760,16 +760,16 @@
         spread_one(plane - step - 1, plane - step - 1 >= 0)
         spread_one(plane + step + 1, plane + step + 1 <= planes - 1)
 
+    keeps[-1].wait()
+    out_line.start(0)
+    keeps[-2].wait()
+    down_line.start(0)
     swaps = [
         sender(columns(ref, part, flipped(place, m)), target, flipped(me, m))
         for m in SWAP_ORDER
         for ref, part, target in qkv_parts
     ]
     near = [sender(small_in, small.at[me], flipped(me, m)) for m in SWAP_ORDER]
-    keeps[-1].wait()
-    out_line.start(0)
-    keeps[-2].wait()
-    down_line.start(0)
     block = gate_in.shape[1] // (planes * TEAM)
     some = planes // parts
     units = some * block
@@ -786,11 +786,6 @@
         copy.wait()
     qkv_line.start(0)
     rows_tokens.start()
-    moves = [
-        sender(sorted_units.at[k, flipped(place, m)], gate_up[k].at[plane, place], flipped(me, m))
-        for k in range(parts)
-        for m in SWAP_ORDER
-    ]
     kept_units = [
         pltpu.make_async_copy(
             sorted_units.at[k, place], gate_up[k].at[plane, place], own.at[spread_own + planes + k]
@@ -799,26 +794,34 @@
     ]
     for copy in kept_units:
         copy.start()
+    step_out(0)
+    rows_tokens.forward()
     spread_one(plane, True)
-    rows_tokens.forward()
-    step_out(0)
     for copy in near:
         copy.wait_recv()
     keeps[3].wait()
     shared = small.at[pl.ds(team, TEAM)]
     far = [sender(shared, shared, other) for other in others]
-    rows_tokens.across()
     for step in range(planes - 1):
+        down_line.arrive(step)
+        if step < planes - 2:
+            down_line.start(step + 1)
         qkv_line.arrive(step)
         if step < planes - 2:
             qkv_line.start(step + 1)
             step_out(step + 1)
-        down_line.arrive(step)
-        if step < planes - 2:
-            down_line.start(step + 1)
         if step == 0:
+            rows_tokens.across()
+            moves = [
+                sender(
+                    sorted_units.at[k, flipped(place, m)],
+                    gate_up[k].at[plane, place],
+                    flipped(me, m),
+                )
+                for k in range(parts)
+                for m in SWAP_ORDER
+            ]
             rows_tokens.diagonal()
-        if step == 1:
             for copy in far:
                 copy.wait_recv()
             for k, ref in enumerate(gain_refs):

time: 503 us -> 503 us (level)
  no operation moved by 1% of the time
where the time goes in v6:
time: 503 us; the launch traced here: 493 us
  Pallas kernels  448 us (89%)
  other arithmetic  18.5 us (4%)
  between operations  14.9 us (3%)
  local copies, waits for them, and re-layouts  8.63 us (2%)
    pallas_call x1, Pallas kernels, opening(): pl.pallas_call(functools.partial(open_kernel, planes, parts), out_shape=(...  115 us
    pallas_call x1, Pallas kernels, last_sums(): pl.pallas_call(functools.partial(last_sums_kernel, planes, parts), out_sh...  81.5 us
    pallas_call x1, Pallas kernels, attend(): pl.pallas_call(functools.partial(attend_kernel, planes), out_shape=(*kept...  60.3 us
    pallas_call x1, Pallas kernels, feed(): pl.pallas_call(functools.partial(feed_kernel, planes), out_shape=(like((T...  55.5 us
    pallas_call x1, Pallas kernels, feed_back(): pl.pallas_call(functools.partial(feed_back_kernel, parts), out_shape=(lik...  39.8 us
    pallas_call x1, Pallas kernels, attend_back(): pl.pallas_call(functools.partial(attend_back_kernel, planes), out_shape=(...  33.7 us
    pallas_call x1, Pallas kernels, gather_down(): pl.pallas_call(functools.partial(gather_down_kernel, parts), out_shape=(l...  33.3 us
    pallas_call x1, Pallas kernels, closing(): pl.pallas_call(functools.partial(close_kernel, planes), out_shape=(*(like...  16.2 us
  transfers between devices with their start and end apart: 4, of which 1 were waited for; matrix products, arithmetic and copies ran while one was open for 4% of the time, Pallas kernels for 44%

profile of v6, /device:TPU:0, one launch (start us, length us, event | category | flops | bytes accessed | tf_op | source)
XLA Modules:
  0.0 493.2 jit_solution(5223518123910138934)
XLA Ops:
  8.0 0.8 convert_element_type.72.live
  8.7 114.6 %shard_map.255 = (bf16[4,8,64,768]{3,2,1,0:T(8,128)(2,1)}, bf16[4,8,64,768]{3,2,1,0:T(8,128)(2,1)}, bf16[4,8,64,512]{3,2,1,0:T(8,128)(2,1)}, bf16[4,64,2048]{2,1...) custom-call(bf16[64,2048]{1,0:T(8,128)(2,1)} %query_in.1, ...), custom_call_target="tpu_custom_call" | custom-call | tf_op jit(solution)/shard_map/pallas_call | solution.py:868
  123.4 60.3 %shard_map.256 = (bf16[1536,2048]{1,0:T(8,128)(2,1)}, f32[1536,384]{1,0:T(8,128)}, bf16[1536,384]{1,0:T(8,128)(2,1)}, bf16[1536,128]{1,0:T(8,128)(2,1)}, bf16[15...) custom-call(bf16[1536,2048]{1,0:T(8,128)(2,1)} %bitcast.50, ...), custom_call_target="tpu_custom_call", output_to_operand_aliasing={{8}: (12, {})} | custom-call | flops 4831838208 | bytes 25165824 | tf_op jit(solution)/shard_map/pallas_call | solution.py:1112
  183.6 55.5 %shard_map.257 = (bf16[8,192,2048]{2,1,0:T(8,128)(2,1)}, bf16[8,192,384]{2,1,0:T(8,128)(2,1)}, bf16[8,192,768]{2,1,0:T(8,128)(2,1)}, bf16[2048,768]{1,0:T(8,128)(2,1)}, bf16[4,8,64,768]{3,2,1,0:T(8,128)(2,1)}) custom-call(bf16[192,2048]{1,0:T(8,128)(2,1)} %get-tuple-element.81.two_in, ...), custom_call_target="tpu_custom_call", output_to_operand_aliasing={{4}: (4, {})} | custom-call | flops 12079595520 | bytes 25165824 | tf_op jit(solution)/shard_map/pallas_call | solution.py:1404
  239.2 13.2 %shard_map.258 = (bf16[8,192,384]{2,1,0:T(8,128)(2,1)}, bf16[8,192,768]{2,1,0:T(8,128)(2,1)}) custom-call(bf16[8,192,2048]{2,1,0:T(8,128)(2,1)} %get-tuple-element.86.two, bf16[8,192,2048]{2,1,0:T(8,128)(2,1)} %get-tuple-element.82.cot_in.cot, bf16[2048,768]{1,0:T(8,128)(2,1)} %bitcast.54, bf16[768,2048]{1,0:T(8,128)(2,1)} %bitcast.52), custom_call_target="tpu_custom_call" | custom-call | flops 7247757312 | bytes 12582912 | tf_op jit(solution)/shard_map/pallas_call | solution.py:1453
  252.4 39.8 %shard_map.259 = (f32[192,2048]{1,0:T(8,128)}, bf16[2048,768]{1,0:T(8,128)(2,1)}) custom-call(bf16[8,192,2048]{2,1,0:T(8,128)(2,1)} %get-tuple-element.86.two, bf16[8,192,768]{2,1,0:T(8,128)(2,1)} %get-tuple-element.87.refs_0_, bf16[8,192,768]{2,1,0:T(8,128)(2,1)} %get-tuple-element.89.refs_1_, bf16[2048,768]{1,0:T(8,128)(2,1)} %bitcast.57, ...), custom_call_target="tpu_custom_call" | custom-call | flops 14495514624 | bytes 11010048 | tf_op jit(solution)/shard_map/pallas_call | solution.py:393
  292.5 1.2 copy-done
  295.3 1.9 fusion.11
  297.3 33.3 %shard_map.260 = (bf16[8,192,2048]{2,1,0:T(8,128)(2,1)}, bf16[768,2048]{1,0:T(8,128)(2,1)}) custom-call(bf16[192,2048]{1,0:T(8,128)(2,1)} %get-tuple-element.137.x, bf16[8,192,2048]{2,1,0:T(8,128)(2,1)} %get-tuple-element.82.cot_in.cot, bf16[8,192,384]{2,1,0:T(8,128)(2,1)} %get-tuple-element.92.refs_0_, bf16[8,192,384]{2,1,0:T(8,128)(2,1)} %get-tuple-element.93.refs_1_), custom_call_target="tpu_custom_call" | custom-call | flops 4831838208 | bytes 18874368 | tf_op jit(solution)/shard_map/pallas_call | solution.py:455
  330.6 33.7 %shard_map.261 = (bf16[1536,512]{1,0:T(8,128)(2,1)}, bf16[4,512,512]{2,1,0:T(8,128)(2,1)}, bf16[4,256,512]{2,1,0:T(8,128)(2,1)}, f32[8,128]{1,0:T(8,128)}, bf16[1,2,256,512]{3,2,1,0:T(8,128)(2,1)}) custom-call(bf16[1536,2048]{1,0:T(8,128)(2,1)} %bitcast.64, bf16[256,2048]{1,0:T(8,128)(2,1)} %bitcast.61, bf16[1536,256]{1,0:T(8,128)(2,1)} %get-tuple-element.95.context, ...), custom_call_target="tpu_custom_call" | custom-call | flops 6442450944 | bytes 25165824 | tf_op jit(solution)/shard_map/pallas_call | solution.py:1278
  365.0 0.8 slice_reduce_fusion.1
  366.4 81.5 %shard_map.262 = (f32[192,2048]{1,0:T(8,128)}, f32[192,2048]{1,0:T(8,128)}, bf16[64,6144]{1,0:T(8,128)(2,1)}, bf16[64,6144]{1,0:T(8,128)(2,1)}, f32[64,2048]{1,0:T(8,128)}, /*index=5*/bf16[2,2,256,512]{3,2,1,0:T(8,128)(2,1)}) custom-call(bf16[8,192,512]{2,1,0:T(8,128)(2,1)} %bitcast.65, bf16[2048,512]{1,0:T(8,128)(2,1)} %bitcast.59, ...), custom_call_target="tpu_custom_call" | custom-call | flops 8053063680 | bytes 3145728 | tf_op jit(solution)/shard_map/pallas_call | solution.py:548
  447.8 1.9 fusion.6
  450.6 2.4 convert_element_type.63
  453.0 1.2 convert_element_type.64
  455.0 1.2 multiply_convert_fusion
  457.1 1.4 fusion.2
  458.5 16.2 %shard_map.263 = (bf16[64,2048]{1,0:T(8,128)(2,1)}, bf16[64,1024]{1,0:T(8,128)(2,1)}, bf16[64,1024]{1,0:T(8,128)(2,1)}, f32[8,128]{1,0:T(8,128)}) custom-call(bf16[512,512]{1,0:T(8,128)(2,1)} %reduce-scatter.5.cloned.1.call-done.x_ref, f32[8,4,8,128]{3,2,1,0:T(8,128)} %bitcast.41), custom_call_target="tpu_custom_call" | custom-call | tf_op jit(solution)/shard_map/pallas_call | solution.py:949
  474.8 1.8 convert_element_type.68
  476.5 1.7 convert_element_type.69
  478.2 1.6 convert_element_type.70
  480.9 2.3 reduce-scatter.11.cloned.1.call-done
  483.2 2.5 convert_element_type.71
  485.7 0.8 copy.42
  (58 shorter events, 6.8 us)
Async XLA Ops:
  7.2 359.1 %reduce-scatter.7.cloned.1.call-start = ((), (), s32[]{:S(2)}) async-start(), calls=%async_computation.5 | async-start | bytes 3932160 | tf_op jit(solution)/shard_map/reduce_scatter | solution.py:1504
  239.2 127.2 %reduce-scatter.9.cloned.1.call-start = ((), (), s32[]{:S(2)}) async-start(), calls=%async_computation.6 | async-start | bytes 3932160 | tf_op jit(solution)/shard_map/reduce_scatter | solution.py:1504
  292.2 1.4 copy-start
  292.3 1.9 copy-start.4
  292.3 1.9 copy-start.10
  292.3 166.2 %reduce-scatter.5.cloned.1.call-start = ((), (), s32[]{:S(2)}) async-start(), calls=%async_computation.4 | async-start | bytes 2621440 | tf_op jit(solution)/shard_map/reduce_scatter | solution.py:1504
  294.2 1.1 copy-start.6
  364.4 118.9 %reduce-scatter.11.cloned.1.call-start = ((), (), s32[]{:S(2)}) async-start(), calls=%async_computation.7 | async-start | bytes 3932160 | tf_op jit(solution)/shard_map/reduce_scatter | solution.py:1504
  364.4 1.6 copy-start.1
  366.3 81.5 %copy-start.9 = (f32[1,2048]{1,0:T(1,128)S(1)}, f32[1,2048]{1,0:T(1,128)}, u32[]{:S(2)}) copy-start(f32[1,2048]{1,0:T(1,128)} %get-tuple-element.73.gain) | copy-start | bytes 24580
  449.8 3.2 copy-start.7
  453.0 2.0 copy-start.5
  455.0 1.7 copy-start.2
  455.0 2.2 copy-start.3
  474.8 5.1 %copy-start.11 = (f32[8,128]{1,0:T(8,128)S(1)}, f32[8,128]{1,0:T(8,128)}, u32[]{:S(2)}) copy-start(f32[8,128]{1,0:T(8,128)} %get-tuple-element.119) | copy-start | bytes 12292
  476.5 9.1 %copy-start.8 = (f32[64,2048]{1,0:T(8,128)S(1)}, f32[64,2048]{1,0:T(8,128)}, u32[]{:S(2)}) copy-start(f32[64,2048]{1,0:T(8,128)} %get-tuple-element.163) | copy-start | bytes 1572868
Sparse Core Ops, SparseCore 0:
  239.3 58.4 reduce-scatter.6
  300.0 62.9 reduce-scatter.8
  365.3 54.4 reduce-scatter.4
  422.1 61.1 reduce-scatter.10
